TPU v7x, 256 devices: a whole 4x4x8 slice. The times are simulated.
256 devices in a mesh: gz: 32 (over y, z), gy: 8 (over x, core).
Axes of the slice: x: 4, y: 4, z: 8, core: 2. Of those that a mesh axis runs over, the one named last changes fastest.
Arguments:
- volume: bfloat16 [32, 64, 128, 128], P('gz', 'gy'), may hold values from -1300 to 1300
- conv_weight: bfloat16 [3, 3, 3, 128, 128], replicated, may hold values from -2 to 2
- target: bfloat16 [32, 64, 128, 128], P('gz', 'gy'), may hold values from -4 to 4
Outputs:
- whitened: bfloat16 [32, 64, 128, 128], P('gz', 'gy')
- input_grad: bfloat16 [32, 64, 128, 128], P('gz', 'gy')
- weight_grad: float32 [3, 3, 3, 128, 128], P(None, None, None, 'gy')
All inputs are finite; a program needn't handle non-finite values.
Results may differ from a plain program's by a relative error of at most 0.0095.
Values may be sent and summed in bfloat16 or wider, within the bound.
No kernel may reach another device: no remote copies, remote signals or barrier semaphores. Data moves between devices by JAX's collectives and lax.ppermute only.
A program may use at most 64 MiB of HBM per device.

v0:
```python
import math

import jax
import jax.numpy as jnp
from jax import lax
from jax.sharding import PartitionSpec as P

G = 64
NEWTON = 5


EPSILON = 1e-05
HIGHEST = lax.Precision.HIGHEST


def extended(block, sides, width):
    for axis, dim in sides:
        count = lax.axis_size(axis)
        forward = [(i, i + 1) for i in range(count - 1)]
        backward = [(target, source) for source, target in forward]
        low = lax.ppermute(
            lax.slice_in_dim(block, block.shape[dim] - width, None, axis=dim), axis, forward
        )
        high = lax.ppermute(lax.slice_in_dim(block, 0, width, axis=dim), axis, backward)
        block = jnp.concatenate([low, block, high], axis=dim)
    return block


def newton_whitener(covariance):
    group_width = covariance.shape[1]
    trace_value = jnp.trace(covariance, axis1=1, axis2=2)
    scaled = covariance / trace_value[:, None, None]
    iterate = jnp.broadcast_to(jnp.eye(group_width, dtype=jnp.float32), covariance.shape)
    for sweep in range(NEWTON):
        squared = jnp.matmul(iterate, iterate, precision=HIGHEST)
        cubic_term = jnp.matmul(
            jnp.matmul(squared, iterate, precision=HIGHEST), scaled, precision=HIGHEST
        )
        iterate = 0.5 * (3.0 * iterate - cubic_term)
    return iterate / jnp.sqrt(trace_value)[:, None, None]


def pad_columns(block):
    return jnp.pad(block, ((0, 0), (0, 0), (1, 1), (0, 0)))


def tap_slabs(padded, depth_cells, row_cells, column_cells):
    slab_list = []
    for tap_z in range(3):
        for tap_y in range(3):
            shifted = [
                padded[
                    tap_z : tap_z + depth_cells,
                    tap_y : tap_y + row_cells,
                    tap_x : tap_x + column_cells,
                ]
                for tap_x in range(3)
            ]
            merged = jnp.concatenate(shifted, axis=-1)
            slab_list.append(
                merged.reshape(depth_cells * row_cells * column_cells, merged.shape[-1])
            )
    return slab_list


def apply_taps(slab_list, kernel):
    channels_in = kernel.shape[3]
    channels_out = kernel.shape[4]
    total = jnp.zeros((slab_list[0].shape[0], channels_out), jnp.float32)
    for index_tap in range(9):
        kernel_rows = kernel[index_tap // 3, index_tap % 3].reshape(3 * channels_in, channels_out)
        total = total + jnp.dot(
            slab_list[index_tap], kernel_rows, preferred_element_type=jnp.float32
        )
    return total


def weight_terms(slab_list, grad_hidden):
    channels = grad_hidden.shape[1]
    pieces = [
        lax.dot_general(
            slab_cols, grad_hidden, (((0,), (0,)), ((), ())), preferred_element_type=jnp.float32
        ).reshape(3, channels, channels)
        for slab_cols in slab_list
    ]
    return jnp.stack(pieces).reshape(3, 3, 3, channels, channels)


def local(volume, conv_weight, target):
    depth_cells, row_cells, column_cells, channels = volume.shape
    count_local = depth_cells * row_cells * column_cells
    voxels = count_local * lax.axis_size("gz") * lax.axis_size("gy")
    groups = channels // G
    padded = pad_columns(extended(volume, (("gz", 0), ("gy", 1)), 1))
    slab_list = tap_slabs(padded, depth_cells, row_cells, column_cells)
    hidden = apply_taps(slab_list, conv_weight).astype(jnp.bfloat16)
    hidden_wide = hidden.astype(jnp.float32)
    eye_block = jnp.eye(G, dtype=jnp.float32)
    channel_sum = lax.psum(jnp.sum(hidden_wide, axis=0), ("gz", "gy"))
    channel_mean = channel_sum / voxels
    centered = (hidden_wide - channel_mean).reshape(count_local, groups, G)
    second = lax.psum(
        jnp.einsum("vga,vgb->gab", centered, centered, precision=HIGHEST), ("gz", "gy")
    )
    covariance = second / voxels + EPSILON * eye_block
    whitener, whiten_pull = jax.vjp(newton_whitener, covariance)
    white = jnp.einsum("gab,vgb->vga", whitener, centered, precision=HIGHEST)
    whitened = white.reshape(volume.shape).astype(jnp.bfloat16)
    residue = white - target.reshape(count_local, groups, G).astype(jnp.float32)
    residue_sum, white_grad = lax.psum(
        (
            jnp.sum(residue, axis=0),
            jnp.einsum("vga,vgb->gab", residue, centered, precision=HIGHEST),
        ),
        ("gz", "gy"),
    )
    sigma_grad = whiten_pull(white_grad)[0]
    symmetric = (sigma_grad + jnp.swapaxes(sigma_grad, 1, 2)) / voxels
    grad_wide = jnp.einsum(
        "gba,vgb->vga", whitener, residue - residue_sum / voxels, precision=HIGHEST
    )
    grad_wide = grad_wide + jnp.einsum("gab,vgb->vga", symmetric, centered, precision=HIGHEST)
    grad_hidden = grad_wide.reshape(count_local, channels).astype(jnp.bfloat16)
    local_term = weight_terms(slab_list, grad_hidden)
    grad_padded = pad_columns(
        extended(grad_hidden.reshape(volume.shape), (("gz", 0), ("gy", 1)), 1)
    )
    flipped = jnp.swapaxes(jnp.flip(conv_weight, (0, 1, 2)), 3, 4)
    input_grad = apply_taps(tap_slabs(grad_padded, depth_cells, row_cells, column_cells), flipped)
    input_grad = input_grad.astype(jnp.bfloat16).reshape(volume.shape)
    summed = lax.psum(local_term, ("gz", "gy"))
    share_rows = channels // lax.axis_size("gy")
    shard_part = lax.dynamic_slice_in_dim(summed, lax.axis_index("gy") * share_rows, share_rows, 3)
    weight_grad = shard_part * (1.0 / math.sqrt(voxels))
    return (whitened, input_grad, weight_grad)


def solution(mesh):
    in_specs = (P("gz", "gy", None, None), P(), P("gz", "gy", None, None))
    out_specs = (
        P("gz", "gy", None, None),
        P("gz", "gy", None, None),
        P(None, None, None, "gy", None),
    )
    return jax.shard_map(local, mesh=mesh, in_specs=in_specs, out_specs=out_specs, check_vma=False)
```

profile of v0, /device:TPU:4, one launch (start us, length us, event | category | flops | bytes accessed | tf_op | source)
XLA Modules:
  0.0 599.7 jit_solution(2058463598211795852)
XLA Ops:
  7.2 4.0 collective-permute-start
  11.2 1.3 collective-permute-start.1
  12.5 2.0 fusion.195
  14.6 1.4 copy.65
  16.3 1.0 fusion.194
  17.3 0.8 fusion.151
  18.2 0.7 copy.45
  19.1 0.9 reshape.228
  20.0 1.2 collective-permute-done.1
  21.3 1.9 collective-permute-start.2
  23.2 3.6 collective-permute-start.3
  27.2 1.8 collective-permute-done.3
  29.4 0.9 fusion.193
  36.5 79.7 %psum.35 = f32[128]{0:T(128)S(1)} all-reduce(f32[128]{0:T(128)S(1)} %get-tuple-element.89), channel_id=1, replica_groups=mesh['gz'=32,'gy'=8] {'gz','gy'}, use_global_device_ids=true, to_apply=%region_1.2 | all-reduce | flops 128 | bytes 1024 | tf_op jit(solution)/shard_map/psum | solution.py:99
  116.3 0.6 fusion.200
  116.9 73.4 %psum.36 = f32[2,64,64]{2,1,0:T(8,128)S(1)} all-reduce(f32[2,64,64]{2,1,0:T(8,128)S(1)} %fusion.200), channel_id=1, replica_groups=mesh['gz'=32,'gy'=8] {'gz','gy'}, use_global_device_ids=true, to_apply=%region_2.3 | all-reduce | flops 8192 | bytes 65536 | tf_op jit(solution)/shard_map/psum | solution.py:102
  191.8 0.6 copy-done.33
  193.1 0.6 copy-done.35
  194.5 0.6 copy-done.37
  196.4 0.6 copy-done.24
  197.0 2.9 fusion.191
  200.0 1.2 fusion.201
  201.2 74.9 %all-reduce.2 = (f32[2,64]{1,0:T(2,128)}, f32[2,64,64]{2,1,0:T(8,128)}) all-reduce(f32[2,64]{1,0:T(2,128)} %get-tuple-element.11, f32[2,64,64]{2,1,0:T(8,128)} %fusion.201), channel_id=1, replica_groups=mesh['gz'=32,'gy'=8] {'gz','gy'}, use_global_device_ids=true, to_apply=%region_5.6 | all-reduce | flops 8320 | bytes 66560 | tf_op jit(solution)/shard_map/psum | solution.py:110
  276.1 1.2 fusion.83
  277.3 1.1 fusion.90
  278.4 1.2 convolution_add_fusion.32
  279.6 1.2 convolution_add_fusion.31
  280.8 1.1 convolution_add_fusion.30
  281.9 1.2 fusion.85
  286.2 0.9 convolution_add_fusion.20
  287.2 0.9 fusion.84
  288.1 2.4 copy.66
  290.5 2.3 copy.68
  292.8 2.4 copy.70
  295.1 2.3 copy.72
  297.4 1.2 copy.74
  298.6 2.4 copy.76
  301.1 1.2 copy.78
  303.0 1.1 convolution_add_fusion.29
  304.8 1.0 multiply_reduce_fusion
  305.8 0.7 copy.63
  306.5 0.7 fusion.74
  307.3 1.6 fusion.13
  308.9 3.7 collective-permute-start.4
  312.6 1.3 collective-permute-start.5
  313.9 1.1 fusion.22
  315.0 1.1 fusion.21
  316.1 1.0 fusion.20
  317.1 1.1 fusion.19
  318.2 1.0 fusion.18
  319.2 1.1 fusion.17
  320.3 1.0 fusion.16
  321.6 1.0 fusion.15
  323.4 2.1 collective-permute-start.6
  325.4 3.9 collective-permute-start.7
  329.3 1.1 fusion.14
  330.4 0.9 copy.84
  331.3 0.9 collective-permute-done.7
  332.2 3.2 fusion.5
  335.5 1.6 fusion.192
  339.1 0.5 fusion.46
  343.6 1.1 fusion.12
  344.7 246.4 %all-reduce.5.cloned.1.call-done = f32[3,3,3,128,128]{4,3,2,1,0:T(8,128)} async-done(((f32[3,3,3,128,128]{4,3,2,1,0:T(8,128)}), f32[3,3,3,128,128]{4,3,2,1,0:T(8,128)}) %all-reduce.5.cloned.1.call-update) | async-done | bytes 1769488 | tf_op jit(solution)/shard_map/psum | solution.py:131
  591.2 1.6 dynamic-slice_multiply_fusion
  (239 shorter events, 22.6 us)
Async XLA Ops:
  7.2 7.4 %copy-start.7 = (bf16[3,3,3,128,128]{4,3,2,1,0:T(8,128)(2,1)S(1)}, bf16[3,3,3,128,128]{4,3,2,1,0:T(8,128)(2,1)}, u32[]{:S(2)}) copy-start(bf16[3,3,3,128,128]{4,3,2,1,0:T(8,128)(2,1)} %param.4) | copy-start | bytes 2654212
  7.2 584.0 %all-reduce.5.cloned.1.call-start = ((), (), s32[]{:S(2)}) async-start(), calls=%async_computation | async-start | bytes 3538944 | tf_op jit(solution)/shard_map/psum | solution.py:131
  7.2 12.7 %collective-permute-start = (bf16[1,8,128,128]{3,2,1,0:T(8,128)(2,1)}, bf16[1,8,128,128]{3,2,1,0:T(8,128)(2,1)S(1)}, u32[]{:S(2)}, u32[]{:S(2)}) collective-permute-start(bf16[1,8,128,128]{3,2,1,0:T(8,128)(2,1)} %param.3), channel_id=1, source_target_pairs={{0,8},{8,16},{16,24},{24,32},{32,40},{40,48},{48,56},{56,64},{64,7... | collective-permute-start | bytes 786440 | tf_op jit(solution)/shard_map/ppermute | solution.py:21
  11.2 10.0 %collective-permute-start.1 = (bf16[1,8,128,128]{3,2,1,0:T(8,128)(2,1)}, bf16[1,8,128,128]{3,2,1,0:T(8,128)(2,1)S(1)}, u32[]{:S(2)}, u32[]{:S(2)}) collective-permute-start(bf16[1,8,128,128]{3,2,1,0:T(8,128)(2,1)} %param.3), channel_id=1, source_target_pairs={{8,0},{16,8},{24,16},{32,24},{40,32},{48,40},{56,48},{64,56},{72,6... | collective-permute-start | bytes 786440 | tf_op jit(solution)/shard_map/ppermute | solution.py:24
  16.2 2.7 copy-start.58
  17.3 2.7 copy-start.22
  21.3 5.9 collective-permute-start.2
  23.2 5.8 collective-permute-start.3
  30.9 1.3 copy-start.1
  30.9 2.8 copy-start
  32.2 1.5 copy-start.3
  32.3 1.5 copy-start.4
  32.3 2.3 copy-start.2
  32.6 1.2 copy-start.54
  36.4 154.7 %copy-start.59 = (f32[2,64,64]{2,1,0:T(8,128)S(1)}, f32[2,64,64]{2,1,0:T(8,128)}, u32[]{:S(2)}) copy-start(f32[2,64,64]{2,1,0:T(8,128)} %fusion.151) | copy-start | bytes 98308
  36.4 154.7 %copy-start.67 = (f32[64,64]{1,0:T(8,128)S(1)}, f32[64,64]{1,0:T(8,128)}, u32[]{:S(2)}) copy-start(f32[64,64]{1,0:T(8,128)} %copy.45) | copy-start | bytes 49156
  190.4 5.7 copy-start.15
  190.6 5.5 copy-start.68
  191.1 8.9 %copy-start.71 = (f32[2]{0:T(128)}, f32[2]{0:T(128)S(1)}, u32[]{:S(2)}) copy-start(f32[2]{0:T(128)S(1)} %get-tuple-element.88) | copy-start | bytes 28
  191.4 4.7 copy-start.18
  191.6 4.5 copy-start.26
  192.9 1.3 copy-start.28
  194.2 1.9 copy-start.30
  276.1 7.3 %copy-start.31 = (f32[2,64,64]{2,1,0:T(8,128)S(1)}, f32[2,64,64]{2,1,0:T(8,128)}, u32[]{:S(2)}) copy-start(f32[2,64,64]{2,1,0:T(8,128)} %copy-done.30) | copy-start | bytes 98308
  276.1 8.1 %copy-start.16 = (f32[2,64,64]{2,1,0:T(8,128)S(1)}, f32[2,64,64]{2,1,0:T(8,128)}, u32[]{:S(2)}) copy-start(f32[2,64,64]{2,1,0:T(8,128)} %copy-done.15) | copy-start | bytes 98308
  276.1 8.1 %copy-start.69 = (f32[2]{0:T(128)S(1)}, f32[2]{0:T(128)}, u32[]{:S(2)}) copy-start(f32[2]{0:T(128)} %copy-done.68) | copy-start | bytes 28
  276.1 8.7 %copy-start.29 = (f32[2,64,64]{2,1,0:T(8,128)S(1)}, f32[2,64,64]{2,1,0:T(8,128)}, u32[]{:S(2)}) copy-start(f32[2,64,64]{2,1,0:T(8,128)} %copy-done.28) | copy-start | bytes 98308
  279.6 6.4 %copy-start.19 = (f32[2,64,64]{2,1,0:T(8,128)S(1)}, f32[2,64,64]{2,1,0:T(8,128)}, u32[]{:S(2)}) copy-start(f32[2,64,64]{2,1,0:T(8,128)} %copy-done.18) | copy-start | bytes 98308
  280.8 5.4 copy-start.27
  281.9 5.2 copy-start.39
  281.9 5.2 copy-start.61
  281.9 5.2 copy-start.66
  281.9 5.2 copy-start.72
  284.2 2.9 copy-start.41
  285.6 1.5 copy-start.43
  298.6 3.7 copy-start.25
  298.6 3.7 copy-start.62
  298.6 3.7 copy-start.74
  298.6 3.9 copy-start.20
  298.6 3.9 copy-start.63
  298.6 4.4 copy-start.38
  298.6 4.4 copy-start.40
  301.0 3.1 copy-start.36
  301.0 3.1 copy-start.42
  301.0 3.4 copy-start.34
  301.0 3.4 copy-start.44
  301.0 3.7 copy-start.17
  301.0 3.7 copy-start.60
  302.2 4.3 copy-start.75
  302.2 4.3 copy-start.73
  302.2 5.0 copy-start.70
  306.5 7.4 %copy-start.13 = (bf16[1024,384]{0,1:T(8,128)(2,1)S(1)}, bf16[1024,384]{0,1:T(8,128)(2,1)}, u32[]{:S(2)}) copy-start(bf16[1024,384]{0,1:T(8,128)(2,1)} %copy.66) | copy-start | bytes 2359300
  307.3 7.7 %copy-start.14 = (bf16[1024,384]{0,1:T(8,128)(2,1)S(1)}, bf16[1024,384]{0,1:T(8,128)(2,1)}, u32[]{:S(2)}) copy-start(bf16[1024,384]{0,1:T(8,128)(2,1)} %copy.68) | copy-start | bytes 2359300
  308.9 7.2 %copy-start.12 = (bf16[1024,384]{0,1:T(8,128)(2,1)S(1)}, bf16[1024,384]{0,1:T(8,128)(2,1)}, u32[]{:S(2)}) copy-start(bf16[1024,384]{0,1:T(8,128)(2,1)} %copy.70) | copy-start | bytes 2359300
  308.9 14.0 %collective-permute-start.4 = (bf16[1,8,128,128]{2,1,3,0:T(8,128)(2,1)S(1)}, bf16[1,8,128,128]{2,1,3,0:T(8,128)(2,1)S(1)}, u32[]{:S(2)}, u32[]{:S(2)}) collective-permute-start(bf16[1,8,128,128]{2,1,3,0:T(8,128)(2,1)S(1)} %bitcast.342), channel_id=1, source_target_pairs={{0,8},{8,16},{16,24},{24,32},{32,40},{40,48},{48,56},{56,64},{64,7... | collective-permute-start | bytes 786440 | tf_op jit(solution)/shard_map/ppermute | solution.py:21
  312.6 10.4 %collective-permute-start.5 = (bf16[1,8,128,128]{2,1,3,0:T(8,128)(2,1)S(1)}, bf16[1,8,128,128]{2,1,3,0:T(8,128)(2,1)S(1)}, u32[]{:S(2)}, u32[]{:S(2)}) collective-permute-start(bf16[1,8,128,128]{2,1,3,0:T(8,128)(2,1)S(1)} %bitcast.343), channel_id=1, source_target_pairs={{8,0},{16,8},{24,16},{32,24},{40,32},{48,40},{56,48},{64,56},{72,6... | collective-permute-start | bytes 786440 | tf_op jit(solution)/shard_map/ppermute | solution.py:24
  313.9 3.2 copy-start.11
  315.0 3.2 copy-start.10
  316.1 3.2 copy-start.9
  317.1 3.2 copy-start.8
  318.2 3.2 copy-start.6
  323.4 7.0 %copy-start.23 = (bf16[1024,2,64]{0,2,1:T(8,128)(2,1)S(1)}, bf16[1024,2,64]{0,2,1:T(8,128)(2,1)}, u32[]{:S(2)}) copy-start(bf16[1024,2,64]{0,2,1:T(8,128)(2,1)} %get-tuple-element.83) | copy-start | bytes 786436
  323.4 8.0 %collective-permute-start.6 = (bf16[3,1,128,128]{2,1,3,0:T(2,128)(2,1)S(1)}, bf16[3,1,128,128]{2,1,3,0:T(2,128)(2,1)S(1)}, u32[]{:S(2)}, u32[]{:S(2)}) collective-permute-start(bf16[3,1,128,128]{2,1,3,0:T(2,128)(2,1)S(1)} %get-tuple-element.80), channel_id=1, source_target_pairs={{0,1},{1,2},{2,3},{3,4},{4,5},{5,6},{6,7},{8,9},{9,10},{10,11},{11... | collective-permute-start | bytes 294920 | tf_op jit(solution)/shard_map/ppermute | solution.py:21
  325.4 6.8 %collective-permute-start.7 = (bf16[3,1,128,128]{2,1,3,0:T(2,128)(2,1)S(1)}, bf16[3,1,128,128]{2,1,3,0:T(2,128)(2,1)S(1)}, u32[]{:S(2)}, u32[]{:S(2)}) collective-permute-start(bf16[3,1,128,128]{2,1,3,0:T(2,128)(2,1)S(1)} %get-tuple-element.79), channel_id=1, source_target_pairs={{1,0},{2,1},{3,2},{4,3},{5,4},{6,5},{7,6},{9,8},{10,9},{11,10},{12... | collective-permute-start | bytes 294920 | tf_op jit(solution)/shard_map/ppermute | solution.py:24
  (21 other events, 17.3 us)
Sparse Core Ops, SparseCore 0:
  330.5 260.6 all-reduce.4
where the time goes:
time: 601 us; the launch traced here: 600 us
  waiting for transfers between devices  251 us (42%)
  blocking collectives  228 us (38%)
  matrix products  43.4 us (7%)
  local copies, waits for them, and re-layouts  31.7 us (5%)
  starting transfers between devices  21.7 us (4%)
  between operations  15.5 us (3%)
  other arithmetic  8.53 us (1%)
    psum x1, waiting for transfers between devices, local(): summed = lax.psum(local_term, ('gz', 'gy'))  246 us
    psum x1, blocking collectives, local(): channel_sum = lax.psum(jnp.sum(hidden_wide, axis=0), ('gz', 'gy'))  79.7 us
    psum x1, blocking collectives, local(): lax.psum((jnp.sum(residue, axis=0), jnp.einsum('vga,vgb->gab', residue, c...  74.9 us
    psum x1, blocking collectives, local(): lax.psum(jnp.einsum('vga,vgb->gab', centered, centered, precision=HIGHEST...  73.4 us
    reshape x9, local copies, waits for them, and re-layouts, tap_slabs(): merged.reshape(depth_cells * row_cells * column_cells, merged.shape[-1])  14.7 us
  transfers between devices with their start and end apart: 9, of which 5 were waited for; matrix products, arithmetic and copies ran while one was open for 5% of the time, Pallas kernels for 0%

commit v1 on v0

v1 whole, which is shorter than its diff:
```python
import math

import jax
import jax.numpy as jnp
from jax import lax
from jax.sharding import Mesh, PartitionSpec as P

G = 64
NEWTON = 5
EPSILON = 1e-05
HIGHEST = lax.Precision.HIGHEST
GZ = ("y", "z")
GY = ("x", "c")
SPREAD = ("y", "x", "c")


def shifted_from(block, axes, count, step):
    pairs = [(i, i + step) for i in range(count) if 0 <= i + step < count]
    return lax.ppermute(block, axes, pairs)


def extended_fast(block):
    nz = lax.axis_size(GZ)
    ny = lax.axis_size(GY)
    below = shifted_from(block, GZ, nz, 1)
    above = shifted_from(block, GZ, nz, -1)
    low = shifted_from(block[:, -1:], GY, ny, 1)
    high = shifted_from(block[:, :1], GY, ny, -1)
    edges = jnp.concatenate([low, high], axis=1)
    edges_below = shifted_from(edges, GZ, nz, 1)
    edges_above = shifted_from(edges, GZ, nz, -1)
    planes = []
    for plane, edge in ((below, edges_below), (block, edges), (above, edges_above)):
        planes.append(jnp.concatenate([edge[:, :1], plane, edge[:, 1:]], axis=1))
    return jnp.concatenate(planes, axis=0)


def newton_whitener(covariance):
    group_width = covariance.shape[1]
    trace_value = jnp.trace(covariance, axis1=1, axis2=2)
    scaled = covariance / trace_value[:, None, None]
    iterate = jnp.broadcast_to(jnp.eye(group_width, dtype=jnp.float32), covariance.shape)
    for sweep in range(NEWTON):
        squared = jnp.matmul(iterate, iterate, precision=HIGHEST)
        cubic_term = jnp.matmul(
            jnp.matmul(squared, iterate, precision=HIGHEST), scaled, precision=HIGHEST
        )
        iterate = 0.5 * (3.0 * iterate - cubic_term)
    return iterate / jnp.sqrt(trace_value)[:, None, None]


def pad_columns(block):
    return jnp.pad(block, ((0, 0), (0, 0), (1, 1), (0, 0)))


def tap_slabs(padded, depth_cells, row_cells, column_cells):
    slab_list = []
    for tap_z in range(3):
        for tap_y in range(3):
            shifted = [
                padded[
                    tap_z : tap_z + depth_cells,
                    tap_y : tap_y + row_cells,
                    tap_x : tap_x + column_cells,
                ]
                for tap_x in range(3)
            ]
            merged = jnp.concatenate(shifted, axis=-1)
            slab_list.append(
                merged.reshape(depth_cells * row_cells * column_cells, merged.shape[-1])
            )
    return slab_list


def apply_taps(slab_list, kernel):
    channels_in = kernel.shape[3]
    channels_out = kernel.shape[4]
    total = jnp.zeros((slab_list[0].shape[0], channels_out), jnp.float32)
    for index_tap in range(9):
        kernel_rows = kernel[index_tap // 3, index_tap % 3].reshape(3 * channels_in, channels_out)
        total = total + jnp.dot(
            slab_list[index_tap], kernel_rows, preferred_element_type=jnp.float32
        )
    return total


def weight_terms(slab_list, grad_hidden):
    channels = grad_hidden.shape[1]
    pieces = [
        lax.dot_general(
            slab_cols, grad_hidden, (((0,), (0,)), ((), ())), preferred_element_type=jnp.float32
        ).reshape(3, channels, channels)
        for slab_cols in slab_list
    ]
    return jnp.concatenate(pieces, axis=0)


def exchange(parts, axes):
    return lax.all_to_all(parts, axes, 0, 0, tiled=True)


def copies(part, count):
    return jnp.broadcast_to(part[None], (count,) + part.shape)


def summed_everywhere(rows):
    spread = lax.axis_size(SPREAD)
    parts = rows.reshape(spread, rows.shape[0] // spread, rows.shape[1])
    mine = exchange(parts, SPREAD).sum(0)
    mine = exchange(copies(mine, lax.axis_size("z")), ("z",)).sum(0)
    return exchange(copies(mine, spread), SPREAD).reshape(rows.shape)


def local(volume, conv_weight, target):
    depth_cells, row_cells, column_cells, channels = volume.shape
    count_local = depth_cells * row_cells * column_cells
    voxels = count_local * lax.axis_size(GZ) * lax.axis_size(GY)
    groups = channels // G
    padded = pad_columns(extended_fast(volume))
    slab_list = tap_slabs(padded, depth_cells, row_cells, column_cells)
    hidden = apply_taps(slab_list, conv_weight).astype(jnp.bfloat16)
    hidden_wide = hidden.astype(jnp.float32)
    eye_block = jnp.eye(G, dtype=jnp.float32)

    flat_target = target.reshape(count_local, channels)
    target_wide = flat_target.astype(jnp.float32)
    pair = hidden.reshape(count_local, groups, G)
    target_pair = flat_target.reshape(count_local, groups, G)
    second_local = jnp.einsum("vga,vgb->agb", pair, pair, preferred_element_type=jnp.float32)
    cross_local = jnp.einsum("vga,vgb->agb", target_pair, pair, preferred_element_type=jnp.float32)
    sums_local = jnp.stack([jnp.sum(hidden_wide, axis=0), jnp.sum(target_wide, axis=0)])
    moments = jnp.concatenate(
        [second_local.reshape(G, channels), cross_local.reshape(G, channels)], axis=0
    )
    spread = lax.axis_size(SPREAD)
    sheet = jnp.concatenate(
        [
            moments.reshape(spread, 2 * G // spread, channels),
            jnp.pad(sums_local, ((0, spread - 2), (0, 0)))[:, None],
        ],
        axis=1,
    )
    depth = sheet.shape[1]
    sheet = summed_everywhere(sheet.reshape(spread * depth, channels)).reshape(
        spread, depth, channels
    )
    moments = sheet[:, : depth - 1].reshape(2 * G, channels)
    channel_mean = sheet[0, depth - 1] / voxels
    target_sum = sheet[1, depth - 1]
    mean_pair = channel_mean.reshape(groups, G)
    target_sum_pair = target_sum.reshape(groups, G)
    second = jnp.swapaxes(moments[:G].reshape(G, groups, G), 0, 1)
    cross = jnp.swapaxes(moments[G:].reshape(G, groups, G), 0, 1)
    centered_second = second - voxels * mean_pair[:, :, None] * mean_pair[:, None, :]
    centered_cross = cross - target_sum_pair[:, :, None] * mean_pair[:, None, :]
    covariance = centered_second / voxels + EPSILON * eye_block
    whitener, whiten_pull = jax.vjp(newton_whitener, covariance)
    white_grad = jnp.matmul(whitener, centered_second, precision=HIGHEST) - centered_cross
    residue_sum = -target_sum_pair
    sigma_grad = whiten_pull(white_grad)[0]
    symmetric = (sigma_grad + jnp.swapaxes(sigma_grad, 1, 2)) / voxels

    centered = (hidden_wide - channel_mean).reshape(count_local, groups, G)
    white = jnp.einsum("gab,vgb->vga", whitener, centered, precision=HIGHEST)
    whitened = white.reshape(volume.shape).astype(jnp.bfloat16)
    residue = white - target.reshape(count_local, groups, G).astype(jnp.float32)
    grad_wide = jnp.einsum(
        "gba,vgb->vga", whitener, residue - residue_sum / voxels, precision=HIGHEST
    )
    grad_wide = grad_wide + jnp.einsum("gab,vgb->vga", symmetric, centered, precision=HIGHEST)
    grad_hidden = grad_wide.reshape(count_local, channels).astype(jnp.bfloat16)

    terms = weight_terms(slab_list, grad_hidden).astype(jnp.bfloat16)
    rows_y = lax.axis_size("y")
    share = channels // lax.axis_size(GY)
    taps = terms.shape[0]
    taps_each = -(-taps // rows_y)
    terms = jnp.pad(terms, ((0, taps_each * rows_y - taps), (0, 0), (0, 0)))
    terms = terms.reshape(rows_y, taps_each, lax.axis_size(GY), share, channels)
    terms = jnp.swapaxes(terms, 1, 2).reshape(spread, taps_each * share, channels)
    part = exchange(terms, SPREAD).astype(jnp.float32).sum(0)
    part = exchange(copies(part.astype(jnp.bfloat16), lax.axis_size("z")), ("z",))
    part = part.astype(jnp.float32).sum(0) * (1.0 / math.sqrt(voxels))
    whole = exchange(copies(part, rows_y), ("y",))
    weight_grad = whole.reshape(rows_y * taps_each, share, channels)[:taps]
    weight_grad = weight_grad.reshape(3, 3, 3, share, channels)

    grad_padded = pad_columns(extended_fast(grad_hidden.reshape(volume.shape)))
    flipped = jnp.swapaxes(jnp.flip(conv_weight, (0, 1, 2)), 3, 4)
    input_grad = apply_taps(tap_slabs(grad_padded, depth_cells, row_cells, column_cells), flipped)
    input_grad = input_grad.astype(jnp.bfloat16).reshape(volume.shape)
    return (whitened, input_grad, weight_grad)


def solution(mesh):
    cells = mesh.devices.reshape(4, 8, 4, 2)
    split = Mesh(cells, ("y", "z", "x", "c"))
    in_specs = (P(GZ, GY, None, None), P(), P(GZ, GY, None, None))
    out_specs = (
        P(GZ, GY, None, None),
        P(GZ, GY, None, None),
        P(None, None, None, GY, None),
    )
    return jax.shard_map(local, mesh=split, in_specs=in_specs, out_specs=out_specs, check_vma=False)
```

time: 601 us -> 185 us (0.31)
  blocking collectives: 228 us -> 0 us
  waiting for transfers between devices: 251 us -> 33.1 us
  starting transfers between devices: 21.7 us -> 74.6 us
  matrix products: 43.4 us -> 28.7 us
  between operations: 15.5 us -> 2.23 us
    psum x1 -> x0, waiting for transfers between devices: 246 us -> none  [local(): summed = lax.psum(local_term, ('gz', 'gy'))]
    psum x3 -> x0, blocking collectives: 228 us -> none  [the longest x1 79.7 us: local(): channel_sum = lax.psum(jnp.sum(hidden_wide, axis=0), ('gz', 'gy'))]
    all_to_all x0 -> x6, starting transfers between devices: none -> 42.4 us  [exchange(): return lax.all_to_all(parts, axes, 0, 0, tiled=True)]
    all_to_all x0 -> x6, waiting for transfers between devices: none -> 23.5 us  [exchange(): return lax.all_to_all(parts, axes, 0, 0, tiled=True)]
    ppermute x8 -> x12, starting transfers between devices: 21.7 us -> 32.1 us  [shifted_from(): return lax.ppermute(block, axes, pairs)]
  transfers between devices with their start and end apart: 9 -> 18, of which waited for: 5 -> 7; matrix products, arithmetic and copies ran while one was open for 5% -> 23% of each run, Pallas kernels for 0% -> 0%
where the time goes in v1:
time: 185 us; the launch traced here: 184 us
  starting transfers between devices  74.6 us (40%)
  waiting for transfers between devices  33.1 us (18%)
  local copies, waits for them, and re-layouts  30.8 us (17%)
  matrix products  28.7 us (16%)
  other arithmetic  14.2 us (8%)
  between operations  2.23 us (1%)
    all_to_all x6, starting transfers between devices, exchange(): return lax.all_to_all(parts, axes, 0, 0, tiled=True)  42.4 us
    ppermute x12, starting transfers between devices, shifted_from(): return lax.ppermute(block, axes, pairs)  32.1 us
    all_to_all x6, waiting for transfers between devices, exchange(): return lax.all_to_all(parts, axes, 0, 0, tiled=True)  23.5 us
    dot_general x18, matrix products, apply_taps(): jnp.dot(slab_list[index_tap], kernel_rows, preferred_element_type=jnp.flo...  10.1 us
    ppermute x12, waiting for transfers between devices, shifted_from(): return lax.ppermute(block, axes, pairs)  9.62 us
    reshape x9, local copies, waits for them, and re-layouts, tap_slabs(): merged.reshape(depth_cells * row_cells * column_cells, merged.shape[-1])  8.91 us
    concatenate x2, other arithmetic, extended_fast(): return jnp.concatenate(planes, axis=0)  7.11 us
    unnamed x126, local copies, waits for them, and re-layouts  6.07 us
  transfers between devices with their start and end apart: 18, of which 7 were waited for; matrix products, arithmetic and copies ran while one was open for 23% of the time, Pallas kernels for 0%

profile of v1, /device:TPU:4, one launch (start us, length us, event | category | flops | bytes accessed | tf_op | source)
XLA Modules:
  0.0 183.6 jit_solution(11972964896910133859)
XLA Ops:
  0.6 4.0 %collective-permute-start.3 = (bf16[1,8,128,128]{3,2,1,0:T(8,128)(2,1)}, bf16[1,8,128,128]{3,2,1,0:T(8,128)(2,1)S(1)}, u32[]{:S(2)}, u32[]{:S(2)}) collective-permute-start(bf16[1,8,128,128]{3,2,1,0:T(8,128)(2,1)} %param.3), channel_id=1, source_target_pairs={{0,8},{8,16},{16,24},{24,32},{32,40},{40,48},{48,56},{56,64},{64,7... | collective-permute-start | bytes 786440 | tf_op jit(solution)/shard_map/ppermute | solution.py:19
  4.6 1.3 collective-permute-start.5
  5.9 0.8 fusion.199
  6.7 1.9 %collective-permute-start = (bf16[1,1,128,128]{3,2,1,0:T(8,128)(2,1)S(1)}, bf16[1,1,128,128]{3,2,1,0:T(8,128)(2,1)S(1)}, u32[]{:S(2)}, u32[]{:S(2)}) collective-permute-start(bf16[1,1,128,128]{3,2,1,0:T(8,128)(2,1)S(1)} %get-tuple-element.91), channel_id=1, source_target_pairs={{0,1},{1,2},{2,3},{3,4},{4,5},{5,6},{6,7},{8,9},{9,10},{10,11},{11... | collective-permute-start | bytes 98312 | tf_op jit(solution)/shard_map/ppermute | solution.py:19
  8.6 3.6 %collective-permute-start.1 = (bf16[1,1,128,128]{3,2,1,0:T(8,128)(2,1)S(1)}, bf16[1,1,128,128]{3,2,1,0:T(8,128)(2,1)S(1)}, u32[]{:S(2)}, u32[]{:S(2)}) collective-permute-start(bf16[1,1,128,128]{3,2,1,0:T(8,128)(2,1)S(1)} %get-tuple-element.90), channel_id=1, source_target_pairs={{1,0},{2,1},{3,2},{4,3},{5,4},{6,5},{7,6},{9,8},{10,9},{11,10},{12... | collective-permute-start | bytes 98312 | tf_op jit(solution)/shard_map/ppermute | solution.py:19
  12.3 2.1 %fusion.197 = (bf16[1,1,3,128,128]{4,3,2,1,0:T(8,128)(2,1)S(1)}, bf16[1,1,3,128,128]{4,3,2,1,0:T(8,128)(2,1)}, bf16[1,1,3,128,128]{4,3,2,1,0:T(8,128)(2,1)}, bf1...) fusion(bf16[3,3,3,128,128]{4,3,2,1,0:T(8,128)(2,1)} %param.4), kind=kLoop, calls=%fused_computation.316 | loop fusion | bytes 1769472 | tf_op jit(solution)/shard_map/slice | solution.py:80
  14.4 1.4 copy.165
  16.2 1.0 fusion.196
  17.2 0.8 fusion.154
  18.2 0.9 reshape_reshape.3
  19.1 4.6 %collective-permute-start.2 = (bf16[1,2,128,128]{3,2,1,0:T(8,128)(2,1)S(1)}, bf16[1,2,128,128]{3,2,1,0:T(8,128)(2,1)S(1)}, u32[]{:S(2)}, u32[]{:S(2)}) collective-permute-start(bf16[1,2,128,128]{3,2,1,0:T(8,128)(2,1)S(1)} %constant_dynamic-update-slice_fusion), channel_id=1, source_target_pairs={{0,8},{8,16},{16,24},{24,32},{32,40},{40,48},{48,56},{56,64},{64,7... | collective-permute-start | bytes 196616 | tf_op jit(solution)/shard_map/ppermute | solution.py:19
  23.8 1.3 collective-permute-start.4
  25.6 4.4 %collective-permute-done.4 = bf16[1,2,128,128]{3,2,1,0:T(8,128)(2,1)S(1)} collective-permute-done((bf16[1,2,128,128]{3,2,1,0:T(8,128)(2,1)S(1)}, bf16[1,2,128,128]{3,2,1,0:T(8,128)(2,1)S(1)}, u32[]{:S(2)}, u32[]{:S(2)}) %collective-permute-start.4) | collective-permute-done | bytes 65568 | tf_op jit(solution)/shard_map/ppermute | solution.py:19
  30.0 1.1 fusion.22
  31.2 0.9 fusion.195
  32.1 1.5 fusion.65
  40.2 0.7 copy.140
  41.0 0.8 pad_maximum_fusion.18
  41.8 0.7 pad_maximum_fusion.17
  42.5 11.3 %all-to-all-start = ((f32[32,5,128]{2,1,0:T(8,128)}), f32[32,5,128]{2,1,0:T(8,128)S(1)}, u32[]{:S(2)}, u32[]{:S(2)}) async-start(f32[32,5,128]{2,1,0:T(8,128)} %pad_maximum_fusion.17), calls=%async_computation | async-start | bytes 262144 | tf_op jit(solution)/shard_map/all_to_all | solution.py:99
  53.8 0.6 fusion.160
  54.4 4.9 %all-to-all-done = f32[32,5,128]{2,1,0:T(8,128)S(1)} async-done(((f32[32,5,128]{2,1,0:T(8,128)}), f32[32,5,128]{2,1,0:T(8,128)S(1)}, u32[]{:S(2)}, u32[]{:S(2)}) %all-to-all-start) | async-done | bytes 81952 | tf_op jit(solution)/shard_map/all_to_all | solution.py:99
  59.4 0.6 broadcast_in_dim.62
  60.0 5.8 %all-to-all-start.1 = ((f32[8,5,128]{2,1,0:T(8,128)}), f32[8,5,128]{2,1,0:T(8,128)S(1)}, u32[]{:S(2)}, u32[]{:S(2)}) async-start(f32[8,5,128]{2,1,0:T(8,128)} %broadcast_in_dim.62), calls=%async_computation.1 | async-start | bytes 65536 | tf_op jit(solution)/shard_map/all_to_all | solution.py:99
  65.8 1.5 copy.146
  67.3 0.7 copy.142
  68.0 5.9 %all-to-all-done.1 = f32[8,5,128]{2,1,0:T(8,128)S(1)} async-done(((f32[8,5,128]{2,1,0:T(8,128)}), f32[8,5,128]{2,1,0:T(8,128)S(1)}, u32[]{:S(2)}, u32[]{:S(2)}) %all-to-all-start.1) | async-done | bytes 20512 | tf_op jit(solution)/shard_map/all_to_all | solution.py:99
  73.9 0.7 broadcast_in_dim.63
  74.5 6.0 %all-to-all-start.2 = ((f32[32,5,128]{2,1,0:T(8,128)}), f32[32,5,128]{2,1,0:T(8,128)S(1)}, u32[]{:S(2)}, u32[]{:S(2)}) async-start(f32[32,5,128]{2,1,0:T(8,128)} %broadcast_in_dim.63), calls=%async_computation.2 | async-start | bytes 262144 | tf_op jit(solution)/shard_map/all_to_all | solution.py:99
  80.6 1.2 copy.166
  81.8 1.2 copy.168
  83.0 1.2 copy.170
  84.2 1.2 copy.172
  85.4 1.2 copy.174
  86.5 1.2 copy.176
  87.7 1.2 copy.178
  93.3 0.9 multiply_reduce_fusion.1
  101.6 1.3 fusion.205
  103.0 0.7 fusion.73
  103.7 0.7 fusion.9
  104.6 1.4 collective-permute-start.11
  106.0 4.6 %collective-permute-start.9 = (bf16[1,8,128,128]{2,1,3,0:T(8,128)(2,1)S(1)}, bf16[1,8,128,128]{2,1,3,0:T(8,128)(2,1)S(1)}, u32[]{:S(2)}, u32[]{:S(2)}) collective-permute-start(bf16[1,8,128,128]{2,1,3,0:T(8,128)(2,1)S(1)} %bitcast.319), channel_id=1, source_target_pairs={{0,8},{8,16},{16,24},{24,32},{32,40},{40,48},{48,56},{56,64},{64,7... | collective-permute-start | bytes 786440 | tf_op jit(solution)/shard_map/ppermute | solution.py:19
  110.6 1.9 %collective-permute-start.6 = (bf16[1,1,128,128]{2,1,3,0:T(2,128)(2,1)S(1)}, bf16[1,1,128,128]{2,1,3,0:T(2,128)(2,1)S(1)}, u32[]{:S(2)}, u32[]{:S(2)}) collective-permute-start(bf16[1,1,128,128]{2,1,3,0:T(2,128)(2,1)S(1)} %get-tuple-element.79), channel_id=1, source_target_pairs={{0,1},{1,2},{2,3},{3,4},{4,5},{5,6},{6,7},{8,9},{9,10},{10,11},{11... | collective-permute-start | bytes 98312 | tf_op jit(solution)/shard_map/ppermute | solution.py:19
  112.5 3.9 %collective-permute-start.7 = (bf16[1,1,128,128]{2,1,3,0:T(2,128)(2,1)S(1)}, bf16[1,1,128,128]{2,1,3,0:T(2,128)(2,1)S(1)}, u32[]{:S(2)}, u32[]{:S(2)}) collective-permute-start(bf16[1,1,128,128]{2,1,3,0:T(2,128)(2,1)S(1)} %get-tuple-element.80), channel_id=1, source_target_pairs={{1,0},{2,1},{3,2},{4,3},{5,4},{6,5},{7,6},{9,8},{10,9},{11,10},{12... | collective-permute-start | bytes 98312 | tf_op jit(solution)/shard_map/ppermute | solution.py:19
  120.0 2.4 %collective-permute-start.8 = (bf16[1,2,128,128]{2,1,3,0:T(2,128)(2,1)S(1)}, bf16[1,2,128,128]{2,1,3,0:T(2,128)(2,1)S(1)}, u32[]{:S(2)}, u32[]{:S(2)}) collective-permute-start(bf16[1,2,128,128]{2,1,3,0:T(2,128)(2,1)S(1)} %pad_maximum_fusion.19), channel_id=1, source_target_pairs={{0,8},{8,16},{16,24},{24,32},{32,40},{40,48},{48,56},{56,64},{64,7... | collective-permute-start | bytes 196616 | tf_op jit(solution)/shard_map/ppermute | solution.py:19
  123.0 1.1 copy.184
  124.2 7.6 %all-to-all-start.3 = ((bf16[32,112,128]{2,1,0:T(8,128)(2,1)}), bf16[32,112,128]{2,1,0:T(8,128)(2,1)S(1)}, u32[]{:S(2)}, u32[]{:S(2)}) async-start(bf16[32,112,128]{2,1,0:T(8,128)(2,1)} %bitcast.76), calls=%async_computation.3 | async-start | bytes 1835008 | tf_op jit(solution)/shard_map/all_to_all | solution.py:99
  131.8 0.9 copy.185
  132.7 1.3 collective-permute-start.10
  134.1 4.7 %collective-permute-done.10 = bf16[1,2,128,128]{2,1,3,0:T(2,128)(2,1)S(1)} collective-permute-done((bf16[1,2,128,128]{2,1,3,0:T(2,128)(2,1)S(1)}, bf16[1,2,128,128]{2,1,3,0:T(2,128)(2,1)S(1)}, u32[]{:S(2)}, u32[]{:S(2)}) %collective-permute-start.10) | collective-permute-done | bytes 65568 | tf_op jit(solution)/shard_map/ppermute | solution.py:19
  139.0 6.0 %fusion.1 = bf16[3,10,130,128]{2,1,3,0:T(8,128)(2,1)S(1)} fusion(bf16[1,1,128,128]{2,1,3,0:T(2,128)(2,1)S(1)} %get-tuple-element.98, bf16[1,8,128,128]{2,1,3,0:T(8,128)(2,1)S(1)} %collective-permute-done.11, bf16[1,1,128,128]{2,1,3,0:T(2,128)(2,1)S(1)} %get-tuple-element.97, bf16[1,1,128,128]{2,1,3,0:T(2,128)(2,1)S(1)} %copy-done.30, ...), kind=kLoop, calls=%fused_computation.4 | loop fusion | flops 14976000 | bytes 1981440 | tf_op jit(solution)/shard_map/concatenate | solution.py:35
  145.0 1.6 fusion.194
  149.0 1.3 fusion.45
  150.6 0.6 copy-done.35
  153.0 0.7 broadcast_in_dim.70
  153.7 7.5 %all-to-all-start.4 = ((bf16[8,112,128]{2,1,0:T(8,128)(2,1)}), bf16[8,112,128]{2,1,0:T(8,128)(2,1)S(1)}, u32[]{:S(2)}, u32[]{:S(2)}) async-start(bf16[8,112,128]{2,1,0:T(8,128)(2,1)} %broadcast_in_dim.70), calls=%async_computation.4 | async-start | bytes 458752 | tf_op jit(solution)/shard_map/all_to_all | solution.py:99
  161.2 1.5 convolution_add_fusion.2
  162.8 1.3 convolution_add_fusion.1
  164.1 7.3 %all-to-all-done.4 = bf16[8,112,128]{2,1,0:T(8,128)(2,1)S(1)} async-done(((bf16[8,112,128]{2,1,0:T(8,128)(2,1)}), bf16[8,112,128]{2,1,0:T(8,128)(2,1)S(1)}, u32[]{:S(2)}, u32[]{:S(2)}) %all-to-all-start.4) | async-done | bytes 229408 | tf_op jit(solution)/shard_map/all_to_all | solution.py:99
  171.4 0.7 broadcast_in_dim.71
  172.2 4.2 %all-to-all-start.5 = ((f32[4,112,128]{2,1,0:T(8,128)}), f32[4,112,128]{2,1,0:T(8,128)S(1)}, u32[]{:S(2)}, u32[]{:S(2)}) async-start(f32[4,112,128]{2,1,0:T(8,128)} %broadcast_in_dim.71), calls=%async_computation.5 | async-start | bytes 458752 | tf_op jit(solution)/shard_map/all_to_all | solution.py:99
  176.4 1.1 fusion.8
  177.5 5.4 %all-to-all-done.5 = f32[4,112,128]{2,1,0:T(8,128)S(1)} async-done(((f32[4,112,128]{2,1,0:T(8,128)}), f32[4,112,128]{2,1,0:T(8,128)S(1)}, u32[]{:S(2)}, u32[]{:S(2)}) %all-to-all-start.5) | async-done | bytes 229408 | tf_op jit(solution)/shard_map/all_to_all | solution.py:99
  182.9 0.7 slice.450
  (242 shorter events, 27.9 us)
Async XLA Ops:
  0.6 13.8 %copy-start.10 = (bf16[3,3,3,128,128]{4,3,2,1,0:T(8,128)(2,1)S(1)}, bf16[3,3,3,128,128]{4,3,2,1,0:T(8,128)(2,1)}, u32[]{:S(2)}) copy-start(bf16[3,3,3,128,128]{4,3,2,1,0:T(8,128)(2,1)} %param.4) | copy-start | bytes 2654212
  0.6 29.3 %collective-permute-start.3 = (bf16[1,8,128,128]{3,2,1,0:T(8,128)(2,1)}, bf16[1,8,128,128]{3,2,1,0:T(8,128)(2,1)S(1)}, u32[]{:S(2)}, u32[]{:S(2)}) collective-permute-start(bf16[1,8,128,128]{3,2,1,0:T(8,128)(2,1)} %param.3), channel_id=1, source_target_pairs={{0,8},{8,16},{16,24},{24,32},{32,40},{40,48},{48,56},{56,64},{64,7... | collective-permute-start | bytes 786440 | tf_op jit(solution)/shard_map/ppermute | solution.py:19
  4.6 25.4 %collective-permute-start.5 = (bf16[1,8,128,128]{3,2,1,0:T(8,128)(2,1)}, bf16[1,8,128,128]{3,2,1,0:T(8,128)(2,1)S(1)}, u32[]{:S(2)}, u32[]{:S(2)}) collective-permute-start(bf16[1,8,128,128]{3,2,1,0:T(8,128)(2,1)} %param.3), channel_id=1, source_target_pairs={{8,0},{16,8},{24,16},{32,24},{40,32},{48,40},{56,48},{64,56},{72,6... | collective-permute-start | bytes 786440 | tf_op jit(solution)/shard_map/ppermute | solution.py:19
  6.7 12.3 %collective-permute-start = (bf16[1,1,128,128]{3,2,1,0:T(8,128)(2,1)S(1)}, bf16[1,1,128,128]{3,2,1,0:T(8,128)(2,1)S(1)}, u32[]{:S(2)}, u32[]{:S(2)}) collective-permute-start(bf16[1,1,128,128]{3,2,1,0:T(8,128)(2,1)S(1)} %get-tuple-element.91), channel_id=1, source_target_pairs={{0,1},{1,2},{2,3},{3,4},{4,5},{5,6},{6,7},{8,9},{9,10},{10,11},{11... | collective-permute-start | bytes 98312 | tf_op jit(solution)/shard_map/ppermute | solution.py:19
  8.6 10.4 %collective-permute-start.1 = (bf16[1,1,128,128]{3,2,1,0:T(8,128)(2,1)S(1)}, bf16[1,1,128,128]{3,2,1,0:T(8,128)(2,1)S(1)}, u32[]{:S(2)}, u32[]{:S(2)}) collective-permute-start(bf16[1,1,128,128]{3,2,1,0:T(8,128)(2,1)S(1)} %get-tuple-element.90), channel_id=1, source_target_pairs={{1,0},{2,1},{3,2},{4,3},{5,4},{6,5},{7,6},{9,8},{10,9},{11,10},{12... | collective-permute-start | bytes 98312 | tf_op jit(solution)/shard_map/ppermute | solution.py:19
  16.1 1.9 %copy-start.22 = (bf16[1,8,128,128]{3,2,1,0:T(8,128)(2,1)S(1)}, bf16[1,8,128,128]{3,2,1,0:T(8,128)(2,1)}, u32[]{:S(2)}) copy-start(bf16[1,8,128,128]{3,2,1,0:T(8,128)(2,1)} %param.5) | copy-start | bytes 786436
  16.2 13.8 %copy-start.20 = (bf16[1,8,128,128]{3,2,1,0:T(8,128)(2,1)S(1)}, bf16[1,8,128,128]{3,2,1,0:T(8,128)(2,1)}, u32[]{:S(2)}) copy-start(bf16[1,8,128,128]{3,2,1,0:T(8,128)(2,1)} %param.3) | copy-start | bytes 786436
  19.0 13.0 %copy-start.47 = (bf16[1,1,128,128]{3,2,1,0:T(8,128)(2,1)}, bf16[1,1,128,128]{3,2,1,0:T(8,128)(2,1)S(1)}, u32[]{:S(2)}) copy-start(bf16[1,1,128,128]{3,2,1,0:T(8,128)(2,1)S(1)} %collective-permute-done.1) | copy-start | bytes 98308
  19.1 6.5 %collective-permute-start.2 = (bf16[1,2,128,128]{3,2,1,0:T(8,128)(2,1)S(1)}, bf16[1,2,128,128]{3,2,1,0:T(8,128)(2,1)S(1)}, u32[]{:S(2)}, u32[]{:S(2)}) collective-permute-start(bf16[1,2,128,128]{3,2,1,0:T(8,128)(2,1)S(1)} %constant_dynamic-update-slice_fusion), channel_id=1, source_target_pairs={{0,8},{8,16},{16,24},{24,32},{32,40},{40,48},{48,56},{56,64},{64,7... | collective-permute-start | bytes 196616 | tf_op jit(solution)/shard_map/ppermute | solution.py:19
  23.8 6.1 %collective-permute-start.4 = (bf16[1,2,128,128]{3,2,1,0:T(8,128)(2,1)S(1)}, bf16[1,2,128,128]{3,2,1,0:T(8,128)(2,1)S(1)}, u32[]{:S(2)}, u32[]{:S(2)}) collective-permute-start(bf16[1,2,128,128]{3,2,1,0:T(8,128)(2,1)S(1)} %constant_dynamic-update-slice_fusion), channel_id=1, source_target_pairs={{8,0},{16,8},{24,16},{32,24},{40,32},{48,40},{56,48},{64,56},{72,6... | collective-permute-start | bytes 196616 | tf_op jit(solution)/shard_map/ppermute | solution.py:19
  30.0 2.1 %copy-start.25 = (bf16[1,8,128,128]{3,2,1,0:T(8,128)(2,1)}, bf16[1,8,128,128]{3,2,1,0:T(8,128)(2,1)S(1)}, u32[]{:S(2)}) copy-start(bf16[1,8,128,128]{3,2,1,0:T(8,128)(2,1)S(1)} %collective-permute-done.3) | copy-start | bytes 786436
  30.0 2.1 %copy-start.23 = (bf16[1,8,128,128]{3,2,1,0:T(8,128)(2,1)}, bf16[1,8,128,128]{3,2,1,0:T(8,128)(2,1)S(1)}, u32[]{:S(2)}) copy-start(bf16[1,8,128,128]{3,2,1,0:T(8,128)(2,1)S(1)} %collective-permute-done.5) | copy-start | bytes 786436
  32.1 1.5 copy-start.46
  32.1 2.0 %copy-start.45 = (bf16[1,1,3,128,128]{4,3,2,1,0:T(8,128)(2,1)S(1)}, bf16[1,1,3,128,128]{4,3,2,1,0:T(8,128)(2,1)}, u32[]{:S(2)}) copy-start(bf16[1,1,3,128,128]{4,3,2,1,0:T(8,128)(2,1)} %get-tuple-element.69) | copy-start | bytes 294916
  35.2 1.5 copy-start
  35.3 1.5 copy-start.2
  35.3 1.0 copy-start.42
  37.6 1.5 copy-start.6
  37.6 1.5 copy-start.8
  37.6 1.5 copy-start.4
  37.6 1.0 copy-start.39
  42.5 16.9 %all-to-all-start = ((f32[32,5,128]{2,1,0:T(8,128)}), f32[32,5,128]{2,1,0:T(8,128)S(1)}, u32[]{:S(2)}, u32[]{:S(2)}) async-start(f32[32,5,128]{2,1,0:T(8,128)} %pad_maximum_fusion.17), calls=%async_computation | async-start | bytes 262144 | tf_op jit(solution)/shard_map/all_to_all | solution.py:99
  60.0 13.9 %all-to-all-start.1 = ((f32[8,5,128]{2,1,0:T(8,128)}), f32[8,5,128]{2,1,0:T(8,128)S(1)}, u32[]{:S(2)}, u32[]{:S(2)}) async-start(f32[8,5,128]{2,1,0:T(8,128)} %broadcast_in_dim.62), calls=%async_computation.1 | async-start | bytes 65536 | tf_op jit(solution)/shard_map/all_to_all | solution.py:99
  74.5 15.0 %all-to-all-start.2 = ((f32[32,5,128]{2,1,0:T(8,128)}), f32[32,5,128]{2,1,0:T(8,128)S(1)}, u32[]{:S(2)}, u32[]{:S(2)}) async-start(f32[32,5,128]{2,1,0:T(8,128)} %broadcast_in_dim.63), calls=%async_computation.2 | async-start | bytes 262144 | tf_op jit(solution)/shard_map/all_to_all | solution.py:99
  81.8 2.4 %copy-start.3 = (bf16[1,8,128,384]{3,2,1,0:T(8,128)(2,1)S(1)}, bf16[1,8,128,384]{3,2,1,0:T(8,128)(2,1)}, u32[]{:S(2)}) copy-start(bf16[1,8,128,384]{3,2,1,0:T(8,128)(2,1)} %copy-done.2) | copy-start | bytes 2359300
  83.0 2.4 %copy-start.1 = (bf16[1,8,128,384]{3,2,1,0:T(8,128)(2,1)S(1)}, bf16[1,8,128,384]{3,2,1,0:T(8,128)(2,1)}, u32[]{:S(2)}) copy-start(bf16[1,8,128,384]{3,2,1,0:T(8,128)(2,1)} %copy-done) | copy-start | bytes 2359300
  85.4 2.4 %copy-start.9 = (bf16[1,8,128,384]{3,2,1,0:T(8,128)(2,1)S(1)}, bf16[1,8,128,384]{3,2,1,0:T(8,128)(2,1)}, u32[]{:S(2)}) copy-start(bf16[1,8,128,384]{3,2,1,0:T(8,128)(2,1)} %copy-done.8) | copy-start | bytes 2359300
  86.5 2.4 %copy-start.7 = (bf16[1,8,128,384]{3,2,1,0:T(8,128)(2,1)S(1)}, bf16[1,8,128,384]{3,2,1,0:T(8,128)(2,1)}, u32[]{:S(2)}) copy-start(bf16[1,8,128,384]{3,2,1,0:T(8,128)(2,1)} %copy-done.6) | copy-start | bytes 2359300
  87.7 1.5 copy-start.5
  88.9 1.2 copy-start.49
  90.1 10.9 %copy-start.54 = (f32[2]{0:T(128)}, f32[2]{0:T(128)S(1)}, u32[]{:S(2)}) copy-start(f32[2]{0:T(128)S(1)} %select_reduce_fusion) | copy-start | bytes 28
  90.1 9.1 %copy-start.56 = (f32[2]{0:T(128)}, f32[2]{0:T(128)S(1)}, u32[]{:S(2)}) copy-start(f32[2]{0:T(128)S(1)} %get-tuple-element.107) | copy-start | bytes 28
  97.5 3.5 %copy-start.50 = (f32[2,64,64]{2,1,0:T(8,128)S(1)}, f32[2,64,64]{2,1,0:T(8,128)}, u32[]{:S(2)}) copy-start(f32[2,64,64]{2,1,0:T(8,128)} %fusion.154) | copy-start | bytes 98308
  99.5 2.1 %copy-start.57 = (f32[2]{0:T(128)S(1)}, f32[2]{0:T(128)}, u32[]{:S(2)}) copy-start(f32[2]{0:T(128)} %copy-done.56) | copy-start | bytes 28
  100.4 2.6 %copy-start.58 = (f32[2]{0:T(128)S(1)}, f32[2]{0:T(128)}, u32[]{:S(2)}) copy-start(f32[2]{0:T(128)} %get-tuple-element.112) | copy-start | bytes 28
  100.4 2.6 %copy-start.19 = (bf16[1024,2,64]{0,2,1:T(8,128)(2,1)S(1)}, bf16[1024,2,64]{0,2,1:T(8,128)(2,1)}, u32[]{:S(2)}) copy-start(bf16[1024,2,64]{0,2,1:T(8,128)(2,1)} %reshape_reshape.3) | copy-start | bytes 786436
  101.4 1.5 copy-start.55
  103.0 13.4 %copy-start.16 = (bf16[1024,384]{0,1:T(8,128)(2,1)S(1)}, bf16[1024,384]{0,1:T(8,128)(2,1)}, u32[]{:S(2)}) copy-start(bf16[1024,384]{0,1:T(8,128)(2,1)} %copy.166) | copy-start | bytes 2359300
  103.7 13.1 %copy-start.17 = (bf16[1024,384]{0,1:T(8,128)(2,1)S(1)}, bf16[1024,384]{0,1:T(8,128)(2,1)}, u32[]{:S(2)}) copy-start(bf16[1024,384]{0,1:T(8,128)(2,1)} %copy.168) | copy-start | bytes 2359300
  104.4 12.8 %copy-start.15 = (bf16[1024,384]{0,1:T(8,128)(2,1)S(1)}, bf16[1024,384]{0,1:T(8,128)(2,1)}, u32[]{:S(2)}) copy-start(bf16[1024,384]{0,1:T(8,128)(2,1)} %copy.170) | copy-start | bytes 2359300
  104.6 34.4 %collective-permute-start.11 = (bf16[1,8,128,128]{2,1,3,0:T(8,128)(2,1)S(1)}, bf16[1,8,128,128]{2,1,3,0:T(8,128)(2,1)S(1)}, u32[]{:S(2)}, u32[]{:S(2)}) collective-permute-start(bf16[1,8,128,128]{2,1,3,0:T(8,128)(2,1)S(1)} %bitcast.318), channel_id=1, source_target_pairs={{8,0},{16,8},{24,16},{32,24},{40,32},{48,40},{56,48},{64,56},{72,6... | collective-permute-start | bytes 786440 | tf_op jit(solution)/shard_map/ppermute | solution.py:19
  106.0 33.0 %collective-permute-start.9 = (bf16[1,8,128,128]{2,1,3,0:T(8,128)(2,1)S(1)}, bf16[1,8,128,128]{2,1,3,0:T(8,128)(2,1)S(1)}, u32[]{:S(2)}, u32[]{:S(2)}) collective-permute-start(bf16[1,8,128,128]{2,1,3,0:T(8,128)(2,1)S(1)} %bitcast.319), channel_id=1, source_target_pairs={{0,8},{8,16},{16,24},{24,32},{32,40},{40,48},{48,56},{56,64},{64,7... | collective-permute-start | bytes 786440 | tf_op jit(solution)/shard_map/ppermute | solution.py:19
  110.6 9.2 %collective-permute-start.6 = (bf16[1,1,128,128]{2,1,3,0:T(2,128)(2,1)S(1)}, bf16[1,1,128,128]{2,1,3,0:T(2,128)(2,1)S(1)}, u32[]{:S(2)}, u32[]{:S(2)}) collective-permute-start(bf16[1,1,128,128]{2,1,3,0:T(2,128)(2,1)S(1)} %get-tuple-element.79), channel_id=1, source_target_pairs={{0,1},{1,2},{2,3},{3,4},{4,5},{5,6},{6,7},{8,9},{9,10},{10,11},{11... | collective-permute-start | bytes 98312 | tf_op jit(solution)/shard_map/ppermute | solution.py:19
  112.5 7.3 %collective-permute-start.7 = (bf16[1,1,128,128]{2,1,3,0:T(2,128)(2,1)S(1)}, bf16[1,1,128,128]{2,1,3,0:T(2,128)(2,1)S(1)}, u32[]{:S(2)}, u32[]{:S(2)}) collective-permute-start(bf16[1,1,128,128]{2,1,3,0:T(2,128)(2,1)S(1)} %get-tuple-element.80), channel_id=1, source_target_pairs={{1,0},{2,1},{3,2},{4,3},{5,4},{6,5},{7,6},{9,8},{10,9},{11,10},{12... | collective-permute-start | bytes 98312 | tf_op jit(solution)/shard_map/ppermute | solution.py:19
  116.4 1.3 copy-start.14
  116.8 1.3 copy-start.13
  117.2 1.3 copy-start.12
  117.7 1.3 copy-start.11
  119.8 3.2 %copy-start.26 = (bf16[1,1,128,128]{2,1,3,0:T(2,128)(2,1)}, bf16[1,1,128,128]{2,1,3,0:T(2,128)(2,1)S(1)}, u32[]{:S(2)}) copy-start(bf16[1,1,128,128]{2,1,3,0:T(2,128)(2,1)S(1)} %collective-permute-done.6) | copy-start | bytes 98308
  119.9 3.1 %copy-start.29 = (bf16[1,1,128,128]{2,1,3,0:T(2,128)(2,1)}, bf16[1,1,128,128]{2,1,3,0:T(2,128)(2,1)S(1)}, u32[]{:S(2)}) copy-start(bf16[1,1,128,128]{2,1,3,0:T(2,128)(2,1)S(1)} %collective-permute-done.7) | copy-start | bytes 98308
  120.0 14.0 %collective-permute-start.8 = (bf16[1,2,128,128]{2,1,3,0:T(2,128)(2,1)S(1)}, bf16[1,2,128,128]{2,1,3,0:T(2,128)(2,1)S(1)}, u32[]{:S(2)}, u32[]{:S(2)}) collective-permute-start(bf16[1,2,128,128]{2,1,3,0:T(2,128)(2,1)S(1)} %pad_maximum_fusion.19), channel_id=1, source_target_pairs={{0,8},{8,16},{16,24},{24,32},{32,40},{40,48},{48,56},{56,64},{64,7... | collective-permute-start | bytes 196616 | tf_op jit(solution)/shard_map/ppermute | solution.py:19
  123.0 8.8 %copy-start.21 = (bf16[1024,2,64]{0,2,1:T(8,128)(2,1)S(1)}, bf16[1024,2,64]{0,2,1:T(8,128)(2,1)}, u32[]{:S(2)}) copy-start(bf16[1024,2,64]{0,2,1:T(8,128)(2,1)} %get-tuple-element.110) | copy-start | bytes 786436
  124.2 14.9 %copy-start.27 = (bf16[1,1,128,128]{2,1,3,0:T(2,128)(2,1)S(1)}, bf16[1,1,128,128]{2,1,3,0:T(2,128)(2,1)}, u32[]{:S(2)}) copy-start(bf16[1,1,128,128]{2,1,3,0:T(2,128)(2,1)} %copy-done.26) | copy-start | bytes 98308
  124.2 14.9 %copy-start.30 = (bf16[1,1,128,128]{2,1,3,0:T(2,128)(2,1)S(1)}, bf16[1,1,128,128]{2,1,3,0:T(2,128)(2,1)}, u32[]{:S(2)}) copy-start(bf16[1,1,128,128]{2,1,3,0:T(2,128)(2,1)} %copy-done.29) | copy-start | bytes 98308
  124.2 28.7 %all-to-all-start.3 = ((bf16[32,112,128]{2,1,0:T(8,128)(2,1)}), bf16[32,112,128]{2,1,0:T(8,128)(2,1)S(1)}, u32[]{:S(2)}, u32[]{:S(2)}) async-start(bf16[32,112,128]{2,1,0:T(8,128)(2,1)} %bitcast.76), calls=%async_computation.3 | async-start | bytes 1835008 | tf_op jit(solution)/shard_map/all_to_all | solution.py:99
  132.7 6.1 %collective-permute-start.10 = (bf16[1,2,128,128]{2,1,3,0:T(2,128)(2,1)S(1)}, bf16[1,2,128,128]{2,1,3,0:T(2,128)(2,1)S(1)}, u32[]{:S(2)}, u32[]{:S(2)}) collective-permute-start(bf16[1,2,128,128]{2,1,3,0:T(2,128)(2,1)S(1)} %pad_maximum_fusion.19), channel_id=1, source_target_pairs={{8,0},{16,8},{24,16},{32,24},{40,32},{48,40},{56,48},{64,56},{72,6... | collective-permute-start | bytes 196616 | tf_op jit(solution)/shard_map/ppermute | solution.py:19
  146.8 1.3 copy-start.37
  149.0 1.3 copy-start.28
  149.0 1.3 copy-start.31
  150.6 1.0 copy-start.52
  152.5 8.7 %copy-start.33 = (bf16[1,1,3,128,128]{4,3,2,1,0:T(8,128)(2,1)S(1)}, bf16[1,1,3,128,128]{4,3,2,1,0:T(8,128)(2,1)}, u32[]{:S(2)}) copy-start(bf16[1,1,3,128,128]{4,3,2,1,0:T(8,128)(2,1)} %get-tuple-element.55) | copy-start | bytes 294916
  153.7 17.6 %all-to-all-start.4 = ((bf16[8,112,128]{2,1,0:T(8,128)(2,1)}), bf16[8,112,128]{2,1,0:T(8,128)(2,1)S(1)}, u32[]{:S(2)}, u32[]{:S(2)}) async-start(bf16[8,112,128]{2,1,0:T(8,128)(2,1)} %broadcast_in_dim.70), calls=%async_computation.4 | async-start | bytes 458752 | tf_op jit(solution)/shard_map/all_to_all | solution.py:99
  162.7 13.7 %copy-start.32 = (bf16[1,1,3,128,128]{4,3,2,1,0:T(8,128)(2,1)S(1)}, bf16[1,1,3,128,128]{4,3,2,1,0:T(8,128)(2,1)}, u32[]{:S(2)}) copy-start(bf16[1,1,3,128,128]{4,3,2,1,0:T(8,128)(2,1)} %get-tuple-element.53) | copy-start | bytes 294916
  172.2 10.8 %all-to-all-start.5 = ((f32[4,112,128]{2,1,0:T(8,128)}), f32[4,112,128]{2,1,0:T(8,128)S(1)}, u32[]{:S(2)}, u32[]{:S(2)}) async-start(f32[4,112,128]{2,1,0:T(8,128)} %broadcast_in_dim.71), calls=%async_computation.5 | async-start | bytes 458752 | tf_op jit(solution)/shard_map/all_to_all | solution.py:99
  (13 other events, 11.7 us)

commit v2 on v1

v2 whole, which is shorter than its diff:
```python
import math

import jax
import jax.numpy as jnp
from jax import lax
from jax.experimental import pallas as pl
from jax.experimental.pallas import tpu as pltpu
from jax.sharding import Mesh, PartitionSpec as P

G = 64
NEWTON = 5
EPSILON = 1e-05
HIGHEST = lax.Precision.HIGHEST
F32 = jnp.float32
BF16 = jnp.bfloat16
GZ = ("y", "z")
GY = ("x", "c")
SPREAD = ("y", "x", "c")
VMEM_BYTES = 48 * 1024 * 1024


def shifted_from(block, axes, count, step):
    pairs = [(i, i + step) for i in range(count) if 0 <= i + step < count]
    return lax.ppermute(block, axes, pairs)


def halo(block):
    nz = lax.axis_size(GZ)
    ny = lax.axis_size(GY)
    low = shifted_from(block[-1:], GY, ny, 1)
    high = shifted_from(block[:1], GY, ny, -1)
    below = shifted_from(block, GZ, nz, 1)
    above = shifted_from(block, GZ, nz, -1)
    edges = jnp.concatenate([low, high], axis=0)
    edges_below = shifted_from(edges, GZ, nz, 1)
    edges_above = shifted_from(edges, GZ, nz, -1)
    return (below, edges_below), (block, edges), (above, edges_above)


def call(kernel, out_shape, scratch, flops, moved, *operands):
    vmem = pl.BlockSpec(memory_space=pltpu.VMEM)
    many = isinstance(out_shape, (list, tuple))
    return pl.pallas_call(
        kernel,
        out_shape=out_shape,
        in_specs=[vmem] * len(operands),
        out_specs=[vmem] * len(out_shape) if many else vmem,
        scratch_shapes=scratch,
        compiler_params=pltpu.CompilerParams(vmem_limit_bytes=VMEM_BYTES),
        cost_estimate=pl.CostEstimate(flops=flops, bytes_accessed=moved, transcendentals=0),
    )(*operands)


def place_rows(wide, slot, plane, edge, tap_y):
    rows, _, channels = plane.shape
    cols = slice(slot * channels, (slot + 1) * channels)
    if tap_y == 0:
        wide[0:1, :, cols] = edge[0:1]
        wide[1:rows, :, cols] = plane[0 : rows - 1]
    elif tap_y == 1:
        wide[:, :, cols] = plane[...]
    else:
        wide[0 : rows - 1, :, cols] = plane[1:rows]
        wide[rows - 1 : rows, :, cols] = edge[1:2]


def moved_columns(flat, step, columns):
    count = flat.shape[0]
    column = lax.broadcasted_iota(jnp.int32, flat.shape, 0) % columns
    if step == 1:
        return jnp.where(column == 0, 0.0, pltpu.roll(flat, 1, 0))
    return jnp.where(column == columns - 1, 0.0, pltpu.roll(flat, count - 1, 0))


def over_rows(left, right):
    return lax.dot_general(left, right, (((0,), (0,)), ((), ())), preferred_element_type=F32)


def conv_kernel(
    below, below_edge, own, own_edge, above, above_edge, weight, target,
    hidden_out, sheet_out, wide, kernel_wide,
):
    rows, columns, channels = own.shape
    planes = ((below, below_edge), (own, own_edge), (above, above_edge))
    for tap_z in range(3):
        for tap_y in range(3):
            slot = tap_z * 3 + tap_y
            place_rows(wide, slot, planes[tap_z][0], planes[tap_z][1], tap_y)
            for tap_x in range(3):
                kernel_wide[
                    slot * channels : (slot + 1) * channels,
                    tap_x * channels : (tap_x + 1) * channels,
                ] = weight[slot * 3 + tap_x]
    flat = wide[...].reshape(rows * columns, 9 * channels)
    product = jnp.dot(flat, kernel_wide[...], preferred_element_type=F32)
    total = product[:, channels : 2 * channels]
    total = total + moved_columns(product[:, :channels], 1, columns)
    total = total + moved_columns(product[:, 2 * channels :], -1, columns)
    hidden = total.astype(BF16)
    hidden_out[...] = hidden
    features = target[...]
    second = over_rows(hidden, hidden)
    cross = over_rows(features, hidden)
    first = lax.broadcasted_iota(jnp.int32, (G, channels), 1) < G
    second = jnp.where(first, second[:G], second[G:])
    cross = jnp.where(first, cross[:G], cross[G:])
    spread, depth, _ = sheet_out.shape
    each = depth - 1
    half = spread // 2
    for j in range(half):
        sheet_out[j, 0:each, :] = second[each * j : each * (j + 1)]
        sheet_out[half + j, 0:each, :] = cross[each * j : each * (j + 1)]
    for j in range(2, spread):
        sheet_out[j, each:depth, :] = jnp.zeros((1, channels), F32)
    sheet_out[0, each:depth, :] = jnp.sum(hidden.astype(F32), axis=0, keepdims=True)
    sheet_out[1, each:depth, :] = jnp.sum(features.astype(F32), axis=0, keepdims=True)


def exact(left, right):
    return jnp.dot(left, right, precision=HIGHEST, preferred_element_type=F32)


def thirds(value):
    high = value.astype(BF16)
    rest = value - high.astype(F32)
    middle = rest.astype(BF16)
    return high, middle, (rest - middle.astype(F32)).astype(BF16)


def through(values, matrix):
    high, middle, low = thirds(matrix)
    total = jnp.dot(values, low, preferred_element_type=F32)
    total = total + jnp.dot(values, middle, preferred_element_type=F32)
    return total + jnp.dot(values, high, preferred_element_type=F32)


def whiten_kernel(voxels, sheet, hidden, target, whitened_out, grad_out, mats):
    spread, depth, channels = sheet.shape
    each = depth - 1
    for j in range(spread):
        mats[each * j : each * (j + 1), :] = sheet[j, 0:each, :]
    row = lax.broadcasted_iota(jnp.int32, (channels, channels), 0)
    col = lax.broadcasted_iota(jnp.int32, (channels, channels), 1)
    same = (row < G) == (col < G)
    diagonal = row == col
    low_lane = lax.broadcasted_iota(jnp.int32, (1, channels), 1) < G

    def group_sums(value):
        line = jnp.sum(value, axis=0, keepdims=True)
        low = jnp.sum(jnp.where(low_lane, line, 0.0), axis=1, keepdims=True)
        high = jnp.sum(jnp.where(low_lane, 0.0, line), axis=1, keepdims=True)
        return jnp.where(low_lane, low, high)

    second = jnp.concatenate([mats[:G], mats[:G]], axis=0)
    cross = jnp.concatenate([mats[G:], mats[G:]], axis=0)
    mean = sheet[0, each:depth, :] / voxels
    target_sum = sheet[1, each:depth, :]
    mean_rows = jnp.broadcast_to(mean, (channels, channels))
    mean_cols = mean_rows.T
    target_cols = jnp.broadcast_to(target_sum, (channels, channels)).T
    second = jnp.where(same, second - voxels * (mean_cols * mean_rows), 0.0)
    cross = jnp.where(same, cross - target_cols * mean_rows, 0.0)
    covariance = second / voxels + jnp.where(diagonal, EPSILON, 0.0)
    trace = group_sums(jnp.where(diagonal, covariance, 0.0))
    scaled = covariance / trace
    root = jnp.sqrt(trace)

    iterate = jnp.where(diagonal, 1.5, 0.0) - 0.5 * scaled
    saved = []
    for sweep in range(1, NEWTON):
        pair = exact(iterate, jnp.concatenate([iterate, scaled], axis=1))
        squared, once = pair[:, :channels], pair[:, channels:]
        triple = exact(squared, jnp.concatenate([once, scaled, iterate], axis=1))
        saved.append(
            (iterate, squared, once, triple[:, channels : 2 * channels], triple[:, 2 * channels :])
        )
        iterate = 1.5 * iterate - 0.5 * triple[:, :channels]
    whitener = iterate / root
    white_grad = exact(whitener, second) - cross
    direction = white_grad / root
    change = -0.5 * direction
    for iterate_k, squared, once, cubic, cube in saved:
        left = exact(jnp.concatenate([iterate_k, squared], axis=0), change)
        both = jnp.concatenate([left[:channels], left[channels:]], axis=1)
        moved = exact(both, jnp.concatenate([once, scaled], axis=0))
        moved = moved + exact(
            jnp.concatenate([change, cube], axis=1), jnp.concatenate([cubic, direction], axis=0)
        )
        change = 1.5 * change - 0.5 * moved
    trace_grad = -0.5 * group_sums(white_grad * whitener) / trace
    trace_grad = trace_grad - group_sums(change * scaled) / trace
    sigma_grad = change / trace + jnp.where(diagonal, trace_grad, 0.0)
    symmetric = (sigma_grad + sigma_grad.T) / voxels
    whitener_t = whitener.T
    backward = (exact(whitener_t, whitener) + symmetric).T

    both = jnp.concatenate([whitener_t, backward], axis=1)
    offset = exact(jnp.broadcast_to(mean, (8, channels)), both)[0:1]
    target_offset = exact(jnp.broadcast_to(target_sum / voxels, (8, channels)), whitener)[0:1]
    mixed = through(hidden[...], both) - offset
    whitened_out[...] = mixed[:, :channels].astype(BF16)
    pulled = through(target[...], whitener) - target_offset
    grad_out[...] = (mixed[:, channels:] - pulled).astype(BF16)


def turn_kernel(below, below_edge, own, own_edge, above, above_edge, turned_out):
    rows, columns, channels = own.shape
    planes = ((below, below_edge), (own, own_edge), (above, above_edge))
    for tap_z in range(3):
        plane, edge = planes[tap_z]
        for source in range(-1, rows + 1):
            if source < 0:
                tile = edge[0]
            elif source == rows:
                tile = edge[1]
            else:
                tile = plane[source]
            tile = tile.T
            for tap_y in range(3):
                here = source + 1 - tap_y
                if 0 <= here < rows:
                    slot = tap_z * 3 + tap_y
                    turned_out[
                        slot * channels : (slot + 1) * channels,
                        here * columns : (here + 1) * columns,
                    ] = tile


def weight_kernel(columns, share, turned, grad, parts_out, wide):
    count, channels = grad.shape
    value = grad[...].astype(F32)
    wide[:, :channels] = moved_columns(value, -1, columns).astype(BF16)
    wide[:, channels : 2 * channels] = grad[...]
    wide[:, 2 * channels :] = moved_columns(value, 1, columns).astype(BF16)
    blocks = channels // share
    taps_each = parts_out.shape[1] // share
    terms = jnp.dot(turned[...], wide[...], preferred_element_type=F32).astype(BF16)
    for tap in range(27):
        slot, tap_x = tap // 3, tap % 3
        group, place = tap // taps_each, tap % taps_each
        for block in range(blocks):
            first = slot * channels + block * share
            parts_out[group * blocks + block, place * share : (place + 1) * share, :] = terms[
                first : first + share, tap_x * channels : (tap_x + 1) * channels
            ]
    spare = parts_out.shape[0] // blocks * taps_each
    for tap in range(27, spare):
        group, place = tap // taps_each, tap % taps_each
        for block in range(blocks):
            parts_out[group * blocks + block, place * share : (place + 1) * share, :] = jnp.zeros(
                (share, channels), BF16
            )


def input_kernel(
    below, below_edge, own, own_edge, above, above_edge, weight, grad_out, wide, kernel_wide
):
    rows, columns, channels = own.shape
    planes = ((below, below_edge), (own, own_edge), (above, above_edge))
    for tap_z in range(3):
        for tap_y in range(3):
            slot = tap_z * 3 + tap_y
            place_rows(wide, slot, planes[2 - tap_z][0], planes[2 - tap_z][1], 2 - tap_y)
            for tap_x in range(3):
                kernel_wide[
                    tap_x * channels : (tap_x + 1) * channels,
                    slot * channels : (slot + 1) * channels,
                ] = weight[slot * 3 + tap_x]
    flat = wide[...].reshape(rows * columns, 9 * channels)
    product = lax.dot_general(
        flat, kernel_wide[...], (((1,), (1,)), ((), ())), preferred_element_type=F32
    )
    total = product[:, channels : 2 * channels]
    total = total + moved_columns(product[:, :channels], -1, columns)
    total = total + moved_columns(product[:, 2 * channels :], 1, columns)
    grad_out[...] = total.astype(BF16)


def exchange(parts, axes):
    return lax.all_to_all(parts, axes, 0, 0, tiled=True)


def copies(part, count):
    return jnp.broadcast_to(part[None], (count,) + part.shape)


def local(volume, conv_weight, target):
    _, rows, columns, channels = volume.shape
    count = rows * columns
    voxels = count * lax.axis_size(GZ) * lax.axis_size(GY)
    spread = lax.axis_size(SPREAD)
    levels = lax.axis_size("z")
    rows_y = lax.axis_size("y")
    share = channels // lax.axis_size(GY)
    taps_each = -(-27 // rows_y)
    flops = 2 * count * 27 * channels * channels
    weight = conv_weight.reshape(27, channels, channels)
    target_flat = target.reshape(count, channels)

    planes = halo(volume.reshape(rows, columns, channels))
    planes = [piece for plane in planes for piece in plane]
    wide = pltpu.VMEM((rows, columns, 9 * channels), BF16)
    hidden, sheet = call(
        conv_kernel,
        [
            jax.ShapeDtypeStruct((count, channels), BF16),
            jax.ShapeDtypeStruct((spread, 2 * G // spread + 1, channels), F32),
        ],
        [wide, pltpu.VMEM((9 * channels, 3 * channels), BF16)],
        flops, 3 * 2**20, *planes, weight, target_flat,
    )
    turned = call(
        turn_kernel,
        jax.ShapeDtypeStruct((9 * channels, count), BF16),
        [], 0, 3 * 2**20, *planes,
    )

    mine = exchange(sheet, SPREAD).sum(0)
    mine = exchange(copies(mine, levels), ("z",)).sum(0)
    sheet = exchange(copies(mine, spread), SPREAD)
    whitened, grad_hidden = call(
        lambda *refs: whiten_kernel(voxels, *refs),
        [jax.ShapeDtypeStruct((count, channels), BF16)] * 2,
        [pltpu.VMEM((2 * G, channels), F32)],
        100 * 2 * channels**3, 2**20, sheet, hidden, target_flat,
    )

    parts = call(
        lambda *refs: weight_kernel(columns, share, *refs),
        jax.ShapeDtypeStruct((spread, taps_each * share, channels), BF16),
        [pltpu.VMEM((count, 3 * channels), BF16)],
        flops, 4 * 2**20, turned, grad_hidden,
    )
    part = exchange(parts, SPREAD).astype(F32).sum(0)
    part = exchange(copies(part.astype(BF16), levels), ("z",))
    part = part.astype(F32).sum(0) * (1.0 / math.sqrt(voxels))
    whole = exchange(copies(part, rows_y), ("y",))
    weight_grad = whole.reshape(rows_y * taps_each, share, channels)[:27]
    weight_grad = weight_grad.reshape(3, 3, 3, share, channels)

    planes = halo(grad_hidden.reshape(rows, columns, channels))
    planes = [piece for plane in planes for piece in plane]
    input_grad = call(
        input_kernel,
        jax.ShapeDtypeStruct((count, channels), BF16),
        [wide, pltpu.VMEM((3 * channels, 9 * channels), BF16)],
        flops, 3 * 2**20, *planes, weight,
    )
    return (whitened.reshape(volume.shape), input_grad.reshape(volume.shape), weight_grad)


def solution(mesh):
    cells = mesh.devices.reshape(4, 8, 4, 2)
    split = Mesh(cells, ("y", "z", "x", "c"))
    in_specs = (P(GZ, GY, None, None), P(), P(GZ, GY, None, None))
    out_specs = (
        P(GZ, GY, None, None),
        P(GZ, GY, None, None),
        P(None, None, None, GY, None),
    )
    return jax.shard_map(local, mesh=split, in_specs=in_specs, out_specs=out_specs, check_vma=False)
```

time: 185 us -> 144 us (0.78)
  the two profiles are of different devices: /device:TPU:4 before, /device:TPU:26 now
where the time goes in v2:
time: 144 us; the launch traced here: 143 us
  starting transfers between devices  59.2 us (41%)
  blocking collectives  45 us (31%)
  waiting for transfers between devices  14.7 us (10%)
  Pallas kernels  13.4 us (9%)
  local copies, waits for them, and re-layouts  9.34 us (6%)
    all_to_all x3, blocking collectives, exchange(): return lax.all_to_all(parts, axes, 0, 0, tiled=True)  45 us
    ppermute x12, starting transfers between devices, shifted_from(): return lax.ppermute(block, axes, pairs)  43.9 us
    all_to_all x3, starting transfers between devices, exchange(): return lax.all_to_all(parts, axes, 0, 0, tiled=True)  15.3 us
    pallas_call x5, Pallas kernels, call(): pl.pallas_call(kernel, out_shape=out_shape, in_specs=[vmem] * len(operand...  13.4 us
    ppermute x12, waiting for transfers between devices, shifted_from(): return lax.ppermute(block, axes, pairs)  10.1 us
    unnamed x18, local copies, waits for them, and re-layouts  5.69 us
    all_to_all x3, waiting for transfers between devices, exchange(): return lax.all_to_all(parts, axes, 0, 0, tiled=True)  4.6 us
  transfers between devices with their start and end apart: 15, of which 5 were waited for; matrix products, arithmetic and copies ran while one was open for 1% of the time, Pallas kernels for 2%

profile of v2, /device:TPU:26, one launch (start us, length us, event | category | flops | bytes accessed | tf_op | source)
XLA Modules:
  0.0 142.7 jit_solution(5840544841770951792)
XLA Ops:
  0.6 0.0 copy-start.1
  0.6 0.8 slice_bitcast_fusion.2
  1.5 1.9 %collective-permute-start.1 = (bf16[1,128,128]{2,1,0:T(8,128)(2,1)S(1)}, bf16[1,128,128]{2,1,0:T(8,128)(2,1)S(1)}, u32[]{:S(2)}, u32[]{:S(2)}) collective-permute-start(bf16[1,128,128]{2,1,0:T(8,128)(2,1)S(1)} %get-tuple-element.14), channel_id=1, source_target_pairs={{0,1},{1,2},{2,3},{3,4},{4,5},{5,6},{6,7},{8,9},{9,10},{10,11},{11... | collective-permute-start | bytes 98312 | tf_op jit(solution)/shard_map/ppermute | solution.py:24
  3.4 3.8 %collective-permute-start = (bf16[8,128,128]{2,1,0:T(8,128)(2,1)}, bf16[8,128,128]{2,1,0:T(8,128)(2,1)S(1)}, u32[]{:S(2)}, u32[]{:S(2)}) collective-permute-start(bf16[8,128,128]{2,1,0:T(8,128)(2,1)} %bitcast.16), channel_id=1, source_target_pairs={{0,8},{8,16},{16,24},{24,32},{32,40},{40,48},{48,56},{56,64},{64,7... | collective-permute-start | bytes 786440 | tf_op jit(solution)/shard_map/ppermute | solution.py:24
  7.2 6.0 %collective-permute-start.4 = (bf16[8,128,128]{2,1,0:T(8,128)(2,1)}, bf16[8,128,128]{2,1,0:T(8,128)(2,1)S(1)}, u32[]{:S(2)}, u32[]{:S(2)}) collective-permute-start(bf16[8,128,128]{2,1,0:T(8,128)(2,1)} %bitcast.17), channel_id=1, source_target_pairs={{8,0},{16,8},{24,16},{32,24},{40,32},{48,40},{56,48},{64,56},{72,6... | collective-permute-start | bytes 786440 | tf_op jit(solution)/shard_map/ppermute | solution.py:24
  13.3 3.4 %collective-permute-start.2 = (bf16[1,128,128]{2,1,0:T(8,128)(2,1)S(1)}, bf16[1,128,128]{2,1,0:T(8,128)(2,1)S(1)}, u32[]{:S(2)}, u32[]{:S(2)}) collective-permute-start(bf16[1,128,128]{2,1,0:T(8,128)(2,1)S(1)} %get-tuple-element.13), channel_id=1, source_target_pairs={{1,0},{2,1},{3,2},{4,3},{5,4},{6,5},{7,6},{9,8},{10,9},{11,10},{12... | collective-permute-start | bytes 98312 | tf_op jit(solution)/shard_map/ppermute | solution.py:24
  16.6 0.0 collective-permute-done.1
  16.7 1.6 %collective-permute-done.2 = bf16[1,128,128]{2,1,0:T(8,128)(2,1)S(1)} collective-permute-done((bf16[1,128,128]{2,1,0:T(8,128)(2,1)S(1)}, bf16[1,128,128]{2,1,0:T(8,128)(2,1)S(1)}, u32[]{:S(2)}, u32[]{:S(2)}) %collective-permute-start.2) | collective-permute-done | bytes 32800 | tf_op jit(solution)/shard_map/ppermute | solution.py:24
  18.2 1.9 %collective-permute-start.3 = (bf16[2,128,128]{2,1,0:T(8,128)(2,1)S(1)}, bf16[2,128,128]{2,1,0:T(8,128)(2,1)S(1)}, u32[]{:S(2)}, u32[]{:S(2)}) collective-permute-start(bf16[2,128,128]{2,1,0:T(8,128)(2,1)S(1)} %constant_dynamic-update-slice_fusion.own_edge), channel_id=1, source_target_pairs={{0,8},{8,16},{16,24},{24,32},{32,40},{40,48},{48,56},{56,64},{64,7... | collective-permute-start | bytes 196616 | tf_op jit(solution)/shard_map/ppermute | solution.py:24
  20.1 6.0 %collective-permute-start.5 = (bf16[2,128,128]{2,1,0:T(8,128)(2,1)S(1)}, bf16[2,128,128]{2,1,0:T(8,128)(2,1)S(1)}, u32[]{:S(2)}, u32[]{:S(2)}) collective-permute-start(bf16[2,128,128]{2,1,0:T(8,128)(2,1)S(1)} %constant_dynamic-update-slice_fusion.own_edge), channel_id=1, source_target_pairs={{8,0},{16,8},{24,16},{32,24},{40,32},{48,40},{56,48},{64,56},{72,6... | collective-permute-start | bytes 196616 | tf_op jit(solution)/shard_map/ppermute | solution.py:24
  26.2 0.4 collective-permute-done.3.below_edge
  26.6 1.8 %collective-permute-done.5.above_edge = bf16[2,128,128]{2,1,0:T(8,128)(2,1)S(1)} collective-permute-done((bf16[2,128,128]{2,1,0:T(8,128)(2,1)S(1)}, bf16[2,128,128]{2,1,0:T(8,128)(2,1)S(1)}, u32[]{:S(2)}, u32[]{:S(2)}) %collective-permute-start.5) | collective-permute-done | bytes 65568 | tf_op jit(solution)/shard_map/ppermute | solution.py:24
  28.4 0.0 collective-permute-done.below
  28.4 0.0 collective-permute-done.4.above
  28.4 0.0 copy-start
  28.4 0.9 copy-done
  29.3 0.0 copy-start.2
  29.3 1.2 copy-done.2
  30.5 0.0 copy-start.4
  30.5 0.9 copy-done.4
  31.5 2.1 %shard_map.58 = (bf16[1024,128]{1,0:T(8,128)(2,1)S(1)}, f32[32,5,128]{2,1,0:T(8,128)S(1)}) custom-call(bf16[8,128,128]{2,1,0:T(8,128)(2,1)S(1)} %collective-permute-done.below, bf16[2,128,128]{2,1,0:T(8,128)(2,1)S(1)} %collective-permute-done.3.below_edge, bf16[8,128,128]{2,1,0:T(8,128)(2,1)S(1)} %bitcast.18, ...), custom_call_target="tpu_custom_call" | custom-call | flops 905969664 | bytes 3145728 | tf_op jit(solution)/shard_map/pallas_call | solution.py:43
  33.5 0.0 copy-start.6
  33.5 0.7 copy-done.6
  34.2 12.2 %all_to_all.30 = f32[32,5,128]{2,1,0:T(8,128)S(1)} all-to-all(f32[32,5,128]{2,1,0:T(8,128)S(1)} %get-tuple-element.7), channel_id=1, replica_groups=mesh['y'=4,'z'=8,'x'=4,'c'=2] {'y','x','c'}, dimensions={0} | all-to-all | bytes 163840 | tf_op jit(solution)/shard_map/all_to_all | solution.py:280
  46.5 13.7 %all_to_all.31 = f32[8,5,128]{2,1,0:T(8,128)S(1)} all-to-all(f32[8,5,128]{2,1,0:T(8,128)S(1)} %broadcast_in_dim.8), channel_id=1, replica_groups=mesh['y'=4,'z'=8,'x'=4,'c'=2] {'z'}, dimensions={0} | all-to-all | bytes 40960 | tf_op jit(solution)/shard_map/all_to_all | solution.py:280
  60.2 0.7 broadcast_in_dim.9
  60.8 6.6 %all-to-all-start.2 = ((f32[32,5,128]{2,1,0:T(8,128)}), f32[32,5,128]{2,1,0:T(8,128)S(1)}, u32[]{:S(2)}, u32[]{:S(2)}) async-start(f32[32,5,128]{2,1,0:T(8,128)} %broadcast_in_dim.9), calls=%async_computation.2 | async-start | bytes 262144 | tf_op jit(solution)/shard_map/all_to_all | solution.py:280
  67.5 0.0 copy-done.1
  67.5 0.4 shard_map.61.refs_0_
  67.9 4.6 %all-to-all-done.2.refs_0_ = f32[32,5,128]{2,1,0:T(8,128)S(1)} async-done(((f32[32,5,128]{2,1,0:T(8,128)}), f32[32,5,128]{2,1,0:T(8,128)S(1)}, u32[]{:S(2)}, u32[]{:S(2)}) %all-to-all-start.2) | async-done | bytes 81952 | tf_op jit(solution)/shard_map/all_to_all | solution.py:280
  72.5 0.0 copy-start.5
  72.5 0.9 copy-done.5
  73.4 0.0 copy-start.7
  73.4 0.9 copy-done.7
  74.4 7.1 %shard_map.59 = (bf16[1024,128]{1,0:T(8,128)(2,1)}, bf16[1024,128]{1,0:T(8,128)(2,1)S(1)}) custom-call(f32[32,5,128]{2,1,0:T(8,128)S(1)} %all-to-all-done.2.refs_0_, bf16[1024,128]{1,0:T(8,128)(2,1)S(1)} %copy-done.7, bf16[1024,128]{1,0:T(8,128)(2,1)S(1)} %bitcast.26), custom_call_target="tpu_custom_call" | custom-call | flops 419430400 | bytes 1048576 | tf_op jit(solution)/shard_map/pallas_call | solution.py:43
  81.5 1.5 %shard_map.62 = bf16[32,112,128]{2,1,0:T(8,128)(2,1)S(1)} custom-call(bf16[1152,1024]{1,0:T(8,128)(2,1)S(1)} %shard_map.61.refs_0_, bf16[1024,128]{1,0:T(8,128)(2,1)S(1)} %get-tuple-element.10.refs_1_), custom_call_target="tpu_custom_call" | custom-call | flops 905969664 | bytes 4194304 | tf_op jit(solution)/shard_map/pallas_call | solution.py:43
  83.0 0.0 copy-start.3
  83.0 19.2 %all_to_all.32 = bf16[32,112,128]{2,1,0:T(8,128)(2,1)S(1)} all-to-all(bf16[32,112,128]{2,1,0:T(8,128)(2,1)S(1)} %shard_map.62), channel_id=1, replica_groups=mesh['y'=4,'z'=8,'x'=4,'c'=2] {'y','x','c'}, dimensions={0} | all-to-all | bytes 1835008 | tf_op jit(solution)/shard_map/all_to_all | solution.py:280
  102.2 0.1 reduce_sum.41
  102.4 0.7 broadcast_in_dim.10
  103.1 3.4 %all-to-all-start.4 = ((bf16[8,112,128]{2,1,0:T(8,128)(2,1)}), bf16[8,112,128]{2,1,0:T(8,128)(2,1)S(1)}, u32[]{:S(2)}, u32[]{:S(2)}) async-start(bf16[8,112,128]{2,1,0:T(8,128)(2,1)} %broadcast_in_dim.10), calls=%async_computation.4 | async-start | bytes 458752 | tf_op jit(solution)/shard_map/all_to_all | solution.py:280
  106.5 2.5 %collective-permute-start.7 = (bf16[1,128,128]{2,1,0:T(8,128)(2,1)S(1)}, bf16[1,128,128]{2,1,0:T(8,128)(2,1)S(1)}, u32[]{:S(2)}, u32[]{:S(2)}) collective-permute-start(bf16[1,128,128]{2,1,0:T(8,128)(2,1)S(1)} %get-tuple-element.12), channel_id=1, source_target_pairs={{0,1},{1,2},{2,3},{3,4},{4,5},{5,6},{6,7},{8,9},{9,10},{10,11},{11... | collective-permute-start | bytes 98312 | tf_op jit(solution)/shard_map/ppermute | solution.py:24
  109.0 5.2 %collective-permute-start.10 = (bf16[8,128,128]{2,1,0:T(8,128)(2,1)S(1)}, bf16[8,128,128]{2,1,0:T(8,128)(2,1)S(1)}, u32[]{:S(2)}, u32[]{:S(2)}) collective-permute-start(bf16[8,128,128]{2,1,0:T(8,128)(2,1)S(1)} %bitcast.20), channel_id=1, source_target_pairs={{8,0},{16,8},{24,16},{32,24},{40,32},{48,40},{56,48},{64,56},{72,6... | collective-permute-start | bytes 786440 | tf_op jit(solution)/shard_map/ppermute | solution.py:24
  114.2 1.9 %collective-permute-start.6 = (bf16[8,128,128]{2,1,0:T(8,128)(2,1)S(1)}, bf16[8,128,128]{2,1,0:T(8,128)(2,1)S(1)}, u32[]{:S(2)}, u32[]{:S(2)}) collective-permute-start(bf16[8,128,128]{2,1,0:T(8,128)(2,1)S(1)} %bitcast.21), channel_id=1, source_target_pairs={{0,8},{8,16},{16,24},{24,32},{32,40},{40,48},{48,56},{56,64},{64,7... | collective-permute-start | bytes 786440 | tf_op jit(solution)/shard_map/ppermute | solution.py:24
  116.1 2.7 %collective-permute-start.8 = (bf16[1,128,128]{2,1,0:T(8,128)(2,1)S(1)}, bf16[1,128,128]{2,1,0:T(8,128)(2,1)S(1)}, u32[]{:S(2)}, u32[]{:S(2)}) collective-permute-start(bf16[1,128,128]{2,1,0:T(8,128)(2,1)S(1)} %get-tuple-element.11), channel_id=1, source_target_pairs={{1,0},{2,1},{3,2},{4,3},{5,4},{6,5},{7,6},{9,8},{10,9},{11,10},{12... | collective-permute-start | bytes 98312 | tf_op jit(solution)/shard_map/ppermute | solution.py:24
  118.8 0.0 collective-permute-done.7
  118.8 0.0 all-to-all-done.4
  118.9 0.7 broadcast_in_dim.11
  119.6 5.2 %all-to-all-start.5 = ((f32[4,112,128]{2,1,0:T(8,128)}), f32[4,112,128]{2,1,0:T(8,128)S(1)}, u32[]{:S(2)}, u32[]{:S(2)}) async-start(f32[4,112,128]{2,1,0:T(8,128)} %broadcast_in_dim.11), calls=%async_computation.5 | async-start | bytes 458752 | tf_op jit(solution)/shard_map/all_to_all | solution.py:280
  124.8 0.0 collective-permute-done.8
  124.8 6.6 %collective-permute-start.11 = (bf16[2,128,128]{2,1,0:T(8,128)(2,1)S(1)}, bf16[2,128,128]{2,1,0:T(8,128)(2,1)S(1)}, u32[]{:S(2)}, u32[]{:S(2)}) collective-permute-start(bf16[2,128,128]{2,1,0:T(8,128)(2,1)S(1)} %constant_dynamic-update-slice_fusion.2.own_edge), channel_id=1, source_target_pairs={{8,0},{16,8},{24,16},{32,24},{40,32},{48,40},{56,48},{64,56},{72,6... | collective-permute-start | bytes 196616 | tf_op jit(solution)/shard_map/ppermute | solution.py:24
  131.5 1.9 %collective-permute-start.9 = (bf16[2,128,128]{2,1,0:T(8,128)(2,1)S(1)}, bf16[2,128,128]{2,1,0:T(8,128)(2,1)S(1)}, u32[]{:S(2)}, u32[]{:S(2)}) collective-permute-start(bf16[2,128,128]{2,1,0:T(8,128)(2,1)S(1)} %constant_dynamic-update-slice_fusion.2.own_edge), channel_id=1, source_target_pairs={{0,8},{8,16},{16,24},{24,32},{32,40},{40,48},{48,56},{56,64},{64,7... | collective-permute-start | bytes 196616 | tf_op jit(solution)/shard_map/ppermute | solution.py:24
  133.4 0.0 collective-permute-done.11.above_edge
  133.4 6.3 %collective-permute-done.9.below_edge = bf16[2,128,128]{2,1,0:T(8,128)(2,1)S(1)} collective-permute-done((bf16[2,128,128]{2,1,0:T(8,128)(2,1)S(1)}, bf16[2,128,128]{2,1,0:T(8,128)(2,1)S(1)}, u32[]{:S(2)}, u32[]{:S(2)}) %collective-permute-start.9) | collective-permute-done | bytes 65568 | tf_op jit(solution)/shard_map/ppermute | solution.py:24
  139.7 0.0 collective-permute-done.10.above
  139.7 0.0 collective-permute-done.6.below
  139.7 0.0 copy-done.3
  139.7 2.3 %shard_map.60 = bf16[1024,128]{1,0:T(8,128)(2,1)} custom-call(bf16[8,128,128]{2,1,0:T(8,128)(2,1)S(1)} %collective-permute-done.6.below, bf16[2,128,128]{2,1,0:T(8,128)(2,1)S(1)} %collective-permute-done.9.below_edge, bf16[8,128,128]{2,1,0:T(8,128)(2,1)S(1)} %bitcast.22, bf16[2,128,128]{2,1,0:T(8,128)(2,1)S(1)} %constant_dynamic-update-slice_fusion.2.own_edge, ...), custom_call_target="tpu_custom_call" | custom-call | flops 905969664 | bytes 3145728 | tf_op jit(solution)/shard_map/pallas_call | solution.py:43
  142.0 0.0 all-to-all-done.5
  142.0 0.7 slice.36
  (10 shorter events, 0.1 us)
Async XLA Ops:
  0.6 66.8 %copy-start.1 = (bf16[1,8,128,128]{3,2,1,0:T(8,128)(2,1)S(1)}, bf16[1,8,128,128]{3,2,1,0:T(8,128)(2,1)}, u32[]{:S(2)}) copy-start(bf16[1,8,128,128]{3,2,1,0:T(8,128)(2,1)} %param.3) | copy-start | bytes 786436
  1.5 15.2 %collective-permute-start.1 = (bf16[1,128,128]{2,1,0:T(8,128)(2,1)S(1)}, bf16[1,128,128]{2,1,0:T(8,128)(2,1)S(1)}, u32[]{:S(2)}, u32[]{:S(2)}) collective-permute-start(bf16[1,128,128]{2,1,0:T(8,128)(2,1)S(1)} %get-tuple-element.14), channel_id=1, source_target_pairs={{0,1},{1,2},{2,3},{3,4},{4,5},{5,6},{6,7},{8,9},{9,10},{10,11},{11... | collective-permute-start | bytes 98312 | tf_op jit(solution)/shard_map/ppermute | solution.py:24
  3.4 25.0 %collective-permute-start = (bf16[8,128,128]{2,1,0:T(8,128)(2,1)}, bf16[8,128,128]{2,1,0:T(8,128)(2,1)S(1)}, u32[]{:S(2)}, u32[]{:S(2)}) collective-permute-start(bf16[8,128,128]{2,1,0:T(8,128)(2,1)} %bitcast.16), channel_id=1, source_target_pairs={{0,8},{8,16},{16,24},{24,32},{32,40},{40,48},{48,56},{56,64},{64,7... | collective-permute-start | bytes 786440 | tf_op jit(solution)/shard_map/ppermute | solution.py:24
  7.2 21.2 %collective-permute-start.4 = (bf16[8,128,128]{2,1,0:T(8,128)(2,1)}, bf16[8,128,128]{2,1,0:T(8,128)(2,1)S(1)}, u32[]{:S(2)}, u32[]{:S(2)}) collective-permute-start(bf16[8,128,128]{2,1,0:T(8,128)(2,1)} %bitcast.17), channel_id=1, source_target_pairs={{8,0},{16,8},{24,16},{32,24},{40,32},{48,40},{56,48},{64,56},{72,6... | collective-permute-start | bytes 786440 | tf_op jit(solution)/shard_map/ppermute | solution.py:24
  13.3 4.9 %collective-permute-start.2 = (bf16[1,128,128]{2,1,0:T(8,128)(2,1)S(1)}, bf16[1,128,128]{2,1,0:T(8,128)(2,1)S(1)}, u32[]{:S(2)}, u32[]{:S(2)}) collective-permute-start(bf16[1,128,128]{2,1,0:T(8,128)(2,1)S(1)} %get-tuple-element.13), channel_id=1, source_target_pairs={{1,0},{2,1},{3,2},{4,3},{5,4},{6,5},{7,6},{9,8},{10,9},{11,10},{12... | collective-permute-start | bytes 98312 | tf_op jit(solution)/shard_map/ppermute | solution.py:24
  18.2 8.4 %collective-permute-start.3 = (bf16[2,128,128]{2,1,0:T(8,128)(2,1)S(1)}, bf16[2,128,128]{2,1,0:T(8,128)(2,1)S(1)}, u32[]{:S(2)}, u32[]{:S(2)}) collective-permute-start(bf16[2,128,128]{2,1,0:T(8,128)(2,1)S(1)} %constant_dynamic-update-slice_fusion.own_edge), channel_id=1, source_target_pairs={{0,8},{8,16},{16,24},{24,32},{32,40},{40,48},{48,56},{56,64},{64,7... | collective-permute-start | bytes 196616 | tf_op jit(solution)/shard_map/ppermute | solution.py:24
  20.1 8.2 %collective-permute-start.5 = (bf16[2,128,128]{2,1,0:T(8,128)(2,1)S(1)}, bf16[2,128,128]{2,1,0:T(8,128)(2,1)S(1)}, u32[]{:S(2)}, u32[]{:S(2)}) collective-permute-start(bf16[2,128,128]{2,1,0:T(8,128)(2,1)S(1)} %constant_dynamic-update-slice_fusion.own_edge), channel_id=1, source_target_pairs={{8,0},{16,8},{24,16},{32,24},{40,32},{48,40},{56,48},{64,56},{72,6... | collective-permute-start | bytes 196616 | tf_op jit(solution)/shard_map/ppermute | solution.py:24
  28.4 1.0 copy-start
  29.3 1.2 copy-start.2
  30.5 0.9 copy-start.4
  33.5 0.7 copy-start.6
  60.8 11.6 %all-to-all-start.2 = ((f32[32,5,128]{2,1,0:T(8,128)}), f32[32,5,128]{2,1,0:T(8,128)S(1)}, u32[]{:S(2)}, u32[]{:S(2)}) async-start(f32[32,5,128]{2,1,0:T(8,128)} %broadcast_in_dim.9), calls=%async_computation.2 | async-start | bytes 262144 | tf_op jit(solution)/shard_map/all_to_all | solution.py:280
  72.5 1.0 copy-start.5
  73.4 0.9 copy-start.7
  83.0 56.7 %copy-start.3 = (bf16[3,3,3,128,128]{4,3,2,1,0:T(8,128)(2,1)S(1)}, bf16[3,3,3,128,128]{4,3,2,1,0:T(8,128)(2,1)}, u32[]{:S(2)}) copy-start(bf16[3,3,3,128,128]{4,3,2,1,0:T(8,128)(2,1)} %param.4) | copy-start | bytes 2654212
  103.1 15.7 %all-to-all-start.4 = ((bf16[8,112,128]{2,1,0:T(8,128)(2,1)}), bf16[8,112,128]{2,1,0:T(8,128)(2,1)S(1)}, u32[]{:S(2)}, u32[]{:S(2)}) async-start(bf16[8,112,128]{2,1,0:T(8,128)(2,1)} %broadcast_in_dim.10), calls=%async_computation.4 | async-start | bytes 458752 | tf_op jit(solution)/shard_map/all_to_all | solution.py:280
  106.5 12.3 %collective-permute-start.7 = (bf16[1,128,128]{2,1,0:T(8,128)(2,1)S(1)}, bf16[1,128,128]{2,1,0:T(8,128)(2,1)S(1)}, u32[]{:S(2)}, u32[]{:S(2)}) collective-permute-start(bf16[1,128,128]{2,1,0:T(8,128)(2,1)S(1)} %get-tuple-element.12), channel_id=1, source_target_pairs={{0,1},{1,2},{2,3},{3,4},{4,5},{5,6},{6,7},{8,9},{9,10},{10,11},{11... | collective-permute-start | bytes 98312 | tf_op jit(solution)/shard_map/ppermute | solution.py:24
  109.0 30.7 %collective-permute-start.10 = (bf16[8,128,128]{2,1,0:T(8,128)(2,1)S(1)}, bf16[8,128,128]{2,1,0:T(8,128)(2,1)S(1)}, u32[]{:S(2)}, u32[]{:S(2)}) collective-permute-start(bf16[8,128,128]{2,1,0:T(8,128)(2,1)S(1)} %bitcast.20), channel_id=1, source_target_pairs={{8,0},{16,8},{24,16},{32,24},{40,32},{48,40},{56,48},{64,56},{72,6... | collective-permute-start | bytes 786440 | tf_op jit(solution)/shard_map/ppermute | solution.py:24
  114.2 25.6 %collective-permute-start.6 = (bf16[8,128,128]{2,1,0:T(8,128)(2,1)S(1)}, bf16[8,128,128]{2,1,0:T(8,128)(2,1)S(1)}, u32[]{:S(2)}, u32[]{:S(2)}) collective-permute-start(bf16[8,128,128]{2,1,0:T(8,128)(2,1)S(1)} %bitcast.21), channel_id=1, source_target_pairs={{0,8},{8,16},{16,24},{24,32},{32,40},{40,48},{48,56},{56,64},{64,7... | collective-permute-start | bytes 786440 | tf_op jit(solution)/shard_map/ppermute | solution.py:24
  116.1 8.7 %collective-permute-start.8 = (bf16[1,128,128]{2,1,0:T(8,128)(2,1)S(1)}, bf16[1,128,128]{2,1,0:T(8,128)(2,1)S(1)}, u32[]{:S(2)}, u32[]{:S(2)}) collective-permute-start(bf16[1,128,128]{2,1,0:T(8,128)(2,1)S(1)} %get-tuple-element.11), channel_id=1, source_target_pairs={{1,0},{2,1},{3,2},{4,3},{5,4},{6,5},{7,6},{9,8},{10,9},{11,10},{12... | collective-permute-start | bytes 98312 | tf_op jit(solution)/shard_map/ppermute | solution.py:24
  119.6 22.5 %all-to-all-start.5 = ((f32[4,112,128]{2,1,0:T(8,128)}), f32[4,112,128]{2,1,0:T(8,128)S(1)}, u32[]{:S(2)}, u32[]{:S(2)}) async-start(f32[4,112,128]{2,1,0:T(8,128)} %broadcast_in_dim.11), calls=%async_computation.5 | async-start | bytes 458752 | tf_op jit(solution)/shard_map/all_to_all | solution.py:280
  124.8 8.6 %collective-permute-start.11 = (bf16[2,128,128]{2,1,0:T(8,128)(2,1)S(1)}, bf16[2,128,128]{2,1,0:T(8,128)(2,1)S(1)}, u32[]{:S(2)}, u32[]{:S(2)}) collective-permute-start(bf16[2,128,128]{2,1,0:T(8,128)(2,1)S(1)} %constant_dynamic-update-slice_fusion.2.own_edge), channel_id=1, source_target_pairs={{8,0},{16,8},{24,16},{32,24},{40,32},{48,40},{56,48},{64,56},{72,6... | collective-permute-start | bytes 196616 | tf_op jit(solution)/shard_map/ppermute | solution.py:24
  131.5 8.3 %collective-permute-start.9 = (bf16[2,128,128]{2,1,0:T(8,128)(2,1)S(1)}, bf16[2,128,128]{2,1,0:T(8,128)(2,1)S(1)}, u32[]{:S(2)}, u32[]{:S(2)}) collective-permute-start(bf16[2,128,128]{2,1,0:T(8,128)(2,1)S(1)} %constant_dynamic-update-slice_fusion.2.own_edge), channel_id=1, source_target_pairs={{0,8},{8,16},{16,24},{24,32},{32,40},{40,48},{48,56},{56,64},{64,7... | collective-permute-start | bytes 196616 | tf_op jit(solution)/shard_map/ppermute | solution.py:24

commit v3 on v2

--- a/solution.py
+++ b/solution.py
@@ -16,25 +16,26 @@
 GZ = ("y", "z")
 GY = ("x", "c")
 SPREAD = ("y", "x", "c")
-VMEM_BYTES = 48 * 1024 * 1024
-
-
-def shifted_from(block, axes, count, step):
-    pairs = [(i, i + step) for i in range(count) if 0 <= i + step < count]
+VMEM_BYTES = 20 * 1024 * 1024
+
+
+def swapped(block, axes, count, first):
+    pairs = []
+    for i in range(first, count - 1, 2):
+        pairs += [(i, i + 1), (i + 1, i)]
     return lax.ppermute(block, axes, pairs)
 
 
-def halo(block):
+def row_swaps(first_send, second_send):
+    ny = lax.axis_size(GY)
+    return jnp.concatenate(
+        [swapped(first_send, GY, ny, 0), swapped(second_send, GY, ny, 1)], axis=0
+    )
+
+
+def plane_swaps(block):
     nz = lax.axis_size(GZ)
-    ny = lax.axis_size(GY)
-    low = shifted_from(block[-1:], GY, ny, 1)
-    high = shifted_from(block[:1], GY, ny, -1)
-    below = shifted_from(block, GZ, nz, 1)
-    above = shifted_from(block, GZ, nz, -1)
-    edges = jnp.concatenate([low, high], axis=0)
-    edges_below = shifted_from(edges, GZ, nz, 1)
-    edges_above = shifted_from(edges, GZ, nz, -1)
-    return (below, edges_below), (block, edges), (above, edges_above)
+    return swapped(block, GZ, nz, 0), swapped(block, GZ, nz, 1)
 
 
 def call(kernel, out_shape, scratch, flops, moved, *operands):
@@ -54,14 +55,39 @@
 def place_rows(wide, slot, plane, edge, tap_y):
     rows, _, channels = plane.shape
     cols = slice(slot * channels, (slot + 1) * channels)
+    odd_row = lax.axis_index("c")
     if tap_y == 0:
-        wide[0:1, :, cols] = edge[0:1]
+        wide[0:1, :, cols] = edge[pl.ds(1 - odd_row, 1)]
         wide[1:rows, :, cols] = plane[0 : rows - 1]
     elif tap_y == 1:
         wide[:, :, cols] = plane[...]
     else:
         wide[0 : rows - 1, :, cols] = plane[1:rows]
-        wide[rows - 1 : rows, :, cols] = edge[1:2]
+        wide[rows - 1 : rows, :, cols] = edge[pl.ds(odd_row, 1)]
+
+
+def place_all(wide, own, even, odd, flip):
+    odd_plane = lax.rem(lax.axis_index("z"), 2)
+
+    order = range(3)
+    for tap_z in order:
+        for tap_y in order:
+            slot = tap_z * 3 + tap_y
+            step_z, step_y = (2 - tap_z, 2 - tap_y) if flip else (tap_z, tap_y)
+            if step_z == 1:
+                place_rows(wide, slot, own[0], own[1], step_y)
+    for parity in range(2):
+
+        @pl.when(odd_plane == parity)
+        def _():
+            below, above = (odd, even) if parity == 0 else (even, odd)
+            for tap_z in order:
+                for tap_y in order:
+                    slot = tap_z * 3 + tap_y
+                    step_z, step_y = (2 - tap_z, 2 - tap_y) if flip else (tap_z, tap_y)
+                    if step_z != 1:
+                        piece = below if step_z == 0 else above
+                        place_rows(wide, slot, piece[0], piece[1], step_y)
 
 
 def moved_columns(flat, step, columns):
@@ -77,20 +103,17 @@
 
 
 def conv_kernel(
-    below, below_edge, own, own_edge, above, above_edge, weight, target,
+    own, own_edge, even, even_edge, odd, odd_edge, weight, target,
     hidden_out, sheet_out, wide, kernel_wide,
 ):
     rows, columns, channels = own.shape
-    planes = ((below, below_edge), (own, own_edge), (above, above_edge))
-    for tap_z in range(3):
-        for tap_y in range(3):
-            slot = tap_z * 3 + tap_y
-            place_rows(wide, slot, planes[tap_z][0], planes[tap_z][1], tap_y)
-            for tap_x in range(3):
-                kernel_wide[
-                    slot * channels : (slot + 1) * channels,
-                    tap_x * channels : (tap_x + 1) * channels,
-                ] = weight[slot * 3 + tap_x]
+    place_all(wide, (own, own_edge), (even, even_edge), (odd, odd_edge), False)
+    for slot in range(9):
+        for tap_x in range(3):
+            kernel_wide[
+                slot * channels : (slot + 1) * channels,
+                tap_x * channels : (tap_x + 1) * channels,
+            ] = weight[slot * 3 + tap_x]
     flat = wide[...].reshape(rows * columns, 9 * channels)
     product = jnp.dot(flat, kernel_wide[...], preferred_element_type=F32)
     total = product[:, channels : 2 * channels]
@@ -134,7 +157,9 @@
     return total + jnp.dot(values, high, preferred_element_type=F32)
 
 
-def whiten_kernel(voxels, sheet, hidden, target, whitened_out, grad_out, mats):
+def whiten_kernel(
+    voxels, columns, sheet, hidden, target, whitened_out, grad_out, first_out, second_out, mats
+):
     spread, depth, channels = sheet.shape
     each = depth - 1
     for j in range(spread):
@@ -200,19 +225,32 @@
     mixed = through(hidden[...], both) - offset
     whitened_out[...] = mixed[:, :channels].astype(BF16)
     pulled = through(target[...], whitener) - target_offset
-    grad_out[...] = (mixed[:, channels:] - pulled).astype(BF16)
-
-
-def turn_kernel(below, below_edge, own, own_edge, above, above_edge, turned_out):
+    grad = (mixed[:, channels:] - pulled).astype(BF16)
+    grad_out[...] = grad
+    odd_row = lax.axis_index("c")
+
+    @pl.when(odd_row == 0)
+    def _():
+        first_out[0] = grad[-columns:]
+        second_out[0] = grad[:columns]
+
+    @pl.when(odd_row == 1)
+    def _():
+        first_out[0] = grad[:columns]
+        second_out[0] = grad[-columns:]
+
+
+def turn_kernel(own, own_edge, even, even_edge, odd, odd_edge, turned_out):
     rows, columns, channels = own.shape
-    planes = ((below, below_edge), (own, own_edge), (above, above_edge))
-    for tap_z in range(3):
-        plane, edge = planes[tap_z]
+    odd_row = lax.axis_index("c")
+    odd_plane = lax.rem(lax.axis_index("z"), 2)
+
+    def turn(tap_z, plane, edge):
         for source in range(-1, rows + 1):
             if source < 0:
-                tile = edge[0]
+                tile = edge[1 - odd_row]
             elif source == rows:
-                tile = edge[1]
+                tile = edge[odd_row]
             else:
                 tile = plane[source]
             tile = tile.T
@@ -224,6 +262,15 @@
                         slot * channels : (slot + 1) * channels,
                         here * columns : (here + 1) * columns,
                     ] = tile
+
+    turn(1, own, own_edge)
+    for parity in range(2):
+
+        @pl.when(odd_plane == parity)
+        def _():
+            below, above = ((odd, odd_edge), (even, even_edge))[:: 1 - 2 * parity]
+            turn(0, *below)
+            turn(2, *above)
 
 
 def weight_kernel(columns, share, turned, grad, parts_out, wide):
@@ -253,19 +300,16 @@
 
 
 def input_kernel(
-    below, below_edge, own, own_edge, above, above_edge, weight, grad_out, wide, kernel_wide
+    own, own_edge, even, even_edge, odd, odd_edge, weight, grad_out, wide, kernel_wide
 ):
     rows, columns, channels = own.shape
-    planes = ((below, below_edge), (own, own_edge), (above, above_edge))
-    for tap_z in range(3):
-        for tap_y in range(3):
-            slot = tap_z * 3 + tap_y
-            place_rows(wide, slot, planes[2 - tap_z][0], planes[2 - tap_z][1], 2 - tap_y)
-            for tap_x in range(3):
-                kernel_wide[
-                    tap_x * channels : (tap_x + 1) * channels,
-                    slot * channels : (slot + 1) * channels,
-                ] = weight[slot * 3 + tap_x]
+    place_all(wide, (own, own_edge), (even, even_edge), (odd, odd_edge), True)
+    for slot in range(9):
+        for tap_x in range(3):
+            kernel_wide[
+                tap_x * channels : (tap_x + 1) * channels,
+                slot * channels : (slot + 1) * channels,
+            ] = weight[slot * 3 + tap_x]
     flat = wide[...].reshape(rows * columns, 9 * channels)
     product = lax.dot_general(
         flat, kernel_wide[...], (((1,), (1,)), ((), ())), preferred_element_type=F32
@@ -276,12 +320,24 @@
     grad_out[...] = total.astype(BF16)
 
 
+def total_kernel(scale, parts, copies_out):
+    total = parts[0].astype(F32)
+    for i in range(1, parts.shape[0]):
+        total = total + parts[i].astype(F32)
+    total = (total * scale if scale != 1.0 else total).astype(copies_out.dtype)
+    for i in range(copies_out.shape[0]):
+        copies_out[i] = total
+
+
 def exchange(parts, axes):
     return lax.all_to_all(parts, axes, 0, 0, tiled=True)
 
 
-def copies(part, count):
-    return jnp.broadcast_to(part[None], (count,) + part.shape)
+def total_copies(parts, count, dtype, scale=1.0):
+    shape = jax.ShapeDtypeStruct((count,) + parts.shape[1:], dtype)
+    return call(
+        lambda *refs: total_kernel(scale, *refs), shape, [], parts.size, 2 * parts.size, parts
+    )
 
 
 def local(volume, conv_weight, target):
@@ -297,8 +353,14 @@
     weight = conv_weight.reshape(27, channels, channels)
     target_flat = target.reshape(count, channels)
 
-    planes = halo(volume.reshape(rows, columns, channels))
-    planes = [piece for plane in planes for piece in plane]
+    block = volume.reshape(rows, columns, channels)
+    odd_row = lax.axis_index("c")
+    first_send = lax.dynamic_slice_in_dim(block, (1 - odd_row) * (rows - 1), 1, 0)
+    second_send = lax.dynamic_slice_in_dim(block, odd_row * (rows - 1), 1, 0)
+    edges = row_swaps(first_send, second_send)
+    even, odd = plane_swaps(block)
+    even_edges, odd_edges = plane_swaps(edges)
+    planes = [block, edges, even, even_edges, odd, odd_edges]
     wide = pltpu.VMEM((rows, columns, 9 * channels), BF16)
     hidden, sheet = call(
         conv_kernel,
@@ -315,12 +377,13 @@
         [], 0, 3 * 2**20, *planes,
     )
 
-    mine = exchange(sheet, SPREAD).sum(0)
-    mine = exchange(copies(mine, levels), ("z",)).sum(0)
-    sheet = exchange(copies(mine, spread), SPREAD)
-    whitened, grad_hidden = call(
-        lambda *refs: whiten_kernel(voxels, *refs),
-        [jax.ShapeDtypeStruct((count, channels), BF16)] * 2,
+    mine = total_copies(exchange(sheet, SPREAD), levels, F32)
+    mine = total_copies(exchange(mine, ("z",)), spread, F32)
+    sheet = exchange(mine, SPREAD)
+    line = jax.ShapeDtypeStruct((1, columns, channels), BF16)
+    whitened, grad_hidden, first_send, second_send = call(
+        lambda *refs: whiten_kernel(voxels, columns, *refs),
+        [jax.ShapeDtypeStruct((count, channels), BF16)] * 2 + [line] * 2,
         [pltpu.VMEM((2 * G, channels), F32)],
         100 * 2 * channels**3, 2**20, sheet, hidden, target_flat,
     )
@@ -331,15 +394,21 @@
         [pltpu.VMEM((count, 3 * channels), BF16)],
         flops, 4 * 2**20, turned, grad_hidden,
     )
-    part = exchange(parts, SPREAD).astype(F32).sum(0)
-    part = exchange(copies(part.astype(BF16), levels), ("z",))
-    part = part.astype(F32).sum(0) * (1.0 / math.sqrt(voxels))
-    whole = exchange(copies(part, rows_y), ("y",))
+    block, first_send, second_send, parts = lax.optimization_barrier(
+        (grad_hidden.reshape(rows, columns, channels), first_send, second_send, parts)
+    )
+    edges = row_swaps(first_send, second_send)
+    even, odd = plane_swaps(block)
+    part = total_copies(exchange(parts, SPREAD), levels, BF16)
+    part, edges, even, odd = lax.optimization_barrier((part, edges, even, odd))
+    even_edges, odd_edges = plane_swaps(edges)
+    part = total_copies(exchange(part, ("z",)), rows_y, F32, 1.0 / math.sqrt(voxels))
+    part, even_edges, odd_edges = lax.optimization_barrier((part, even_edges, odd_edges))
+    whole = exchange(part, ("y",))
     weight_grad = whole.reshape(rows_y * taps_each, share, channels)[:27]
     weight_grad = weight_grad.reshape(3, 3, 3, share, channels)
 
-    planes = halo(grad_hidden.reshape(rows, columns, channels))
-    planes = [piece for plane in planes for piece in plane]
+    planes = [block, edges, even, even_edges, odd, odd_edges]
     input_grad = call(
         input_kernel,
         jax.ShapeDtypeStruct((count, channels), BF16),

time: 144 us -> 131 us (0.910)
  the two profiles are of different devices: /device:TPU:26 before, /device:TPU:4 now
where the time goes in v3:
time: 131 us; the launch traced here: 130 us
  starting transfers between devices  44.9 us (34%)
  waiting for transfers between devices  35 us (27%)
  blocking collectives  25.7 us (20%)
  Pallas kernels  17.2 us (13%)
  local copies, waits for them, and re-layouts  6.52 us (5%)
    ppermute x12, starting transfers between devices, swapped(): return lax.ppermute(block, axes, pairs)  25.8 us
    all_to_all x2, blocking collectives, exchange(): return lax.all_to_all(parts, axes, 0, 0, tiled=True)  25.7 us
    all_to_all x4, waiting for transfers between devices, exchange(): return lax.all_to_all(parts, axes, 0, 0, tiled=True)  23.5 us
    all_to_all x4, starting transfers between devices, exchange(): return lax.all_to_all(parts, axes, 0, 0, tiled=True)  19.2 us
    pallas_call x9, Pallas kernels, call(): pl.pallas_call(kernel, out_shape=out_shape, in_specs=[vmem] * len(operand...  17.2 us
    ppermute x12, waiting for transfers between devices, swapped(): return lax.ppermute(block, axes, pairs)  11.5 us
    unnamed x17, local copies, waits for them, and re-layouts  4.99 us
  transfers between devices with their start and end apart: 16, of which 7 were waited for; matrix products, arithmetic and copies ran while one was open for 0% of the time, Pallas kernels for 4%

profile of v3, /device:TPU:4, one launch (start us, length us, event | category | flops | bytes accessed | tf_op | source)
XLA Modules:
  0.0 130.1 jit_solution(10438990980178864593)
XLA Ops:
  0.6 0.0 copy-start.1
  0.6 0.8 dynamic-slice_bitcast_fusion
  1.5 0.0 collective-permute-start
  1.5 0.7 collective-permute-start.4
  2.2 5.2 %collective-permute-start.2 = (bf16[8,128,128]{2,1,0:T(8,128)(2,1)}, bf16[8,128,128]{2,1,0:T(8,128)(2,1)S(1)}, u32[]{:S(2)}, u32[]{:S(2)}) collective-permute-start(bf16[8,128,128]{2,1,0:T(8,128)(2,1)} %bitcast.13), channel_id=1, source_target_pairs={{0,8},{8,0},{16,24},{24,16},{32,40},{40,32},{48,56},{56,48},{64,72... | collective-permute-start | bytes 786440 | tf_op jit(solution)/shard_map/ppermute | solution.py:26
  7.3 2.0 %collective-permute-start.1 = (bf16[1,128,128]{2,1,0:T(8,128)(2,1)S(1)}, bf16[1,128,128]{2,1,0:T(8,128)(2,1)S(1)}, u32[]{:S(2)}, u32[]{:S(2)}) collective-permute-start(bf16[1,128,128]{2,1,0:T(8,128)(2,1)S(1)} %get-tuple-element.37), channel_id=1, source_target_pairs={{1,2},{2,1},{3,4},{4,3},{5,6},{6,5},{9,10},{10,9},{11,12},{12,11},... | collective-permute-start | bytes 98312 | tf_op jit(solution)/shard_map/ppermute | solution.py:26
  9.3 0.0 collective-permute-done
  9.3 3.2 %collective-permute-done.1 = bf16[1,128,128]{2,1,0:T(8,128)(2,1)S(1)} collective-permute-done((bf16[1,128,128]{2,1,0:T(8,128)(2,1)S(1)}, bf16[1,128,128]{2,1,0:T(8,128)(2,1)S(1)}, u32[]{:S(2)}, u32[]{:S(2)}) %collective-permute-start.1) | collective-permute-done | bytes 32800 | tf_op jit(solution)/shard_map/ppermute | solution.py:26
  12.6 0.7 collective-permute-start.5
  13.2 6.4 %collective-permute-start.3 = (bf16[2,128,128]{2,1,0:T(8,128)(2,1)S(1)}, bf16[2,128,128]{2,1,0:T(8,128)(2,1)S(1)}, u32[]{:S(2)}, u32[]{:S(2)}) collective-permute-start(bf16[2,128,128]{2,1,0:T(8,128)(2,1)S(1)} %constant_dynamic-update-slice_fusion.own_edge), channel_id=1, source_target_pairs={{0,8},{8,0},{16,24},{24,16},{32,40},{40,32},{48,56},{56,48},{64,72... | collective-permute-start | bytes 196616 | tf_op jit(solution)/shard_map/ppermute | solution.py:26
  19.6 0.0 collective-permute-done.5.odd_edge
  19.6 2.2 %collective-permute-done.3.even_edge = bf16[2,128,128]{2,1,0:T(8,128)(2,1)S(1)} collective-permute-done((bf16[2,128,128]{2,1,0:T(8,128)(2,1)S(1)}, bf16[2,128,128]{2,1,0:T(8,128)(2,1)S(1)}, u32[]{:S(2)}, u32[]{:S(2)}) %collective-permute-start.3) | collective-permute-done | bytes 65568 | tf_op jit(solution)/shard_map/ppermute | solution.py:26
  21.8 0.0 collective-permute-done.4.odd
  21.8 0.0 collective-permute-done.2.even
  21.8 0.0 copy-start
  21.8 0.9 copy-done
  22.8 0.0 copy-start.2
  22.8 1.2 copy-done.2
  24.0 0.0 copy-start.4
  24.0 0.9 copy-done.4
  24.9 2.3 %shard_map.58 = (bf16[1024,128]{1,0:T(8,128)(2,1)S(1)}, f32[32,5,128]{2,1,0:T(8,128)S(1)}) custom-call(bf16[8,128,128]{2,1,0:T(8,128)(2,1)S(1)} %bitcast.14, bf16[2,128,128]{2,1,0:T(8,128)(2,1)S(1)} %constant_dynamic-update-slice_fusion.own_edge, bf16[8,128,128]{2,1,0:T(8,128)(2,1)S(1)} %collective-permute-done.2.even, ...), custom_call_target="tpu_custom_call" | custom-call | flops 905969664 | bytes 3145728 | tf_op jit(solution)/shard_map/pallas_call | solution.py:44
  27.2 0.0 copy-start.6
  27.2 14.2 %all_to_all.30.refs_0_ = f32[32,5,128]{2,1,0:T(8,128)S(1)} all-to-all(f32[32,5,128]{2,1,0:T(8,128)S(1)} %get-tuple-element.20), channel_id=1, replica_groups=mesh['y'=4,'z'=8,'x'=4,'c'=2] {'y','x','c'}, dimensions={0} | all-to-all | bytes 163840 | tf_op jit(solution)/shard_map/all_to_all | solution.py:333
  41.5 11.4 %all_to_all.31.refs_0_ = f32[8,5,128]{2,1,0:T(8,128)S(1)} all-to-all(f32[8,5,128]{2,1,0:T(8,128)S(1)} %shard_map.59), channel_id=1, replica_groups=mesh['y'=4,'z'=8,'x'=4,'c'=2] {'z'}, dimensions={0} | all-to-all | bytes 40960 | tf_op jit(solution)/shard_map/all_to_all | solution.py:333
  52.9 0.0 copy-done.6
  52.9 0.7 shard_map.60
  53.6 6.0 %all-to-all-start.2 = ((f32[32,5,128]{2,1,0:T(8,128)}), f32[32,5,128]{2,1,0:T(8,128)S(1)}, u32[]{:S(2)}, u32[]{:S(2)}) async-start(f32[32,5,128]{2,1,0:T(8,128)} %shard_map.60), calls=%async_computation.2 | async-start | bytes 262144 | tf_op jit(solution)/shard_map/all_to_all | solution.py:333
  59.6 0.0 copy-done.1
  59.6 0.4 shard_map.62.refs_0_
  60.0 5.2 %all-to-all-done.2.refs_0_ = f32[32,5,128]{2,1,0:T(8,128)S(1)} async-done(((f32[32,5,128]{2,1,0:T(8,128)}), f32[32,5,128]{2,1,0:T(8,128)S(1)}, u32[]{:S(2)}, u32[]{:S(2)}) %all-to-all-start.2) | async-done | bytes 81952 | tf_op jit(solution)/shard_map/all_to_all | solution.py:333
  65.2 0.0 copy-start.5
  65.2 0.9 copy-done.5
  66.2 0.0 copy-start.7
  66.2 0.9 copy-done.7
  67.1 7.1 %shard_map.61 = (bf16[1024,128]{1,0:T(8,128)(2,1)}, bf16[1024,128]{1,0:T(8,128)(2,1)S(1)}, bf16[1,128,128]{2,1,0:T(8,128)(2,1)S(1)}, bf16[1,128,128]{2,1,0:T(8,128)(2,1)S(1)}) custom-call(f32[32,5,128]{2,1,0:T(8,128)S(1)} %all-to-all-done.2.refs_0_, bf16[1024,128]{1,0:T(8,128)(2,1)S(1)} %copy-done.7, bf16[1024,128]{1,0:T(8,128)(2,1)S(1)} %bitcast.22), custom_call_target="tpu_custom_call" | custom-call | flops 419430400 | bytes 1048576 | tf_op jit(solution)/shard_map/pallas_call | solution.py:44
  74.3 2.5 %shard_map.63 = bf16[32,112,128]{2,1,0:T(8,128)(2,1)} custom-call(bf16[1152,1024]{1,0:T(8,128)(2,1)S(1)} %shard_map.62.refs_0_, bf16[1024,128]{1,0:T(8,128)(2,1)S(1)} %get-tuple-element.23.refs_1_), custom_call_target="tpu_custom_call" | custom-call | flops 905969664 | bytes 4194304 | tf_op jit(solution)/shard_map/pallas_call | solution.py:44
  76.7 0.0 copy-start.3
  76.8 6.4 %all-to-all-start.3 = ((bf16[32,112,128]{2,1,0:T(8,128)(2,1)}), bf16[32,112,128]{2,1,0:T(8,128)(2,1)S(1)}, u32[]{:S(2)}, u32[]{:S(2)}) async-start(bf16[32,112,128]{2,1,0:T(8,128)(2,1)} %shard_map.63), calls=%async_computation.3 | async-start | bytes 1835008 | tf_op jit(solution)/shard_map/all_to_all | solution.py:333
  83.1 0.7 collective-permute-start.9
  83.8 2.3 %collective-permute-start.8 = (bf16[8,128,128]{2,1,0:T(8,128)(2,1)S(1)}, bf16[8,128,128]{2,1,0:T(8,128)(2,1)S(1)}, u32[]{:S(2)}, u32[]{:S(2)}) collective-permute-start(bf16[8,128,128]{2,1,0:T(8,128)(2,1)S(1)} %bitcast.17), channel_id=1, source_target_pairs={{0,8},{8,0},{16,24},{24,16},{32,40},{40,32},{48,56},{56,48},{64,72... | collective-permute-start | bytes 786440 | tf_op jit(solution)/shard_map/ppermute | solution.py:26
  86.1 0.0 collective-permute-start.6
  86.2 2.6 %collective-permute-start.7 = (bf16[1,128,128]{2,1,0:T(8,128)(2,1)S(1)}, bf16[1,128,128]{2,1,0:T(8,128)(2,1)S(1)}, u32[]{:S(2)}, u32[]{:S(2)}) collective-permute-start(bf16[1,128,128]{2,1,0:T(8,128)(2,1)S(1)} %get-tuple-element.29), channel_id=1, source_target_pairs={{1,2},{2,1},{3,4},{4,3},{5,6},{6,5},{9,10},{10,9},{11,12},{12,11},... | collective-permute-start | bytes 98312 | tf_op jit(solution)/shard_map/ppermute | solution.py:26
  88.7 0.0 collective-permute-done.6
  88.7 6.0 %collective-permute-done.7 = bf16[1,128,128]{2,1,0:T(8,128)(2,1)S(1)} collective-permute-done((bf16[1,128,128]{2,1,0:T(8,128)(2,1)S(1)}, bf16[1,128,128]{2,1,0:T(8,128)(2,1)S(1)}, u32[]{:S(2)}, u32[]{:S(2)}) %collective-permute-start.7) | collective-permute-done | bytes 32800 | tf_op jit(solution)/shard_map/ppermute | solution.py:26
  94.8 8.0 %all-to-all-done.3.refs_0_ = bf16[32,112,128]{2,1,0:T(8,128)(2,1)S(1)} async-done(((bf16[32,112,128]{2,1,0:T(8,128)(2,1)}), bf16[32,112,128]{2,1,0:T(8,128)(2,1)S(1)}, u32[]{:S(2)}, u32[]{:S(2)}) %all-to-all-start.3) | async-done | bytes 917536 | tf_op jit(solution)/shard_map/all_to_all | solution.py:333
  102.7 0.8 shard_map.64
  103.6 0.0 collective-permute-done.9.odd
  103.6 0.0 collective-permute-done.8.even
  103.6 3.4 %all-to-all-start.4 = ((bf16[8,112,128]{2,1,0:T(8,128)(2,1)}), bf16[8,112,128]{2,1,0:T(8,128)(2,1)S(1)}, u32[]{:S(2)}, u32[]{:S(2)}) async-start(bf16[8,112,128]{2,1,0:T(8,128)(2,1)} %shard_map.64), calls=%async_computation.4 | async-start | bytes 458752 | tf_op jit(solution)/shard_map/all_to_all | solution.py:333
  107.0 0.7 collective-permute-start.11
  107.6 4.7 %collective-permute-start.10 = (bf16[2,128,128]{2,1,0:T(8,128)(2,1)S(1)}, bf16[2,128,128]{2,1,0:T(8,128)(2,1)S(1)}, u32[]{:S(2)}, u32[]{:S(2)}) collective-permute-start(bf16[2,128,128]{2,1,0:T(8,128)(2,1)S(1)} %pad_maximum_fusion.own_edge), channel_id=1, source_target_pairs={{0,8},{8,0},{16,24},{24,16},{32,40},{40,32},{48,56},{56,48},{64,72... | collective-permute-start | bytes 196616 | tf_op jit(solution)/shard_map/ppermute | solution.py:26
  112.4 6.5 %all-to-all-done.4.refs_0_ = bf16[8,112,128]{2,1,0:T(8,128)(2,1)S(1)} async-done(((bf16[8,112,128]{2,1,0:T(8,128)(2,1)}), bf16[8,112,128]{2,1,0:T(8,128)(2,1)S(1)}, u32[]{:S(2)}, u32[]{:S(2)}) %all-to-all-start.4) | async-done | bytes 229408 | tf_op jit(solution)/shard_map/all_to_all | solution.py:333
  118.8 0.7 shard_map.65
  119.5 0.0 collective-permute-done.11.odd_edge
  119.5 0.0 collective-permute-done.10.even_edge
  119.5 3.4 %all-to-all-start.5 = ((f32[4,112,128]{2,1,0:T(8,128)}), f32[4,112,128]{2,1,0:T(8,128)S(1)}, u32[]{:S(2)}, u32[]{:S(2)}) async-start(f32[4,112,128]{2,1,0:T(8,128)} %shard_map.65), calls=%async_computation.5 | async-start | bytes 458752 | tf_op jit(solution)/shard_map/all_to_all | solution.py:333
  122.9 0.0 copy-done.3
  122.9 2.6 %shard_map.66 = bf16[1024,128]{1,0:T(8,128)(2,1)} custom-call(bf16[8,128,128]{2,1,0:T(8,128)(2,1)S(1)} %bitcast.18, bf16[2,128,128]{2,1,0:T(8,128)(2,1)S(1)} %pad_maximum_fusion.own_edge, bf16[8,128,128]{2,1,0:T(8,128)(2,1)S(1)} %collective-permute-done.8.even, bf16[2,128,128]{2,1,0:T(8,128)(2,1)S(1)} %collective-permute-done.10.even_edge, ...), custom_call_target="tpu_custom_call" | custom-call | flops 905969664 | bytes 3145728 | tf_op jit(solution)/shard_map/pallas_call | solution.py:44
  125.6 3.8 %all-to-all-done.5 = f32[4,112,128]{2,1,0:T(8,128)S(1)} async-done(((f32[4,112,128]{2,1,0:T(8,128)}), f32[4,112,128]{2,1,0:T(8,128)S(1)}, u32[]{:S(2)}, u32[]{:S(2)}) %all-to-all-start.5) | async-done | bytes 229408 | tf_op jit(solution)/shard_map/all_to_all | solution.py:333
  129.4 0.7 slice.4
  (4 shorter events, 0.1 us)
Async XLA Ops:
  0.6 59.0 %copy-start.1 = (bf16[1,8,128,128]{3,2,1,0:T(8,128)(2,1)S(1)}, bf16[1,8,128,128]{3,2,1,0:T(8,128)(2,1)}, u32[]{:S(2)}) copy-start(bf16[1,8,128,128]{3,2,1,0:T(8,128)(2,1)} %param.3) | copy-start | bytes 786436
  1.5 7.8 %collective-permute-start = (bf16[1,128,128]{2,1,0:T(8,128)(2,1)S(1)}, bf16[1,128,128]{2,1,0:T(8,128)(2,1)S(1)}, u32[]{:S(2)}, u32[]{:S(2)}) collective-permute-start(bf16[1,128,128]{2,1,0:T(8,128)(2,1)S(1)} %get-tuple-element.38), channel_id=1, source_target_pairs={{0,1},{1,0},{2,3},{3,2},{4,5},{5,4},{6,7},{7,6},{8,9},{9,8},{10,11... | collective-permute-start | bytes 98312 | tf_op jit(solution)/shard_map/ppermute | solution.py:26
  1.5 20.4 %collective-permute-start.4 = (bf16[8,128,128]{2,1,0:T(8,128)(2,1)}, bf16[8,128,128]{2,1,0:T(8,128)(2,1)S(1)}, u32[]{:S(2)}, u32[]{:S(2)}) collective-permute-start(bf16[8,128,128]{2,1,0:T(8,128)(2,1)} %bitcast.12), channel_id=1, source_target_pairs={{8,16},{16,8},{24,32},{32,24},{40,48},{48,40},{56,64},{64,56},{72,... | collective-permute-start | bytes 786440 | tf_op jit(solution)/shard_map/ppermute | solution.py:26
  2.2 19.7 %collective-permute-start.2 = (bf16[8,128,128]{2,1,0:T(8,128)(2,1)}, bf16[8,128,128]{2,1,0:T(8,128)(2,1)S(1)}, u32[]{:S(2)}, u32[]{:S(2)}) collective-permute-start(bf16[8,128,128]{2,1,0:T(8,128)(2,1)} %bitcast.13), channel_id=1, source_target_pairs={{0,8},{8,0},{16,24},{24,16},{32,40},{40,32},{48,56},{56,48},{64,72... | collective-permute-start | bytes 786440 | tf_op jit(solution)/shard_map/ppermute | solution.py:26
  7.3 5.2 %collective-permute-start.1 = (bf16[1,128,128]{2,1,0:T(8,128)(2,1)S(1)}, bf16[1,128,128]{2,1,0:T(8,128)(2,1)S(1)}, u32[]{:S(2)}, u32[]{:S(2)}) collective-permute-start(bf16[1,128,128]{2,1,0:T(8,128)(2,1)S(1)} %get-tuple-element.37), channel_id=1, source_target_pairs={{1,2},{2,1},{3,4},{4,3},{5,6},{6,5},{9,10},{10,9},{11,12},{12,11},... | collective-permute-start | bytes 98312 | tf_op jit(solution)/shard_map/ppermute | solution.py:26
  12.6 7.0 %collective-permute-start.5 = (bf16[2,128,128]{2,1,0:T(8,128)(2,1)S(1)}, bf16[2,128,128]{2,1,0:T(8,128)(2,1)S(1)}, u32[]{:S(2)}, u32[]{:S(2)}) collective-permute-start(bf16[2,128,128]{2,1,0:T(8,128)(2,1)S(1)} %constant_dynamic-update-slice_fusion.own_edge), channel_id=1, source_target_pairs={{8,16},{16,8},{24,32},{32,24},{40,48},{48,40},{56,64},{64,56},{72,... | collective-permute-start | bytes 196616 | tf_op jit(solution)/shard_map/ppermute | solution.py:26
  13.2 8.6 %collective-permute-start.3 = (bf16[2,128,128]{2,1,0:T(8,128)(2,1)S(1)}, bf16[2,128,128]{2,1,0:T(8,128)(2,1)S(1)}, u32[]{:S(2)}, u32[]{:S(2)}) collective-permute-start(bf16[2,128,128]{2,1,0:T(8,128)(2,1)S(1)} %constant_dynamic-update-slice_fusion.own_edge), channel_id=1, source_target_pairs={{0,8},{8,0},{16,24},{24,16},{32,40},{40,32},{48,56},{56,48},{64,72... | collective-permute-start | bytes 196616 | tf_op jit(solution)/shard_map/ppermute | solution.py:26
  21.8 1.0 copy-start
  22.8 1.2 copy-start.2
  24.0 0.9 copy-start.4
  27.2 25.7 %copy-start.6 = (bf16[1024,128]{1,0:T(8,128)(2,1)}, bf16[1024,128]{1,0:T(8,128)(2,1)S(1)}, u32[]{:S(2)}) copy-start(bf16[1024,128]{1,0:T(8,128)(2,1)S(1)} %get-tuple-element.21.refs_1_) | copy-start | bytes 786436
  53.6 11.6 %all-to-all-start.2 = ((f32[32,5,128]{2,1,0:T(8,128)}), f32[32,5,128]{2,1,0:T(8,128)S(1)}, u32[]{:S(2)}, u32[]{:S(2)}) async-start(f32[32,5,128]{2,1,0:T(8,128)} %shard_map.60), calls=%async_computation.2 | async-start | bytes 262144 | tf_op jit(solution)/shard_map/all_to_all | solution.py:333
  65.2 1.0 copy-start.5
  66.2 0.9 copy-start.7
  76.7 46.2 %copy-start.3 = (bf16[3,3,3,128,128]{4,3,2,1,0:T(8,128)(2,1)S(1)}, bf16[3,3,3,128,128]{4,3,2,1,0:T(8,128)(2,1)}, u32[]{:S(2)}) copy-start(bf16[3,3,3,128,128]{4,3,2,1,0:T(8,128)(2,1)} %param.4) | copy-start | bytes 2654212
  76.8 26.0 %all-to-all-start.3 = ((bf16[32,112,128]{2,1,0:T(8,128)(2,1)}), bf16[32,112,128]{2,1,0:T(8,128)(2,1)S(1)}, u32[]{:S(2)}, u32[]{:S(2)}) async-start(bf16[32,112,128]{2,1,0:T(8,128)(2,1)} %shard_map.63), calls=%async_computation.3 | async-start | bytes 1835008 | tf_op jit(solution)/shard_map/all_to_all | solution.py:333
  83.1 20.4 %collective-permute-start.9 = (bf16[8,128,128]{2,1,0:T(8,128)(2,1)S(1)}, bf16[8,128,128]{2,1,0:T(8,128)(2,1)S(1)}, u32[]{:S(2)}, u32[]{:S(2)}) collective-permute-start(bf16[8,128,128]{2,1,0:T(8,128)(2,1)S(1)} %bitcast.16), channel_id=1, source_target_pairs={{8,16},{16,8},{24,32},{32,24},{40,48},{48,40},{56,64},{64,56},{72,... | collective-permute-start | bytes 786440 | tf_op jit(solution)/shard_map/ppermute | solution.py:26
  83.8 19.7 %collective-permute-start.8 = (bf16[8,128,128]{2,1,0:T(8,128)(2,1)S(1)}, bf16[8,128,128]{2,1,0:T(8,128)(2,1)S(1)}, u32[]{:S(2)}, u32[]{:S(2)}) collective-permute-start(bf16[8,128,128]{2,1,0:T(8,128)(2,1)S(1)} %bitcast.17), channel_id=1, source_target_pairs={{0,8},{8,0},{16,24},{24,16},{32,40},{40,32},{48,56},{56,48},{64,72... | collective-permute-start | bytes 786440 | tf_op jit(solution)/shard_map/ppermute | solution.py:26
  86.1 2.6 %collective-permute-start.6 = (bf16[1,128,128]{2,1,0:T(8,128)(2,1)S(1)}, bf16[1,128,128]{2,1,0:T(8,128)(2,1)S(1)}, u32[]{:S(2)}, u32[]{:S(2)}) collective-permute-start(bf16[1,128,128]{2,1,0:T(8,128)(2,1)S(1)} %get-tuple-element.28), channel_id=1, source_target_pairs={{0,1},{1,0},{2,3},{3,2},{4,5},{5,4},{6,7},{7,6},{8,9},{9,8},{10,11... | collective-permute-start | bytes 98312 | tf_op jit(solution)/shard_map/ppermute | solution.py:26
  86.2 8.6 %collective-permute-start.7 = (bf16[1,128,128]{2,1,0:T(8,128)(2,1)S(1)}, bf16[1,128,128]{2,1,0:T(8,128)(2,1)S(1)}, u32[]{:S(2)}, u32[]{:S(2)}) collective-permute-start(bf16[1,128,128]{2,1,0:T(8,128)(2,1)S(1)} %get-tuple-element.29), channel_id=1, source_target_pairs={{1,2},{2,1},{3,4},{4,3},{5,6},{6,5},{9,10},{10,9},{11,12},{12,11},... | collective-permute-start | bytes 98312 | tf_op jit(solution)/shard_map/ppermute | solution.py:26
  103.6 15.2 %all-to-all-start.4 = ((bf16[8,112,128]{2,1,0:T(8,128)(2,1)}), bf16[8,112,128]{2,1,0:T(8,128)(2,1)S(1)}, u32[]{:S(2)}, u32[]{:S(2)}) async-start(bf16[8,112,128]{2,1,0:T(8,128)(2,1)} %shard_map.64), calls=%async_computation.4 | async-start | bytes 458752 | tf_op jit(solution)/shard_map/all_to_all | solution.py:333
  107.0 12.6 %collective-permute-start.11 = (bf16[2,128,128]{2,1,0:T(8,128)(2,1)S(1)}, bf16[2,128,128]{2,1,0:T(8,128)(2,1)S(1)}, u32[]{:S(2)}, u32[]{:S(2)}) collective-permute-start(bf16[2,128,128]{2,1,0:T(8,128)(2,1)S(1)} %pad_maximum_fusion.own_edge), channel_id=1, source_target_pairs={{8,16},{16,8},{24,32},{32,24},{40,48},{48,40},{56,64},{64,56},{72,... | collective-permute-start | bytes 196616 | tf_op jit(solution)/shard_map/ppermute | solution.py:26
  107.6 11.9 %collective-permute-start.10 = (bf16[2,128,128]{2,1,0:T(8,128)(2,1)S(1)}, bf16[2,128,128]{2,1,0:T(8,128)(2,1)S(1)}, u32[]{:S(2)}, u32[]{:S(2)}) collective-permute-start(bf16[2,128,128]{2,1,0:T(8,128)(2,1)S(1)} %pad_maximum_fusion.own_edge), channel_id=1, source_target_pairs={{0,8},{8,0},{16,24},{24,16},{32,40},{40,32},{48,56},{56,48},{64,72... | collective-permute-start | bytes 196616 | tf_op jit(solution)/shard_map/ppermute | solution.py:26
  119.5 9.9 %all-to-all-start.5 = ((f32[4,112,128]{2,1,0:T(8,128)}), f32[4,112,128]{2,1,0:T(8,128)S(1)}, u32[]{:S(2)}, u32[]{:S(2)}) async-start(f32[4,112,128]{2,1,0:T(8,128)} %shard_map.65), calls=%async_computation.5 | async-start | bytes 458752 | tf_op jit(solution)/shard_map/all_to_all | solution.py:333

commit v4 on v3

--- a/solution.py
+++ b/solution.py
@@ -38,13 +38,14 @@
     return swapped(block, GZ, nz, 0), swapped(block, GZ, nz, 1)
 
 
-def call(kernel, out_shape, scratch, flops, moved, *operands):
+def call(kernel, out_shape, scratch, flops, moved, *operands, far=()):
     vmem = pl.BlockSpec(memory_space=pltpu.VMEM)
+    hbm = pl.BlockSpec(memory_space=pltpu.HBM)
     many = isinstance(out_shape, (list, tuple))
     return pl.pallas_call(
         kernel,
         out_shape=out_shape,
-        in_specs=[vmem] * len(operands),
+        in_specs=[hbm if i in far else vmem for i in range(len(operands))],
         out_specs=[vmem] * len(out_shape) if many else vmem,
         scratch_shapes=scratch,
         compiler_params=pltpu.CompilerParams(vmem_limit_bytes=VMEM_BYTES),
@@ -102,18 +103,30 @@
     return lax.dot_general(left, right, (((0,), (0,)), ((), ())), preferred_element_type=F32)
 
 
+def ready_kernel(block, weight, target, block_out, wide_out, target_out, sems):
+    _, channels, _ = weight.shape
+    moves = [
+        pltpu.make_async_copy(block, block_out, sems.at[27]),
+        pltpu.make_async_copy(target, target_out, sems.at[28]),
+    ]
+    for tap in range(27):
+        slot, tap_x = tap // 3, tap % 3
+        place = wide_out.at[
+            slot * channels : (slot + 1) * channels, tap_x * channels : (tap_x + 1) * channels
+        ]
+        moves.append(pltpu.make_async_copy(weight.at[tap], place, sems.at[tap]))
+    for move in moves:
+        move.start()
+    for move in moves:
+        move.wait()
+
+
 def conv_kernel(
-    own, own_edge, even, even_edge, odd, odd_edge, weight, target,
-    hidden_out, sheet_out, wide, kernel_wide,
+    own, own_edge, even, even_edge, odd, odd_edge, kernel_wide, target,
+    hidden_out, sheet_out, wide,
 ):
     rows, columns, channels = own.shape
     place_all(wide, (own, own_edge), (even, even_edge), (odd, odd_edge), False)
-    for slot in range(9):
-        for tap_x in range(3):
-            kernel_wide[
-                slot * channels : (slot + 1) * channels,
-                tap_x * channels : (tap_x + 1) * channels,
-            ] = weight[slot * 3 + tap_x]
     flat = wide[...].reshape(rows * columns, 9 * channels)
     product = jnp.dot(flat, kernel_wide[...], preferred_element_type=F32)
     total = product[:, channels : 2 * channels]
@@ -139,10 +152,6 @@
     sheet_out[1, each:depth, :] = jnp.sum(features.astype(F32), axis=0, keepdims=True)
 
 
-def exact(left, right):
-    return jnp.dot(left, right, precision=HIGHEST, preferred_element_type=F32)
-
-
 def thirds(value):
     high = value.astype(BF16)
     rest = value - high.astype(F32)
@@ -150,6 +159,24 @@
     return high, middle, (rest - middle.astype(F32)).astype(BF16)
 
 
+def left_terms(value):
+    high, middle, low = thirds(value)
+    return jnp.concatenate([low, high, middle, middle, high, high], axis=1)
+
+
+def right_terms(value):
+    high, middle, low = thirds(value)
+    return jnp.concatenate([high, low, middle, high, middle, high], axis=0)
+
+
+def exact(left, *rights):
+    if len(rights) == 1:
+        right = right_terms(rights[0])
+    else:
+        right = jnp.concatenate([right_terms(value) for value in rights], axis=1)
+    return jnp.dot(left_terms(left), right, preferred_element_type=F32)
+
+
 def through(values, matrix):
     high, middle, low = thirds(matrix)
     total = jnp.dot(values, low, preferred_element_type=F32)
@@ -158,8 +185,13 @@
 
 
 def whiten_kernel(
-    voxels, columns, sheet, hidden, target, whitened_out, grad_out, first_out, second_out, mats
+    voxels, columns, sheet, hidden, target, whitened_out, grad_out, first_out, second_out,
+    mats, hidden_here, target_here, sems,
 ):
+    hidden_move = pltpu.make_async_copy(hidden, hidden_here, sems.at[0])
+    target_move = pltpu.make_async_copy(target, target_here, sems.at[1])
+    hidden_move.start()
+    target_move.start()
     spread, depth, channels = sheet.shape
     each = depth - 1
     for j in range(spread):
@@ -190,41 +222,43 @@
     scaled = covariance / trace
     root = jnp.sqrt(trace)
 
+    direction = cross / root
     iterate = jnp.where(diagonal, 1.5, 0.0) - 0.5 * scaled
-    saved = []
+    change = -0.5 * direction
+    slope = jnp.where(diagonal, -0.5, 0.0)
+
+    def column(value, i):
+        return value[:, i * channels : (i + 1) * channels]
+
     for sweep in range(1, NEWTON):
-        pair = exact(iterate, jnp.concatenate([iterate, scaled], axis=1))
-        squared, once = pair[:, :channels], pair[:, channels:]
-        triple = exact(squared, jnp.concatenate([once, scaled, iterate], axis=1))
-        saved.append(
-            (iterate, squared, once, triple[:, channels : 2 * channels], triple[:, 2 * channels :])
-        )
-        iterate = 1.5 * iterate - 0.5 * triple[:, :channels]
+        first = exact(iterate, iterate, scaled, change, direction)
+        squared, once = column(first, 0), column(first, 1)
+        turned = exact(change, iterate, scaled)
+        steep = exact(slope, scaled)
+        second_level = exact(squared, once, column(first, 3) + column(turned, 1), steep, iterate)
+        moved = column(second_level, 1) + exact(column(first, 2) + column(turned, 0), once)
+        change = 1.5 * change - 0.5 * moved
+        slope = 1.5 * slope - 0.5 * (3.0 * column(second_level, 2) + column(second_level, 3))
+        iterate = 1.5 * iterate - 0.5 * column(second_level, 0)
     whitener = iterate / root
-    white_grad = exact(whitener, second) - cross
-    direction = white_grad / root
-    change = -0.5 * direction
-    for iterate_k, squared, once, cubic, cube in saved:
-        left = exact(jnp.concatenate([iterate_k, squared], axis=0), change)
-        both = jnp.concatenate([left[:channels], left[channels:]], axis=1)
-        moved = exact(both, jnp.concatenate([once, scaled], axis=0))
-        moved = moved + exact(
-            jnp.concatenate([change, cube], axis=1), jnp.concatenate([cubic, direction], axis=0)
-        )
-        change = 1.5 * change - 0.5 * moved
+    whitener_t = whitener.T
+    aligned = exact(whitener, second)
+    white_grad = aligned - cross
+    change = exact(slope, aligned) / root - change
     trace_grad = -0.5 * group_sums(white_grad * whitener) / trace
     trace_grad = trace_grad - group_sums(change * scaled) / trace
     sigma_grad = change / trace + jnp.where(diagonal, trace_grad, 0.0)
     symmetric = (sigma_grad + sigma_grad.T) / voxels
-    whitener_t = whitener.T
     backward = (exact(whitener_t, whitener) + symmetric).T
 
     both = jnp.concatenate([whitener_t, backward], axis=1)
-    offset = exact(jnp.broadcast_to(mean, (8, channels)), both)[0:1]
+    offset = exact(jnp.broadcast_to(mean, (8, channels)), whitener_t, backward)[0:1]
     target_offset = exact(jnp.broadcast_to(target_sum / voxels, (8, channels)), whitener)[0:1]
-    mixed = through(hidden[...], both) - offset
+    hidden_move.wait()
+    target_move.wait()
+    mixed = through(hidden_here[...], both) - offset
     whitened_out[...] = mixed[:, :channels].astype(BF16)
-    pulled = through(target[...], whitener) - target_offset
+    pulled = through(target_here[...], whitener) - target_offset
     grad = (mixed[:, channels:] - pulled).astype(BF16)
     grad_out[...] = grad
     odd_row = lax.axis_index("c")
@@ -273,30 +307,34 @@
             turn(2, *above)
 
 
-def weight_kernel(columns, share, turned, grad, parts_out, wide):
+def weight_kernel(columns, share, turned, grad, keep_out, send_out, wide, terms):
     count, channels = grad.shape
     value = grad[...].astype(F32)
     wide[:, :channels] = moved_columns(value, -1, columns).astype(BF16)
     wide[:, channels : 2 * channels] = grad[...]
     wide[:, 2 * channels :] = moved_columns(value, 1, columns).astype(BF16)
-    blocks = channels // share
-    taps_each = parts_out.shape[1] // share
-    terms = jnp.dot(turned[...], wide[...], preferred_element_type=F32).astype(BF16)
-    for tap in range(27):
+    pairs = channels // share // 2
+    taps_each = keep_out.shape[1] // share
+    terms[...] = jnp.dot(turned[...], wide[...], preferred_element_type=F32)
+    mine = pl.multiple_of(lax.axis_index("c") * share, share)
+    others = pl.multiple_of((1 - lax.axis_index("c")) * share, share)
+    for tap in range(keep_out.shape[0] // pairs * taps_each):
         slot, tap_x = tap // 3, tap % 3
-        group, place = tap // taps_each, tap % taps_each
-        for block in range(blocks):
-            first = slot * channels + block * share
-            parts_out[group * blocks + block, place * share : (place + 1) * share, :] = terms[
-                first : first + share, tap_x * channels : (tap_x + 1) * channels
-            ]
-    spare = parts_out.shape[0] // blocks * taps_each
-    for tap in range(27, spare):
-        group, place = tap // taps_each, tap % taps_each
-        for block in range(blocks):
-            parts_out[group * blocks + block, place * share : (place + 1) * share, :] = jnp.zeros(
-                (share, channels), BF16
-            )
+        cols = slice(tap_x * channels, (tap_x + 1) * channels)
+        place = slice(tap % taps_each * share, (tap % taps_each + 1) * share)
+        for pair in range(pairs):
+            group = tap // taps_each * pairs + pair
+            base = slot * channels + pair * 2 * share
+            if tap < 27:
+                keep_out[group, place, :] = terms[pl.ds(base + mine, share), cols]
+                send_out[group, place, :] = terms[pl.ds(base + others, share), cols].astype(BF16)
+            else:
+                keep_out[group, place, :] = jnp.zeros((share, channels), F32)
+                send_out[group, place, :] = jnp.zeros((share, channels), BF16)
+
+
+def pair_kernel(kept, received, sum_out):
+    sum_out[...] = (kept[...] + received[...].astype(F32)).astype(BF16)
 
 
 def input_kernel(
@@ -360,7 +398,17 @@
     edges = row_swaps(first_send, second_send)
     even, odd = plane_swaps(block)
     even_edges, odd_edges = plane_swaps(edges)
-    planes = [block, edges, even, even_edges, odd, odd_edges]
+    near, kernel_wide, target_near = call(
+        ready_kernel,
+        [
+            jax.ShapeDtypeStruct(block.shape, BF16),
+            jax.ShapeDtypeStruct((9 * channels, 3 * channels), BF16),
+            jax.ShapeDtypeStruct((count, channels), BF16),
+        ],
+        [pltpu.SemaphoreType.DMA((29,))],
+        0, 2**20, block, weight, target_flat, far=(0, 1, 2),
+    )
+    planes = [near, edges, even, even_edges, odd, odd_edges]
     wide = pltpu.VMEM((rows, columns, 9 * channels), BF16)
     hidden, sheet = call(
         conv_kernel,
@@ -368,8 +416,8 @@
             jax.ShapeDtypeStruct((count, channels), BF16),
             jax.ShapeDtypeStruct((spread, 2 * G // spread + 1, channels), F32),
         ],
-        [wide, pltpu.VMEM((9 * channels, 3 * channels), BF16)],
-        flops, 3 * 2**20, *planes, weight, target_flat,
+        [wide],
+        flops, 3 * 2**20, *planes, kernel_wide, target_near,
     )
     turned = call(
         turn_kernel,
@@ -384,22 +432,36 @@
     whitened, grad_hidden, first_send, second_send = call(
         lambda *refs: whiten_kernel(voxels, columns, *refs),
         [jax.ShapeDtypeStruct((count, channels), BF16)] * 2 + [line] * 2,
-        [pltpu.VMEM((2 * G, channels), F32)],
-        100 * 2 * channels**3, 2**20, sheet, hidden, target_flat,
-    )
-
+        [
+            pltpu.VMEM((2 * G, channels), F32),
+            pltpu.VMEM((count, channels), BF16),
+            pltpu.VMEM((count, channels), BF16),
+            pltpu.SemaphoreType.DMA((2,)),
+        ],
+        100 * 2 * channels**3, 2**20, sheet, hidden, target_flat, far=(1, 2),
+    )
+
+    groups = spread // 2
+    shape = (groups, taps_each * share, channels)
+    keep, send = call(
+        lambda *refs: weight_kernel(columns, share, *refs),
+        [jax.ShapeDtypeStruct(shape, F32), jax.ShapeDtypeStruct(shape, BF16)],
+        [
+            pltpu.VMEM((count, 3 * channels), BF16),
+            pltpu.VMEM((9 * channels, 3 * channels), F32),
+        ],
+        flops, 4 * 2**20, turned, grad_hidden,
+    )
+    received = lax.ppermute(send, ("c",), [(0, 1), (1, 0)])
     parts = call(
-        lambda *refs: weight_kernel(columns, share, *refs),
-        jax.ShapeDtypeStruct((spread, taps_each * share, channels), BF16),
-        [pltpu.VMEM((count, 3 * channels), BF16)],
-        flops, 4 * 2**20, turned, grad_hidden,
+        pair_kernel, jax.ShapeDtypeStruct(shape, BF16), [], keep.size, 2**21, keep, received
     )
     block, first_send, second_send, parts = lax.optimization_barrier(
         (grad_hidden.reshape(rows, columns, channels), first_send, second_send, parts)
     )
     edges = row_swaps(first_send, second_send)
     even, odd = plane_swaps(block)
-    part = total_copies(exchange(parts, SPREAD), levels, BF16)
+    part = total_copies(exchange(parts, ("y", "x")), levels, BF16)
     part, edges, even, odd = lax.optimization_barrier((part, edges, even, odd))
     even_edges, odd_edges = plane_swaps(edges)
     part = total_copies(exchange(part, ("z",)), rows_y, F32, 1.0 / math.sqrt(voxels))

time: 131 us -> 122 us (0.931)
  waiting for transfers between devices: 35 us -> 26.1 us
    ppermute x12, waiting for transfers between devices: 11.5 us -> 5.89 us  [swapped(): return lax.ppermute(block, axes, pairs)]
    all_to_all x4, waiting for transfers between devices: 23.5 us -> 18.5 us  [exchange(): return lax.all_to_all(parts, axes, 0, 0, tiled=True)]
    ppermute x0 -> x1, waiting for transfers between devices: none -> 1.7 us  [local(): received = lax.ppermute(send, ('c',), [(0, 1), (1, 0)])]
    pallas_call x9 -> x11, Pallas kernels: 17.2 us -> 16.7 us  [call(): pl.pallas_call(kernel, out_shape=out_shape, in_specs=[hbm if i in far els...]
    unnamed x17 -> x19, local copies, waits for them, and re-layouts: 4.99 us -> 4.88 us
  transfers between devices with their start and end apart: 16 -> 17, of which waited for: 7 -> 7; matrix products, arithmetic and copies ran while one was open for 0% -> 0% of each run, Pallas kernels for 4% -> 4%
where the time goes in v4:
time: 122 us; the launch traced here: 120 us
  starting transfers between devices  45.5 us (37%)
  waiting for transfers between devices  26.1 us (21%)
  blocking collectives  24.8 us (20%)
  Pallas kernels  16.7 us (14%)
  local copies, waits for them, and re-layouts  6.37 us (5%)
    ppermute x12, starting transfers between devices, swapped(): return lax.ppermute(block, axes, pairs)  25.9 us
    all_to_all x2, blocking collectives, exchange(): return lax.all_to_all(parts, axes, 0, 0, tiled=True)  24.8 us
    all_to_all x4, starting transfers between devices, exchange(): return lax.all_to_all(parts, axes, 0, 0, tiled=True)  19.4 us
    all_to_all x4, waiting for transfers between devices, exchange(): return lax.all_to_all(parts, axes, 0, 0, tiled=True)  18.5 us
    pallas_call x11, Pallas kernels, call(): pl.pallas_call(kernel, out_shape=out_shape, in_specs=[hbm if i in far els...  16.7 us
    ppermute x12, waiting for transfers between devices, swapped(): return lax.ppermute(block, axes, pairs)  5.89 us
    unnamed x19, local copies, waits for them, and re-layouts  4.88 us
  transfers between devices with their start and end apart: 17, of which 7 were waited for; matrix products, arithmetic and copies ran while one was open for 0% of the time, Pallas kernels for 4%

profile of v4, /device:TPU:4, one launch (start us, length us, event | category | flops | bytes accessed | tf_op | source)
XLA Modules:
  0.0 120.3 jit_solution(5041203983404366534)
XLA Ops:
  0.6 0.8 dynamic-slice_bitcast_fusion
  1.4 0.0 collective-permute-start
  1.4 0.7 collective-permute-start.4
  2.1 5.2 %collective-permute-start.2 = (bf16[8,128,128]{2,1,0:T(8,128)(2,1)}, bf16[8,128,128]{2,1,0:T(8,128)(2,1)S(1)}, u32[]{:S(2)}, u32[]{:S(2)}) collective-permute-start(bf16[8,128,128]{2,1,0:T(8,128)(2,1)} %bitcast.15), channel_id=1, source_target_pairs={{0,8},{8,0},{16,24},{24,16},{32,40},{40,32},{48,56},{56,48},{64,72... | collective-permute-start | bytes 786440 | tf_op jit(solution)/shard_map/ppermute | solution.py:26
  7.3 2.0 %collective-permute-start.1 = (bf16[1,128,128]{2,1,0:T(8,128)(2,1)S(1)}, bf16[1,128,128]{2,1,0:T(8,128)(2,1)S(1)}, u32[]{:S(2)}, u32[]{:S(2)}) collective-permute-start(bf16[1,128,128]{2,1,0:T(8,128)(2,1)S(1)} %get-tuple-element.47), channel_id=1, source_target_pairs={{1,2},{2,1},{3,4},{4,3},{5,6},{6,5},{9,10},{10,9},{11,12},{12,11},... | collective-permute-start | bytes 98312 | tf_op jit(solution)/shard_map/ppermute | solution.py:26
  9.2 0.0 collective-permute-done
  9.3 3.2 %collective-permute-done.1 = bf16[1,128,128]{2,1,0:T(8,128)(2,1)S(1)} collective-permute-done((bf16[1,128,128]{2,1,0:T(8,128)(2,1)S(1)}, bf16[1,128,128]{2,1,0:T(8,128)(2,1)S(1)}, u32[]{:S(2)}, u32[]{:S(2)}) %collective-permute-start.1) | collective-permute-done | bytes 32800 | tf_op jit(solution)/shard_map/ppermute | solution.py:26
  12.5 0.7 collective-permute-start.5
  13.2 6.4 %collective-permute-start.3 = (bf16[2,128,128]{2,1,0:T(8,128)(2,1)S(1)}, bf16[2,128,128]{2,1,0:T(8,128)(2,1)S(1)}, u32[]{:S(2)}, u32[]{:S(2)}) collective-permute-start(bf16[2,128,128]{2,1,0:T(8,128)(2,1)S(1)} %constant_dynamic-update-slice_fusion.own_edge), channel_id=1, source_target_pairs={{0,8},{8,0},{16,24},{24,16},{32,40},{40,32},{48,56},{56,48},{64,72... | collective-permute-start | bytes 196616 | tf_op jit(solution)/shard_map/ppermute | solution.py:26
  19.5 0.0 copy-start
  19.5 1.2 copy-done
  20.7 0.0 copy-start.2
  20.7 0.9 copy-done.2
  21.7 0.0 copy-start.3
  21.7 0.9 copy-done.3
  22.6 0.5 shard_map.58
  23.1 0.0 collective-permute-done.5.odd_edge
  23.1 0.0 collective-permute-done.3.even_edge
  23.1 0.0 copy-start.5
  23.2 0.0 collective-permute-done.4.odd
  23.2 0.0 collective-permute-done.2.even
  23.2 2.2 %shard_map.59 = (bf16[1024,128]{1,0:T(8,128)(2,1)S(1)}, f32[32,5,128]{2,1,0:T(8,128)S(1)}) custom-call(bf16[8,128,128]{2,1,0:T(8,128)(2,1)S(1)} %get-tuple-element.25.own, bf16[2,128,128]{2,1,0:T(8,128)(2,1)S(1)} %constant_dynamic-update-slice_fusion.own_edge, bf16[8,128,128]{2,1,0:T(8,128)(2,1)S(1)} %collective-permute-done.2.even, ...), custom_call_target="tpu_custom_call" | custom-call | flops 905969664 | bytes 3145728 | tf_op jit(solution)/shard_map/pallas_call | solution.py:45
  25.4 0.0 copy-start.7
  25.4 0.0 copy-start.4
  25.4 13.1 %all_to_all.30.refs_0_ = f32[32,5,128]{2,1,0:T(8,128)S(1)} all-to-all(f32[32,5,128]{2,1,0:T(8,128)S(1)} %get-tuple-element.28), channel_id=1, replica_groups=mesh['y'=4,'z'=8,'x'=4,'c'=2] {'y','x','c'}, dimensions={0} | all-to-all | bytes 163840 | tf_op jit(solution)/shard_map/all_to_all | solution.py:371
  38.5 11.7 %all_to_all.31.refs_0_ = f32[8,5,128]{2,1,0:T(8,128)S(1)} all-to-all(f32[8,5,128]{2,1,0:T(8,128)S(1)} %shard_map.60), channel_id=1, replica_groups=mesh['y'=4,'z'=8,'x'=4,'c'=2] {'z'}, dimensions={0} | all-to-all | bytes 40960 | tf_op jit(solution)/shard_map/all_to_all | solution.py:371
  50.2 0.0 copy-done.5
  50.2 0.0 copy-done.7
  50.2 0.7 shard_map.61
  50.9 6.6 %all-to-all-start.2 = ((f32[32,5,128]{2,1,0:T(8,128)}), f32[32,5,128]{2,1,0:T(8,128)}, u32[]{:S(2)}, u32[]{:S(2)}) async-start(f32[32,5,128]{2,1,0:T(8,128)} %shard_map.61), calls=%async_computation.2 | async-start | bytes 262144 | tf_op jit(solution)/shard_map/all_to_all | solution.py:371
  57.6 0.0 copy-start.6
  57.6 0.8 copy-done.6
  58.4 0.4 shard_map.63.refs_0_
  58.8 4.4 %all-to-all-done.2.refs_0_ = f32[32,5,128]{2,1,0:T(8,128)} async-done(((f32[32,5,128]{2,1,0:T(8,128)}), f32[32,5,128]{2,1,0:T(8,128)}, u32[]{:S(2)}, u32[]{:S(2)}) %all-to-all-start.2) | async-done | bytes 81952 | tf_op jit(solution)/shard_map/all_to_all | solution.py:371
  63.3 0.0 copy-done.4
  63.3 0.9 copy-done.8
  64.2 6.1 %shard_map.62 = (bf16[1024,128]{1,0:T(8,128)(2,1)}, bf16[1024,128]{1,0:T(8,128)(2,1)S(1)}, bf16[1,128,128]{2,1,0:T(8,128)(2,1)S(1)}, bf16[1,128,128]{2,1,0:T(8,128)(2,1)S(1)}) custom-call(f32[32,5,128]{2,1,0:T(8,128)} %all-to-all-done.2.refs_0_, bf16[1024,128]{1,0:T(8,128)(2,1)S(1)} %copy-done.8, bf16[1024,128]{1,0:T(8,128)(2,1)S(1)} %bitcast.18), custom_call_target="tpu_custom_call" | custom-call | flops 419430400 | bytes 1048576 | tf_op jit(solution)/shard_map/pallas_call | solution.py:45
  70.3 1.8 %shard_map.64 = (f32[16,112,128]{2,1,0:T(8,128)S(1)}, bf16[16,112,128]{2,1,0:T(8,128)(2,1)S(1)}) custom-call(bf16[1152,1024]{1,0:T(8,128)(2,1)S(1)} %shard_map.63.refs_0_, bf16[1024,128]{1,0:T(8,128)(2,1)S(1)} %get-tuple-element.31.refs_1_), custom_call_target="tpu_custom_call" | custom-call | flops 905969664 | bytes 4194304 | tf_op jit(solution)/shard_map/pallas_call | solution.py:45
  72.1 0.2 collective-permute-start.6
  72.3 1.7 %collective-permute-done.6.received = bf16[16,112,128]{2,1,0:T(8,128)(2,1)S(1)} collective-permute-done((bf16[16,112,128]{2,1,0:T(8,128)(2,1)S(1)}, bf16[16,112,128]{2,1,0:T(8,128)(2,1)S(1)}, u32[]{:S(2)}, u32[]{:S(2)}) %collective-permute-start.6) | collective-permute-done | bytes 458784 | tf_op jit(solution)/shard_map/ppermute | solution.py:455
  74.0 0.9 shard_map.65
  74.9 5.9 %all-to-all-start.3 = ((bf16[16,112,128]{2,1,0:T(8,128)(2,1)}), bf16[16,112,128]{2,1,0:T(8,128)(2,1)S(1)}, u32[]{:S(2)}, u32[]{:S(2)}) async-start(bf16[16,112,128]{2,1,0:T(8,128)(2,1)} %shard_map.65), calls=%async_computation.3 | async-start | bytes 917504 | tf_op jit(solution)/shard_map/all_to_all | solution.py:371
  80.7 0.7 collective-permute-start.10
  81.4 2.5 %collective-permute-start.9 = (bf16[8,128,128]{2,1,0:T(8,128)(2,1)S(1)}, bf16[8,128,128]{2,1,0:T(8,128)(2,1)S(1)}, u32[]{:S(2)}, u32[]{:S(2)}) collective-permute-start(bf16[8,128,128]{2,1,0:T(8,128)(2,1)S(1)} %bitcast.20), channel_id=1, source_target_pairs={{0,8},{8,0},{16,24},{24,16},{32,40},{40,32},{48,56},{56,48},{64,72... | collective-permute-start | bytes 786440 | tf_op jit(solution)/shard_map/ppermute | solution.py:26
  83.9 0.0 collective-permute-start.7
  83.9 2.6 %collective-permute-start.8 = (bf16[1,128,128]{2,1,0:T(8,128)(2,1)S(1)}, bf16[1,128,128]{2,1,0:T(8,128)(2,1)S(1)}, u32[]{:S(2)}, u32[]{:S(2)}) collective-permute-start(bf16[1,128,128]{2,1,0:T(8,128)(2,1)S(1)} %get-tuple-element.39), channel_id=1, source_target_pairs={{1,2},{2,1},{3,4},{4,3},{5,6},{6,5},{9,10},{10,9},{11,12},{12,11},... | collective-permute-start | bytes 98312 | tf_op jit(solution)/shard_map/ppermute | solution.py:26
  86.5 0.0 collective-permute-done.7
  86.5 2.6 %collective-permute-done.8 = bf16[1,128,128]{2,1,0:T(8,128)(2,1)S(1)} collective-permute-done((bf16[1,128,128]{2,1,0:T(8,128)(2,1)S(1)}, bf16[1,128,128]{2,1,0:T(8,128)(2,1)S(1)}, u32[]{:S(2)}, u32[]{:S(2)}) %collective-permute-start.8) | collective-permute-done | bytes 32800 | tf_op jit(solution)/shard_map/ppermute | solution.py:26
  89.1 6.0 %all-to-all-done.3.refs_0_ = bf16[16,112,128]{2,1,0:T(8,128)(2,1)S(1)} async-done(((bf16[16,112,128]{2,1,0:T(8,128)(2,1)}), bf16[16,112,128]{2,1,0:T(8,128)(2,1)S(1)}, u32[]{:S(2)}, u32[]{:S(2)}) %all-to-all-start.3) | async-done | bytes 458784 | tf_op jit(solution)/shard_map/all_to_all | solution.py:371
  95.2 0.8 shard_map.66
  95.9 0.0 collective-permute-done.10.odd
  95.9 0.0 collective-permute-done.9.even
  95.9 3.4 %all-to-all-start.4 = ((bf16[8,112,128]{2,1,0:T(8,128)(2,1)}), bf16[8,112,128]{2,1,0:T(8,128)(2,1)S(1)}, u32[]{:S(2)}, u32[]{:S(2)}) async-start(bf16[8,112,128]{2,1,0:T(8,128)(2,1)} %shard_map.66), calls=%async_computation.4 | async-start | bytes 458752 | tf_op jit(solution)/shard_map/all_to_all | solution.py:371
  99.3 0.7 collective-permute-start.12
  100.0 4.7 %collective-permute-start.11 = (bf16[2,128,128]{2,1,0:T(8,128)(2,1)S(1)}, bf16[2,128,128]{2,1,0:T(8,128)(2,1)S(1)}, u32[]{:S(2)}, u32[]{:S(2)}) collective-permute-start(bf16[2,128,128]{2,1,0:T(8,128)(2,1)S(1)} %pad_maximum_fusion.own_edge), channel_id=1, source_target_pairs={{0,8},{8,0},{16,24},{24,16},{32,40},{40,32},{48,56},{56,48},{64,72... | collective-permute-start | bytes 196616 | tf_op jit(solution)/shard_map/ppermute | solution.py:26
  104.7 4.1 %all-to-all-done.4.refs_0_ = bf16[8,112,128]{2,1,0:T(8,128)(2,1)S(1)} async-done(((bf16[8,112,128]{2,1,0:T(8,128)(2,1)}), bf16[8,112,128]{2,1,0:T(8,128)(2,1)S(1)}, u32[]{:S(2)}, u32[]{:S(2)}) %all-to-all-start.4) | async-done | bytes 229408 | tf_op jit(solution)/shard_map/all_to_all | solution.py:371
  108.9 0.7 shard_map.67
  109.6 0.0 collective-permute-done.12.odd_edge
  109.6 0.0 collective-permute-done.11.even_edge
  109.6 3.5 %all-to-all-start.5 = ((f32[4,112,128]{2,1,0:T(8,128)}), f32[4,112,128]{2,1,0:T(8,128)S(1)}, u32[]{:S(2)}, u32[]{:S(2)}) async-start(f32[4,112,128]{2,1,0:T(8,128)} %shard_map.67), calls=%async_computation.5 | async-start | bytes 458752 | tf_op jit(solution)/shard_map/all_to_all | solution.py:371
  113.1 0.0 copy-done.1
  113.1 2.6 %shard_map.68 = bf16[1024,128]{1,0:T(8,128)(2,1)} custom-call(bf16[8,128,128]{2,1,0:T(8,128)(2,1)S(1)} %bitcast.21, bf16[2,128,128]{2,1,0:T(8,128)(2,1)S(1)} %pad_maximum_fusion.own_edge, bf16[8,128,128]{2,1,0:T(8,128)(2,1)S(1)} %collective-permute-done.9.even, bf16[2,128,128]{2,1,0:T(8,128)(2,1)S(1)} %collective-permute-done.11.even_edge, ...), custom_call_target="tpu_custom_call" | custom-call | flops 905969664 | bytes 3145728 | tf_op jit(solution)/shard_map/pallas_call | solution.py:45
  115.7 3.9 %all-to-all-done.5 = f32[4,112,128]{2,1,0:T(8,128)S(1)} async-done(((f32[4,112,128]{2,1,0:T(8,128)}), f32[4,112,128]{2,1,0:T(8,128)S(1)}, u32[]{:S(2)}, u32[]{:S(2)}) %all-to-all-start.5) | async-done | bytes 229408 | tf_op jit(solution)/shard_map/all_to_all | solution.py:371
  119.6 0.7 slice.4
  (6 shorter events, 0.1 us)
Async XLA Ops:
  1.4 7.8 %collective-permute-start = (bf16[1,128,128]{2,1,0:T(8,128)(2,1)S(1)}, bf16[1,128,128]{2,1,0:T(8,128)(2,1)S(1)}, u32[]{:S(2)}, u32[]{:S(2)}) collective-permute-start(bf16[1,128,128]{2,1,0:T(8,128)(2,1)S(1)} %get-tuple-element.48), channel_id=1, source_target_pairs={{0,1},{1,0},{2,3},{3,2},{4,5},{5,4},{6,7},{7,6},{8,9},{9,8},{10,11... | collective-permute-start | bytes 98312 | tf_op jit(solution)/shard_map/ppermute | solution.py:26
  1.4 21.7 %collective-permute-start.4 = (bf16[8,128,128]{2,1,0:T(8,128)(2,1)}, bf16[8,128,128]{2,1,0:T(8,128)(2,1)S(1)}, u32[]{:S(2)}, u32[]{:S(2)}) collective-permute-start(bf16[8,128,128]{2,1,0:T(8,128)(2,1)} %bitcast.14), channel_id=1, source_target_pairs={{8,16},{16,8},{24,32},{32,24},{40,48},{48,40},{56,64},{64,56},{72,... | collective-permute-start | bytes 786440 | tf_op jit(solution)/shard_map/ppermute | solution.py:26
  2.1 21.1 %collective-permute-start.2 = (bf16[8,128,128]{2,1,0:T(8,128)(2,1)}, bf16[8,128,128]{2,1,0:T(8,128)(2,1)S(1)}, u32[]{:S(2)}, u32[]{:S(2)}) collective-permute-start(bf16[8,128,128]{2,1,0:T(8,128)(2,1)} %bitcast.15), channel_id=1, source_target_pairs={{0,8},{8,0},{16,24},{24,16},{32,40},{40,32},{48,56},{56,48},{64,72... | collective-permute-start | bytes 786440 | tf_op jit(solution)/shard_map/ppermute | solution.py:26
  7.3 5.2 %collective-permute-start.1 = (bf16[1,128,128]{2,1,0:T(8,128)(2,1)S(1)}, bf16[1,128,128]{2,1,0:T(8,128)(2,1)S(1)}, u32[]{:S(2)}, u32[]{:S(2)}) collective-permute-start(bf16[1,128,128]{2,1,0:T(8,128)(2,1)S(1)} %get-tuple-element.47), channel_id=1, source_target_pairs={{1,2},{2,1},{3,4},{4,3},{5,6},{6,5},{9,10},{10,9},{11,12},{12,11},... | collective-permute-start | bytes 98312 | tf_op jit(solution)/shard_map/ppermute | solution.py:26
  12.5 10.6 %collective-permute-start.5 = (bf16[2,128,128]{2,1,0:T(8,128)(2,1)S(1)}, bf16[2,128,128]{2,1,0:T(8,128)(2,1)S(1)}, u32[]{:S(2)}, u32[]{:S(2)}) collective-permute-start(bf16[2,128,128]{2,1,0:T(8,128)(2,1)S(1)} %constant_dynamic-update-slice_fusion.own_edge), channel_id=1, source_target_pairs={{8,16},{16,8},{24,32},{32,24},{40,48},{48,40},{56,64},{64,56},{72,... | collective-permute-start | bytes 196616 | tf_op jit(solution)/shard_map/ppermute | solution.py:26
  13.2 10.0 %collective-permute-start.3 = (bf16[2,128,128]{2,1,0:T(8,128)(2,1)S(1)}, bf16[2,128,128]{2,1,0:T(8,128)(2,1)S(1)}, u32[]{:S(2)}, u32[]{:S(2)}) collective-permute-start(bf16[2,128,128]{2,1,0:T(8,128)(2,1)S(1)} %constant_dynamic-update-slice_fusion.own_edge), channel_id=1, source_target_pairs={{0,8},{8,0},{16,24},{24,16},{32,40},{40,32},{48,56},{56,48},{64,72... | collective-permute-start | bytes 196616 | tf_op jit(solution)/shard_map/ppermute | solution.py:26
  19.5 1.2 copy-start
  20.7 0.9 copy-start.2
  21.7 0.9 copy-start.3
  23.1 27.1 %copy-start.5 = (bf16[2,128,128]{2,1,0:T(8,128)(2,1)}, bf16[2,128,128]{2,1,0:T(8,128)(2,1)S(1)}, u32[]{:S(2)}) copy-start(bf16[2,128,128]{2,1,0:T(8,128)(2,1)S(1)} %collective-permute-done.3.even_edge) | copy-start | bytes 196612
  25.4 24.9 %copy-start.7 = (bf16[1024,128]{1,0:T(8,128)(2,1)}, bf16[1024,128]{1,0:T(8,128)(2,1)S(1)}, u32[]{:S(2)}) copy-start(bf16[1024,128]{1,0:T(8,128)(2,1)S(1)} %get-tuple-element.29.refs_1_) | copy-start | bytes 786436
  25.4 37.9 %copy-start.4 = (bf16[1,8,128,128]{3,2,1,0:T(8,128)(2,1)S(1)}, bf16[1,8,128,128]{3,2,1,0:T(8,128)(2,1)}, u32[]{:S(2)}) copy-start(bf16[1,8,128,128]{3,2,1,0:T(8,128)(2,1)} %param.5) | copy-start | bytes 786436
  50.9 12.3 %all-to-all-start.2 = ((f32[32,5,128]{2,1,0:T(8,128)}), f32[32,5,128]{2,1,0:T(8,128)}, u32[]{:S(2)}, u32[]{:S(2)}) async-start(f32[32,5,128]{2,1,0:T(8,128)} %shard_map.61), calls=%async_computation.2 | async-start | bytes 262144 | tf_op jit(solution)/shard_map/all_to_all | solution.py:371
  57.6 0.8 copy-start.6
  63.3 1.0 copy-start.8
  72.1 1.9 %collective-permute-start.6 = (bf16[16,112,128]{2,1,0:T(8,128)(2,1)S(1)}, bf16[16,112,128]{2,1,0:T(8,128)(2,1)S(1)}, u32[]{:S(2)}, u32[]{:S(2)}) collective-permute-start(bf16[16,112,128]{2,1,0:T(8,128)(2,1)S(1)} %get-tuple-element.35), channel_id=1, source_target_pairs={{0,1},{1,0},{2,3},{3,2},{4,5},{5,4},{6,7},{7,6},{8,9},{9,8},{10,11... | collective-permute-start | bytes 1376264 | tf_op jit(solution)/shard_map/ppermute | solution.py:455
  74.0 39.1 %copy-start.1 = (bf16[3,3,3,128,128]{4,3,2,1,0:T(8,128)(2,1)S(1)}, bf16[3,3,3,128,128]{4,3,2,1,0:T(8,128)(2,1)}, u32[]{:S(2)}) copy-start(bf16[3,3,3,128,128]{4,3,2,1,0:T(8,128)(2,1)} %param.4) | copy-start | bytes 2654212
  74.9 20.3 %all-to-all-start.3 = ((bf16[16,112,128]{2,1,0:T(8,128)(2,1)}), bf16[16,112,128]{2,1,0:T(8,128)(2,1)S(1)}, u32[]{:S(2)}, u32[]{:S(2)}) async-start(bf16[16,112,128]{2,1,0:T(8,128)(2,1)} %shard_map.65), calls=%async_computation.3 | async-start | bytes 917504 | tf_op jit(solution)/shard_map/all_to_all | solution.py:371
  80.7 15.2 %collective-permute-start.10 = (bf16[8,128,128]{2,1,0:T(8,128)(2,1)S(1)}, bf16[8,128,128]{2,1,0:T(8,128)(2,1)S(1)}, u32[]{:S(2)}, u32[]{:S(2)}) collective-permute-start(bf16[8,128,128]{2,1,0:T(8,128)(2,1)S(1)} %bitcast.19), channel_id=1, source_target_pairs={{8,16},{16,8},{24,32},{32,24},{40,48},{48,40},{56,64},{64,56},{72,... | collective-permute-start | bytes 786440 | tf_op jit(solution)/shard_map/ppermute | solution.py:26
  81.4 14.5 %collective-permute-start.9 = (bf16[8,128,128]{2,1,0:T(8,128)(2,1)S(1)}, bf16[8,128,128]{2,1,0:T(8,128)(2,1)S(1)}, u32[]{:S(2)}, u32[]{:S(2)}) collective-permute-start(bf16[8,128,128]{2,1,0:T(8,128)(2,1)S(1)} %bitcast.20), channel_id=1, source_target_pairs={{0,8},{8,0},{16,24},{24,16},{32,40},{40,32},{48,56},{56,48},{64,72... | collective-permute-start | bytes 786440 | tf_op jit(solution)/shard_map/ppermute | solution.py:26
  83.9 2.6 %collective-permute-start.7 = (bf16[1,128,128]{2,1,0:T(8,128)(2,1)S(1)}, bf16[1,128,128]{2,1,0:T(8,128)(2,1)S(1)}, u32[]{:S(2)}, u32[]{:S(2)}) collective-permute-start(bf16[1,128,128]{2,1,0:T(8,128)(2,1)S(1)} %get-tuple-element.38), channel_id=1, source_target_pairs={{0,1},{1,0},{2,3},{3,2},{4,5},{5,4},{6,7},{7,6},{8,9},{9,8},{10,11... | collective-permute-start | bytes 98312 | tf_op jit(solution)/shard_map/ppermute | solution.py:26
  83.9 5.2 %collective-permute-start.8 = (bf16[1,128,128]{2,1,0:T(8,128)(2,1)S(1)}, bf16[1,128,128]{2,1,0:T(8,128)(2,1)S(1)}, u32[]{:S(2)}, u32[]{:S(2)}) collective-permute-start(bf16[1,128,128]{2,1,0:T(8,128)(2,1)S(1)} %get-tuple-element.39), channel_id=1, source_target_pairs={{1,2},{2,1},{3,4},{4,3},{5,6},{6,5},{9,10},{10,9},{11,12},{12,11},... | collective-permute-start | bytes 98312 | tf_op jit(solution)/shard_map/ppermute | solution.py:26
  95.9 12.9 %all-to-all-start.4 = ((bf16[8,112,128]{2,1,0:T(8,128)(2,1)}), bf16[8,112,128]{2,1,0:T(8,128)(2,1)S(1)}, u32[]{:S(2)}, u32[]{:S(2)}) async-start(bf16[8,112,128]{2,1,0:T(8,128)(2,1)} %shard_map.66), calls=%async_computation.4 | async-start | bytes 458752 | tf_op jit(solution)/shard_map/all_to_all | solution.py:371
  99.3 10.3 %collective-permute-start.12 = (bf16[2,128,128]{2,1,0:T(8,128)(2,1)S(1)}, bf16[2,128,128]{2,1,0:T(8,128)(2,1)S(1)}, u32[]{:S(2)}, u32[]{:S(2)}) collective-permute-start(bf16[2,128,128]{2,1,0:T(8,128)(2,1)S(1)} %pad_maximum_fusion.own_edge), channel_id=1, source_target_pairs={{8,16},{16,8},{24,32},{32,24},{40,48},{48,40},{56,64},{64,56},{72,... | collective-permute-start | bytes 196616 | tf_op jit(solution)/shard_map/ppermute | solution.py:26
  100.0 9.6 %collective-permute-start.11 = (bf16[2,128,128]{2,1,0:T(8,128)(2,1)S(1)}, bf16[2,128,128]{2,1,0:T(8,128)(2,1)S(1)}, u32[]{:S(2)}, u32[]{:S(2)}) collective-permute-start(bf16[2,128,128]{2,1,0:T(8,128)(2,1)S(1)} %pad_maximum_fusion.own_edge), channel_id=1, source_target_pairs={{0,8},{8,0},{16,24},{24,16},{32,40},{40,32},{48,56},{56,48},{64,72... | collective-permute-start | bytes 196616 | tf_op jit(solution)/shard_map/ppermute | solution.py:26
  109.6 10.0 %all-to-all-start.5 = ((f32[4,112,128]{2,1,0:T(8,128)}), f32[4,112,128]{2,1,0:T(8,128)S(1)}, u32[]{:S(2)}, u32[]{:S(2)}) async-start(f32[4,112,128]{2,1,0:T(8,128)} %shard_map.67), calls=%async_computation.5 | async-start | bytes 458752 | tf_op jit(solution)/shard_map/all_to_all | solution.py:371

commit v5 on v4

--- a/solution.py
+++ b/solution.py
@@ -17,6 +17,7 @@
 GY = ("x", "c")
 SPREAD = ("y", "x", "c")
 VMEM_BYTES = 20 * 1024 * 1024
+JOIN_FLOPS = 2 * 2**30
 
 
 def swapped(block, axes, count, first):
@@ -26,11 +27,16 @@
     return lax.ppermute(block, axes, pairs)
 
 
+def join_kernel(even, odd, rows_out):
+    rows_out[0:1] = even[...]
+    rows_out[1:2] = odd[...]
+
+
 def row_swaps(first_send, second_send):
     ny = lax.axis_size(GY)
-    return jnp.concatenate(
-        [swapped(first_send, GY, ny, 0), swapped(second_send, GY, ny, 1)], axis=0
-    )
+    even, odd = swapped(first_send, GY, ny, 0), swapped(second_send, GY, ny, 1)
+    joined = jax.ShapeDtypeStruct((2,) + even.shape[1:], BF16)
+    return call(join_kernel, joined, [], JOIN_FLOPS, 2**18, even, odd)
 
 
 def plane_swaps(block):
@@ -184,14 +190,11 @@
     return total + jnp.dot(values, high, preferred_element_type=F32)
 
 
-def whiten_kernel(
-    voxels, columns, sheet, hidden, target, whitened_out, grad_out, first_out, second_out,
-    mats, hidden_here, target_here, sems,
+def grad_kernel(
+    voxels, columns, share, sheet, hidden, target, turned,
+    grad_out, first_out, second_out, keep_out, send_out, whitener_out, offset_out,
+    mats, wide, terms,
 ):
-    hidden_move = pltpu.make_async_copy(hidden, hidden_here, sems.at[0])
-    target_move = pltpu.make_async_copy(target, target_here, sems.at[1])
-    hidden_move.start()
-    target_move.start()
     spread, depth, channels = sheet.shape
     each = depth - 1
     for j in range(spread):
@@ -233,10 +236,10 @@
     for sweep in range(1, NEWTON):
         first = exact(iterate, iterate, scaled, change, direction)
         squared, once = column(first, 0), column(first, 1)
-        turned = exact(change, iterate, scaled)
+        crossed = exact(change, iterate, scaled)
         steep = exact(slope, scaled)
-        second_level = exact(squared, once, column(first, 3) + column(turned, 1), steep, iterate)
-        moved = column(second_level, 1) + exact(column(first, 2) + column(turned, 0), once)
+        second_level = exact(squared, once, column(first, 3) + column(crossed, 1), steep, iterate)
+        moved = column(second_level, 1) + exact(column(first, 2) + column(crossed, 0), once)
         change = 1.5 * change - 0.5 * moved
         slope = 1.5 * slope - 0.5 * (3.0 * column(second_level, 2) + column(second_level, 3))
         iterate = 1.5 * iterate - 0.5 * column(second_level, 0)
@@ -251,15 +254,13 @@
     symmetric = (sigma_grad + sigma_grad.T) / voxels
     backward = (exact(whitener_t, whitener) + symmetric).T
 
-    both = jnp.concatenate([whitener_t, backward], axis=1)
-    offset = exact(jnp.broadcast_to(mean, (8, channels)), whitener_t, backward)[0:1]
-    target_offset = exact(jnp.broadcast_to(target_sum / voxels, (8, channels)), whitener)[0:1]
-    hidden_move.wait()
-    target_move.wait()
-    mixed = through(hidden_here[...], both) - offset
-    whitened_out[...] = mixed[:, :channels].astype(BF16)
-    pulled = through(target_here[...], whitener) - target_offset
-    grad = (mixed[:, channels:] - pulled).astype(BF16)
+    offset = exact(jnp.broadcast_to(mean, (8, channels)), whitener_t, backward)
+    target_offset = exact(jnp.broadcast_to(target_sum / voxels, (8, channels)), whitener)
+    whitener_out[...] = whitener_t
+    offset_out[...] = offset[:, :channels]
+    grad = through(hidden[...], backward) - through(target[...], whitener)
+    wide_grad = grad - (offset[:1, channels:] - target_offset[:1])
+    grad = wide_grad.astype(BF16)
     grad_out[...] = grad
     odd_row = lax.axis_index("c")
 
@@ -273,8 +274,19 @@
         first_out[0] = grad[:columns]
         second_out[0] = grad[-columns:]
 
-
-def turn_kernel(own, own_edge, even, even_edge, odd, odd_edge, turned_out):
+    weight_terms(columns, share, turned, grad, keep_out, send_out, wide, terms)
+
+
+def white_kernel(hidden, whitener, offset, whitened_out):
+    whitened_out[...] = (through(hidden[...], whitener[...]) - offset[0:1]).astype(BF16)
+
+
+def turn_kernel(
+    own, own_edge, even, even_edge, odd, odd_edge, hidden, target,
+    turned_out, hidden_out, target_out,
+):
+    hidden_out[...] = hidden[...]
+    target_out[...] = target[...]
     rows, columns, channels = own.shape
     odd_row = lax.axis_index("c")
     odd_plane = lax.rem(lax.axis_index("z"), 2)
@@ -307,11 +319,11 @@
             turn(2, *above)
 
 
-def weight_kernel(columns, share, turned, grad, keep_out, send_out, wide, terms):
-    count, channels = grad.shape
-    value = grad[...].astype(F32)
+def weight_terms(columns, share, turned, grad, keep_out, send_out, wide, terms):
+    _, channels = grad.shape
+    value = grad.astype(F32)
     wide[:, :channels] = moved_columns(value, -1, columns).astype(BF16)
-    wide[:, channels : 2 * channels] = grad[...]
+    wide[:, channels : 2 * channels] = grad
     wide[:, 2 * channels :] = moved_columns(value, 1, columns).astype(BF16)
     pairs = channels // share // 2
     taps_each = keep_out.shape[1] // share
@@ -419,55 +431,54 @@
         [wide],
         flops, 3 * 2**20, *planes, kernel_wide, target_near,
     )
-    turned = call(
+    flat = jax.ShapeDtypeStruct((count, channels), BF16)
+    turned, hidden, target_near = call(
         turn_kernel,
-        jax.ShapeDtypeStruct((9 * channels, count), BF16),
-        [], 0, 3 * 2**20, *planes,
+        [jax.ShapeDtypeStruct((9 * channels, count), BF16), flat, flat],
+        [], 0, 3 * 2**20, *planes, hidden, target_flat,
     )
 
     mine = total_copies(exchange(sheet, SPREAD), levels, F32)
     mine = total_copies(exchange(mine, ("z",)), spread, F32)
     sheet = exchange(mine, SPREAD)
     line = jax.ShapeDtypeStruct((1, columns, channels), BF16)
-    whitened, grad_hidden, first_send, second_send = call(
-        lambda *refs: whiten_kernel(voxels, columns, *refs),
-        [jax.ShapeDtypeStruct((count, channels), BF16)] * 2 + [line] * 2,
+    groups = spread // 2
+    shape = (groups, taps_each * share, channels)
+    grad_hidden, first_send, second_send, keep, send, whitener, offset = call(
+        lambda *refs: grad_kernel(voxels, columns, share, *refs),
+        [
+            flat, line, line,
+            jax.ShapeDtypeStruct(shape, F32),
+            jax.ShapeDtypeStruct(shape, BF16),
+            jax.ShapeDtypeStruct((channels, channels), F32),
+            jax.ShapeDtypeStruct((8, channels), F32),
+        ],
         [
             pltpu.VMEM((2 * G, channels), F32),
-            pltpu.VMEM((count, channels), BF16),
-            pltpu.VMEM((count, channels), BF16),
-            pltpu.SemaphoreType.DMA((2,)),
-        ],
-        100 * 2 * channels**3, 2**20, sheet, hidden, target_flat, far=(1, 2),
-    )
-
-    groups = spread // 2
-    shape = (groups, taps_each * share, channels)
-    keep, send = call(
-        lambda *refs: weight_kernel(columns, share, *refs),
-        [jax.ShapeDtypeStruct(shape, F32), jax.ShapeDtypeStruct(shape, BF16)],
-        [
             pltpu.VMEM((count, 3 * channels), BF16),
             pltpu.VMEM((9 * channels, 3 * channels), F32),
         ],
-        flops, 4 * 2**20, turned, grad_hidden,
+        flops, 2**20, sheet, hidden, target_near, turned,
     )
     received = lax.ppermute(send, ("c",), [(0, 1), (1, 0)])
     parts = call(
         pair_kernel, jax.ShapeDtypeStruct(shape, BF16), [], keep.size, 2**21, keep, received
     )
-    block, first_send, second_send, parts = lax.optimization_barrier(
-        (grad_hidden.reshape(rows, columns, channels), first_send, second_send, parts)
-    )
+    block, first_send, second_send, whitener, parts = lax.optimization_barrier(
+        (grad_hidden.reshape(rows, columns, channels), first_send, second_send, whitener, parts)
+    )
+    whitened = call(white_kernel, flat, [], flops, 2**20, hidden, whitener, offset)
     edges = row_swaps(first_send, second_send)
     even, odd = plane_swaps(block)
     part = total_copies(exchange(parts, ("y", "x")), levels, BF16)
-    part, edges, even, odd = lax.optimization_barrier((part, edges, even, odd))
+    part, edges, even, odd, whitened = lax.optimization_barrier(
+        (part, edges, even, odd, whitened)
+    )
     even_edges, odd_edges = plane_swaps(edges)
-    part = total_copies(exchange(part, ("z",)), rows_y, F32, 1.0 / math.sqrt(voxels))
+    part = total_copies(exchange(part, ("z",)), rows_y, BF16, 1.0 / math.sqrt(voxels))
     part, even_edges, odd_edges = lax.optimization_barrier((part, even_edges, odd_edges))
     whole = exchange(part, ("y",))
-    weight_grad = whole.reshape(rows_y * taps_each, share, channels)[:27]
+    weight_grad = whole.reshape(rows_y * taps_each, share, channels)[:27].astype(F32)
     weight_grad = weight_grad.reshape(3, 3, 3, share, channels)
 
     planes = [block, edges, even, even_edges, odd, odd_edges]

time: 122 us -> 118 us (0.967)
  waiting for transfers between devices: 26.1 us -> 22.3 us
  local copies, waits for them, and re-layouts: 6.37 us -> 3.89 us
  blocking collectives: 24.8 us -> 27.1 us
    ppermute x12, waiting for transfers between devices: 5.89 us -> 3.31 us  [swapped(): return lax.ppermute(block, axes, pairs)]
    all_to_all x2, blocking collectives: 24.8 us -> 27.1 us  [exchange(): return lax.all_to_all(parts, axes, 0, 0, tiled=True)]
    unnamed x19 -> x10, local copies, waits for them, and re-layouts: 4.88 us -> 3.09 us
    ppermute x12, starting transfers between devices: 25.9 us -> 27.4 us  [swapped(): return lax.ppermute(block, axes, pairs)]
    all_to_all x4, waiting for transfers between devices: 18.5 us -> 17.2 us  [exchange(): return lax.all_to_all(parts, axes, 0, 0, tiled=True)]
    pallas_call x11 -> x13, Pallas kernels: 16.7 us -> 15.7 us  [call(): pl.pallas_call(kernel, out_shape=out_shape, in_specs=[hbm if i in far els...]
  transfers between devices with their start and end apart: 17 -> 17, of which waited for: 7 -> 7; matrix products, arithmetic and copies ran while one was open for 0% -> 0% of each run, Pallas kernels for 4% -> 5%
where the time goes in v5:
time: 118 us; the launch traced here: 117 us
  starting transfers between devices  46.3 us (39%)
  blocking collectives  27.1 us (23%)
  waiting for transfers between devices  22.3 us (19%)
  Pallas kernels  15.7 us (13%)
  local copies, waits for them, and re-layouts  3.89 us (3%)
    ppermute x12, starting transfers between devices, swapped(): return lax.ppermute(block, axes, pairs)  27.4 us
    all_to_all x2, blocking collectives, exchange(): return lax.all_to_all(parts, axes, 0, 0, tiled=True)  27.1 us
    all_to_all x4, starting transfers between devices, exchange(): return lax.all_to_all(parts, axes, 0, 0, tiled=True)  18.7 us
    all_to_all x4, waiting for transfers between devices, exchange(): return lax.all_to_all(parts, axes, 0, 0, tiled=True)  17.2 us
    pallas_call x13, Pallas kernels, call(): pl.pallas_call(kernel, out_shape=out_shape, in_specs=[hbm if i in far els...  15.7 us
    ppermute x12, waiting for transfers between devices, swapped(): return lax.ppermute(block, axes, pairs)  3.31 us
    unnamed x10, local copies, waits for them, and re-layouts  3.09 us
  transfers between devices with their start and end apart: 17, of which 7 were waited for; matrix products, arithmetic and copies ran while one was open for 0% of the time, Pallas kernels for 5%

profile of v5, /device:TPU:4, one launch (start us, length us, event | category | flops | bytes accessed | tf_op | source)
XLA Modules:
  0.0 116.8 jit_solution(3484347190198598437)
XLA Ops:
  0.6 0.8 dynamic-slice_bitcast_fusion
  1.4 1.9 %collective-permute-start.1 = (bf16[1,128,128]{2,1,0:T(8,128)(2,1)S(1)}, bf16[1,128,128]{2,1,0:T(8,128)(2,1)S(1)}, u32[]{:S(2)}, u32[]{:S(2)}) collective-permute-start(bf16[1,128,128]{2,1,0:T(8,128)(2,1)S(1)} %get-tuple-element.59), channel_id=1, source_target_pairs={{1,2},{2,1},{3,4},{4,3},{5,6},{6,5},{9,10},{10,9},{11,12},{12,11},... | collective-permute-start | bytes 98312 | tf_op jit(solution)/shard_map/ppermute | solution.py:27
  3.3 1.4 %collective-permute-start = (bf16[1,128,128]{2,1,0:T(8,128)(2,1)S(1)}, bf16[1,128,128]{2,1,0:T(8,128)(2,1)S(1)}, u32[]{:S(2)}, u32[]{:S(2)}) collective-permute-start(bf16[1,128,128]{2,1,0:T(8,128)(2,1)S(1)} %get-tuple-element.60), channel_id=1, source_target_pairs={{0,1},{1,0},{2,3},{3,2},{4,5},{5,4},{6,7},{7,6},{8,9},{9,8},{10,11... | collective-permute-start | bytes 98312 | tf_op jit(solution)/shard_map/ppermute | solution.py:27
  4.7 0.0 copy-start
  4.7 0.0 copy-start.1
  4.7 0.0 copy-start.2
  4.7 0.8 collective-permute-start.4
  5.5 5.2 %collective-permute-start.2 = (bf16[8,128,128]{2,1,0:T(8,128)(2,1)}, bf16[8,128,128]{2,1,0:T(8,128)(2,1)S(1)}, u32[]{:S(2)}, u32[]{:S(2)}) collective-permute-start(bf16[8,128,128]{2,1,0:T(8,128)(2,1)} %bitcast.18), channel_id=1, source_target_pairs={{0,8},{8,0},{16,24},{24,16},{32,40},{40,32},{48,56},{56,48},{64,72... | collective-permute-start | bytes 786440 | tf_op jit(solution)/shard_map/ppermute | solution.py:27
  10.7 0.0 collective-permute-done.1.odd
  10.7 0.0 collective-permute-done.even
  10.7 0.7 collective-permute-start.5
  11.4 6.4 %collective-permute-start.3 = (bf16[2,128,128]{2,1,0:T(8,128)(2,1)S(1)}, bf16[2,128,128]{2,1,0:T(8,128)(2,1)S(1)}, u32[]{:S(2)}, u32[]{:S(2)}) collective-permute-start(bf16[2,128,128]{2,1,0:T(8,128)(2,1)S(1)} %shard_map.59.own_edge), channel_id=1, source_target_pairs={{0,8},{8,0},{16,24},{24,16},{32,40},{40,32},{48,56},{56,48},{64,72... | collective-permute-start | bytes 196616 | tf_op jit(solution)/shard_map/ppermute | solution.py:27
  17.8 0.0 copy-done
  17.8 0.0 copy-done.1
  17.8 0.0 copy-done.2
  17.8 0.5 shard_map.58
  18.3 0.0 collective-permute-done.5.odd_edge
  18.3 1.7 %collective-permute-done.3.even_edge = bf16[2,128,128]{2,1,0:T(8,128)(2,1)S(1)} collective-permute-done((bf16[2,128,128]{2,1,0:T(8,128)(2,1)S(1)}, bf16[2,128,128]{2,1,0:T(8,128)(2,1)S(1)}, u32[]{:S(2)}, u32[]{:S(2)}) %collective-permute-start.3) | collective-permute-done | bytes 65568 | tf_op jit(solution)/shard_map/ppermute | solution.py:27
  20.0 0.0 collective-permute-done.4.odd
  20.0 0.0 collective-permute-done.2.even
  20.0 2.2 %shard_map.60 = (bf16[1024,128]{1,0:T(8,128)(2,1)S(1)}, f32[32,5,128]{2,1,0:T(8,128)S(1)}) custom-call(bf16[8,128,128]{2,1,0:T(8,128)(2,1)S(1)} %get-tuple-element.31.own, bf16[2,128,128]{2,1,0:T(8,128)(2,1)S(1)} %shard_map.59.own_edge, bf16[8,128,128]{2,1,0:T(8,128)(2,1)S(1)} %collective-permute-done.2.even, ...), custom_call_target="tpu_custom_call" | custom-call | flops 905969664 | bytes 3145728 | tf_op jit(solution)/shard_map/pallas_call | solution.py:51
  22.2 15.3 %all_to_all.30.refs_0_ = f32[32,5,128]{2,1,0:T(8,128)S(1)} all-to-all(f32[32,5,128]{2,1,0:T(8,128)S(1)} %get-tuple-element.34), channel_id=1, replica_groups=mesh['y'=4,'z'=8,'x'=4,'c'=2] {'y','x','c'}, dimensions={0} | all-to-all | bytes 163840 | tf_op jit(solution)/shard_map/all_to_all | solution.py:383
  37.5 11.8 %all_to_all.31.refs_0_ = f32[8,5,128]{2,1,0:T(8,128)S(1)} all-to-all(f32[8,5,128]{2,1,0:T(8,128)S(1)} %shard_map.61), channel_id=1, replica_groups=mesh['y'=4,'z'=8,'x'=4,'c'=2] {'z'}, dimensions={0} | all-to-all | bytes 40960 | tf_op jit(solution)/shard_map/all_to_all | solution.py:383
  49.3 0.7 shard_map.62
  50.0 6.0 %all-to-all-start.2 = ((f32[32,5,128]{2,1,0:T(8,128)}), f32[32,5,128]{2,1,0:T(8,128)S(1)}, u32[]{:S(2)}, u32[]{:S(2)}) async-start(f32[32,5,128]{2,1,0:T(8,128)} %shard_map.62), calls=%async_computation.2 | async-start | bytes 262144 | tf_op jit(solution)/shard_map/all_to_all | solution.py:383
  56.0 0.5 shard_map.63
  56.5 0.0 copy-start.3
  56.5 1.4 %copy-done.3 = bf16[1152,1024]{1,0:T(8,128)(2,1)} copy-done((bf16[1152,1024]{1,0:T(8,128)(2,1)}, bf16[1152,1024]{1,0:T(8,128)(2,1)S(1)}, u32[]{:S(2)}) %copy-start.3) | copy-done | bytes 2359320
  57.9 3.8 %all-to-all-done.2.refs_0_ = f32[32,5,128]{2,1,0:T(8,128)S(1)} async-done(((f32[32,5,128]{2,1,0:T(8,128)}), f32[32,5,128]{2,1,0:T(8,128)S(1)}, u32[]{:S(2)}, u32[]{:S(2)}) %all-to-all-start.2) | async-done | bytes 81952 | tf_op jit(solution)/shard_map/all_to_all | solution.py:383
  61.7 0.0 copy-start.4
  61.7 1.7 %copy-done.4 = bf16[1152,1024]{1,0:T(8,128)(2,1)S(1)} copy-done((bf16[1152,1024]{1,0:T(8,128)(2,1)S(1)}, bf16[1152,1024]{1,0:T(8,128)(2,1)}, u32[]{:S(2)}) %copy-start.4) | copy-done | bytes 2359320
  63.3 5.9 %shard_map.64 = (bf16[1024,128]{1,0:T(8,128)(2,1)S(1)}, bf16[1,128,128]{2,1,0:T(8,128)(2,1)S(1)}, bf16[1,128,128]{2,1,0:T(8,128)(2,1)S(1)}, f32[16,112,128]{2,1,...) custom-call(f32[32,5,128]{2,1,0:T(8,128)S(1)} %all-to-all-done.2.refs_0_, ...), custom_call_target="tpu_custom_call" | custom-call | flops 905969664 | bytes 1048576 | tf_op jit(solution)/shard_map/pallas_call | solution.py:51
  69.2 0.2 collective-permute-start.6
  69.4 1.7 %collective-permute-done.6.received = bf16[16,112,128]{2,1,0:T(8,128)(2,1)S(1)} collective-permute-done((bf16[16,112,128]{2,1,0:T(8,128)(2,1)S(1)}, bf16[16,112,128]{2,1,0:T(8,128)(2,1)S(1)}, u32[]{:S(2)}, u32[]{:S(2)}) %collective-permute-start.6) | collective-permute-done | bytes 458784 | tf_op jit(solution)/shard_map/ppermute | solution.py:463
  71.1 0.8 shard_map.65
  72.0 5.8 %all-to-all-start.3 = ((bf16[16,112,128]{2,1,0:T(8,128)(2,1)}), bf16[16,112,128]{2,1,0:T(8,128)(2,1)S(1)}, u32[]{:S(2)}, u32[]{:S(2)}) async-start(bf16[16,112,128]{2,1,0:T(8,128)(2,1)} %shard_map.65), calls=%async_computation.3 | async-start | bytes 917504 | tf_op jit(solution)/shard_map/all_to_all | solution.py:383
  77.8 0.7 collective-permute-start.10
  78.5 2.5 %collective-permute-start.9 = (bf16[8,128,128]{2,1,0:T(8,128)(2,1)S(1)}, bf16[8,128,128]{2,1,0:T(8,128)(2,1)S(1)}, u32[]{:S(2)}, u32[]{:S(2)}) collective-permute-start(bf16[8,128,128]{2,1,0:T(8,128)(2,1)S(1)} %bitcast.21), channel_id=1, source_target_pairs={{0,8},{8,0},{16,24},{24,16},{32,40},{40,32},{48,56},{56,48},{64,72... | collective-permute-start | bytes 786440 | tf_op jit(solution)/shard_map/ppermute | solution.py:27
  81.0 0.0 collective-permute-start.7
  81.0 2.6 %collective-permute-start.8 = (bf16[1,128,128]{2,1,0:T(8,128)(2,1)S(1)}, bf16[1,128,128]{2,1,0:T(8,128)(2,1)S(1)}, u32[]{:S(2)}, u32[]{:S(2)}) collective-permute-start(bf16[1,128,128]{2,1,0:T(8,128)(2,1)S(1)} %get-tuple-element.47), channel_id=1, source_target_pairs={{1,2},{2,1},{3,4},{4,3},{5,6},{6,5},{9,10},{10,9},{11,12},{12,11},... | collective-permute-start | bytes 98312 | tf_op jit(solution)/shard_map/ppermute | solution.py:27
  83.6 1.1 shard_map.68
  84.6 0.0 collective-permute-done.7.even
  84.6 1.6 %collective-permute-done.8.odd = bf16[1,128,128]{2,1,0:T(8,128)(2,1)S(1)} collective-permute-done((bf16[1,128,128]{2,1,0:T(8,128)(2,1)S(1)}, bf16[1,128,128]{2,1,0:T(8,128)(2,1)S(1)}, u32[]{:S(2)}, u32[]{:S(2)}) %collective-permute-start.8) | collective-permute-done | bytes 32800 | tf_op jit(solution)/shard_map/ppermute | solution.py:27
  86.2 6.1 %all-to-all-done.3.refs_0_ = bf16[16,112,128]{2,1,0:T(8,128)(2,1)S(1)} async-done(((bf16[16,112,128]{2,1,0:T(8,128)(2,1)}), bf16[16,112,128]{2,1,0:T(8,128)(2,1)S(1)}, u32[]{:S(2)}, u32[]{:S(2)}) %all-to-all-start.3) | async-done | bytes 458784 | tf_op jit(solution)/shard_map/all_to_all | solution.py:383
  92.3 0.8 shard_map.66
  93.0 0.0 collective-permute-done.10.odd
  93.0 0.0 collective-permute-done.9.even
  93.0 3.4 %all-to-all-start.4 = ((bf16[8,112,128]{2,1,0:T(8,128)(2,1)}), bf16[8,112,128]{2,1,0:T(8,128)(2,1)S(1)}, u32[]{:S(2)}, u32[]{:S(2)}) async-start(bf16[8,112,128]{2,1,0:T(8,128)(2,1)} %shard_map.66), calls=%async_computation.4 | async-start | bytes 458752 | tf_op jit(solution)/shard_map/all_to_all | solution.py:383
  96.5 0.7 collective-permute-start.12
  97.1 4.7 %collective-permute-start.11 = (bf16[2,128,128]{2,1,0:T(8,128)(2,1)S(1)}, bf16[2,128,128]{2,1,0:T(8,128)(2,1)S(1)}, u32[]{:S(2)}, u32[]{:S(2)}) collective-permute-start(bf16[2,128,128]{2,1,0:T(8,128)(2,1)S(1)} %shard_map.67.own_edge), channel_id=1, source_target_pairs={{0,8},{8,0},{16,24},{24,16},{32,40},{40,32},{48,56},{56,48},{64,72... | collective-permute-start | bytes 196616 | tf_op jit(solution)/shard_map/ppermute | solution.py:27
  101.8 4.1 %all-to-all-done.4.refs_0_ = bf16[8,112,128]{2,1,0:T(8,128)(2,1)S(1)} async-done(((bf16[8,112,128]{2,1,0:T(8,128)(2,1)}), bf16[8,112,128]{2,1,0:T(8,128)(2,1)S(1)}, u32[]{:S(2)}, u32[]{:S(2)}) %all-to-all-start.4) | async-done | bytes 229408 | tf_op jit(solution)/shard_map/all_to_all | solution.py:383
  106.0 0.7 shard_map.69
  106.7 0.0 collective-permute-done.12.odd_edge
  106.7 0.0 collective-permute-done.11.even_edge
  106.7 3.5 %all-to-all-start.5 = ((bf16[4,112,128]{2,1,0:T(8,128)(2,1)}), bf16[4,112,128]{2,1,0:T(8,128)(2,1)S(1)}, u32[]{:S(2)}, u32[]{:S(2)}) async-start(bf16[4,112,128]{2,1,0:T(8,128)(2,1)} %shard_map.69), calls=%async_computation.5 | async-start | bytes 229376 | tf_op jit(solution)/shard_map/all_to_all | solution.py:383
  110.2 2.6 %shard_map.70 = bf16[1024,128]{1,0:T(8,128)(2,1)} custom-call(bf16[8,128,128]{2,1,0:T(8,128)(2,1)S(1)} %bitcast.22, bf16[2,128,128]{2,1,0:T(8,128)(2,1)S(1)} %shard_map.67.own_edge, bf16[8,128,128]{2,1,0:T(8,128)(2,1)S(1)} %collective-permute-done.9.even, bf16[2,128,128]{2,1,0:T(8,128)(2,1)S(1)} %collective-permute-done.11.even_edge, ...), custom_call_target="tpu_custom_call" | custom-call | flops 905969664 | bytes 3145728 | tf_op jit(solution)/shard_map/pallas_call | solution.py:51
  112.8 3.3 %all-to-all-done.5 = bf16[4,112,128]{2,1,0:T(8,128)(2,1)S(1)} async-done(((bf16[4,112,128]{2,1,0:T(8,128)(2,1)}), bf16[4,112,128]{2,1,0:T(8,128)(2,1)S(1)}, u32[]{:S(2)}, u32[]{:S(2)}) %all-to-all-start.5) | async-done | bytes 114720 | tf_op jit(solution)/shard_map/all_to_all | solution.py:383
  116.1 0.7 convert.1
  (4 shorter events, 0.1 us)
Async XLA Ops:
  1.4 9.3 %collective-permute-start.1 = (bf16[1,128,128]{2,1,0:T(8,128)(2,1)S(1)}, bf16[1,128,128]{2,1,0:T(8,128)(2,1)S(1)}, u32[]{:S(2)}, u32[]{:S(2)}) collective-permute-start(bf16[1,128,128]{2,1,0:T(8,128)(2,1)S(1)} %get-tuple-element.59), channel_id=1, source_target_pairs={{1,2},{2,1},{3,4},{4,3},{5,6},{6,5},{9,10},{10,9},{11,12},{12,11},... | collective-permute-start | bytes 98312 | tf_op jit(solution)/shard_map/ppermute | solution.py:27
  3.3 7.4 %collective-permute-start = (bf16[1,128,128]{2,1,0:T(8,128)(2,1)S(1)}, bf16[1,128,128]{2,1,0:T(8,128)(2,1)S(1)}, u32[]{:S(2)}, u32[]{:S(2)}) collective-permute-start(bf16[1,128,128]{2,1,0:T(8,128)(2,1)S(1)} %get-tuple-element.60), channel_id=1, source_target_pairs={{0,1},{1,0},{2,3},{3,2},{4,5},{5,4},{6,7},{7,6},{8,9},{9,8},{10,11... | collective-permute-start | bytes 98312 | tf_op jit(solution)/shard_map/ppermute | solution.py:27
  4.7 13.0 %copy-start = (bf16[1,8,128,128]{3,2,1,0:T(8,128)(2,1)S(1)}, bf16[1,8,128,128]{3,2,1,0:T(8,128)(2,1)}, u32[]{:S(2)}) copy-start(bf16[1,8,128,128]{3,2,1,0:T(8,128)(2,1)} %param.5) | copy-start | bytes 786436
  4.7 13.0 %copy-start.1 = (bf16[3,3,3,128,128]{4,3,2,1,0:T(8,128)(2,1)S(1)}, bf16[3,3,3,128,128]{4,3,2,1,0:T(8,128)(2,1)}, u32[]{:S(2)}) copy-start(bf16[3,3,3,128,128]{4,3,2,1,0:T(8,128)(2,1)} %param.4) | copy-start | bytes 2654212
  4.7 13.0 %copy-start.2 = (bf16[1,8,128,128]{3,2,1,0:T(8,128)(2,1)S(1)}, bf16[1,8,128,128]{3,2,1,0:T(8,128)(2,1)}, u32[]{:S(2)}) copy-start(bf16[1,8,128,128]{3,2,1,0:T(8,128)(2,1)} %param.3) | copy-start | bytes 786436
  4.7 15.3 %collective-permute-start.4 = (bf16[8,128,128]{2,1,0:T(8,128)(2,1)}, bf16[8,128,128]{2,1,0:T(8,128)(2,1)S(1)}, u32[]{:S(2)}, u32[]{:S(2)}) collective-permute-start(bf16[8,128,128]{2,1,0:T(8,128)(2,1)} %bitcast.17), channel_id=1, source_target_pairs={{8,16},{16,8},{24,32},{32,24},{40,48},{48,40},{56,64},{64,56},{72,... | collective-permute-start | bytes 786440 | tf_op jit(solution)/shard_map/ppermute | solution.py:27
  5.5 14.5 %collective-permute-start.2 = (bf16[8,128,128]{2,1,0:T(8,128)(2,1)}, bf16[8,128,128]{2,1,0:T(8,128)(2,1)S(1)}, u32[]{:S(2)}, u32[]{:S(2)}) collective-permute-start(bf16[8,128,128]{2,1,0:T(8,128)(2,1)} %bitcast.18), channel_id=1, source_target_pairs={{0,8},{8,0},{16,24},{24,16},{32,40},{40,32},{48,56},{56,48},{64,72... | collective-permute-start | bytes 786440 | tf_op jit(solution)/shard_map/ppermute | solution.py:27
  10.7 7.6 %collective-permute-start.5 = (bf16[2,128,128]{2,1,0:T(8,128)(2,1)S(1)}, bf16[2,128,128]{2,1,0:T(8,128)(2,1)S(1)}, u32[]{:S(2)}, u32[]{:S(2)}) collective-permute-start(bf16[2,128,128]{2,1,0:T(8,128)(2,1)S(1)} %shard_map.59.own_edge), channel_id=1, source_target_pairs={{8,16},{16,8},{24,32},{32,24},{40,48},{48,40},{56,64},{64,56},{72,... | collective-permute-start | bytes 196616 | tf_op jit(solution)/shard_map/ppermute | solution.py:27
  11.4 8.6 %collective-permute-start.3 = (bf16[2,128,128]{2,1,0:T(8,128)(2,1)S(1)}, bf16[2,128,128]{2,1,0:T(8,128)(2,1)S(1)}, u32[]{:S(2)}, u32[]{:S(2)}) collective-permute-start(bf16[2,128,128]{2,1,0:T(8,128)(2,1)S(1)} %shard_map.59.own_edge), channel_id=1, source_target_pairs={{0,8},{8,0},{16,24},{24,16},{32,40},{40,32},{48,56},{56,48},{64,72... | collective-permute-start | bytes 196616 | tf_op jit(solution)/shard_map/ppermute | solution.py:27
  50.0 11.6 %all-to-all-start.2 = ((f32[32,5,128]{2,1,0:T(8,128)}), f32[32,5,128]{2,1,0:T(8,128)S(1)}, u32[]{:S(2)}, u32[]{:S(2)}) async-start(f32[32,5,128]{2,1,0:T(8,128)} %shard_map.62), calls=%async_computation.2 | async-start | bytes 262144 | tf_op jit(solution)/shard_map/all_to_all | solution.py:383
  56.5 1.4 %copy-start.3 = (bf16[1152,1024]{1,0:T(8,128)(2,1)}, bf16[1152,1024]{1,0:T(8,128)(2,1)S(1)}, u32[]{:S(2)}) copy-start(bf16[1152,1024]{1,0:T(8,128)(2,1)S(1)} %get-tuple-element.38.refs_3_) | copy-start | bytes 7077892
  61.7 1.7 %copy-start.4 = (bf16[1152,1024]{1,0:T(8,128)(2,1)S(1)}, bf16[1152,1024]{1,0:T(8,128)(2,1)}, u32[]{:S(2)}) copy-start(bf16[1152,1024]{1,0:T(8,128)(2,1)} %copy-done.3) | copy-start | bytes 7077892
  69.2 1.9 %collective-permute-start.6 = (bf16[16,112,128]{2,1,0:T(8,128)(2,1)S(1)}, bf16[16,112,128]{2,1,0:T(8,128)(2,1)S(1)}, u32[]{:S(2)}, u32[]{:S(2)}) collective-permute-start(bf16[16,112,128]{2,1,0:T(8,128)(2,1)S(1)} %get-tuple-element.44), channel_id=1, source_target_pairs={{0,1},{1,0},{2,3},{3,2},{4,5},{5,4},{6,7},{7,6},{8,9},{9,8},{10,11... | collective-permute-start | bytes 1376264 | tf_op jit(solution)/shard_map/ppermute | solution.py:463
  72.0 20.3 %all-to-all-start.3 = ((bf16[16,112,128]{2,1,0:T(8,128)(2,1)}), bf16[16,112,128]{2,1,0:T(8,128)(2,1)S(1)}, u32[]{:S(2)}, u32[]{:S(2)}) async-start(bf16[16,112,128]{2,1,0:T(8,128)(2,1)} %shard_map.65), calls=%async_computation.3 | async-start | bytes 917504 | tf_op jit(solution)/shard_map/all_to_all | solution.py:383
  77.8 15.2 %collective-permute-start.10 = (bf16[8,128,128]{2,1,0:T(8,128)(2,1)S(1)}, bf16[8,128,128]{2,1,0:T(8,128)(2,1)S(1)}, u32[]{:S(2)}, u32[]{:S(2)}) collective-permute-start(bf16[8,128,128]{2,1,0:T(8,128)(2,1)S(1)} %bitcast.20), channel_id=1, source_target_pairs={{8,16},{16,8},{24,32},{32,24},{40,48},{48,40},{56,64},{64,56},{72,... | collective-permute-start | bytes 786440 | tf_op jit(solution)/shard_map/ppermute | solution.py:27
  78.5 14.5 %collective-permute-start.9 = (bf16[8,128,128]{2,1,0:T(8,128)(2,1)S(1)}, bf16[8,128,128]{2,1,0:T(8,128)(2,1)S(1)}, u32[]{:S(2)}, u32[]{:S(2)}) collective-permute-start(bf16[8,128,128]{2,1,0:T(8,128)(2,1)S(1)} %bitcast.21), channel_id=1, source_target_pairs={{0,8},{8,0},{16,24},{24,16},{32,40},{40,32},{48,56},{56,48},{64,72... | collective-permute-start | bytes 786440 | tf_op jit(solution)/shard_map/ppermute | solution.py:27
  81.0 3.6 %collective-permute-start.7 = (bf16[1,128,128]{2,1,0:T(8,128)(2,1)S(1)}, bf16[1,128,128]{2,1,0:T(8,128)(2,1)S(1)}, u32[]{:S(2)}, u32[]{:S(2)}) collective-permute-start(bf16[1,128,128]{2,1,0:T(8,128)(2,1)S(1)} %get-tuple-element.46), channel_id=1, source_target_pairs={{0,1},{1,0},{2,3},{3,2},{4,5},{5,4},{6,7},{7,6},{8,9},{9,8},{10,11... | collective-permute-start | bytes 98312 | tf_op jit(solution)/shard_map/ppermute | solution.py:27
  81.0 5.2 %collective-permute-start.8 = (bf16[1,128,128]{2,1,0:T(8,128)(2,1)S(1)}, bf16[1,128,128]{2,1,0:T(8,128)(2,1)S(1)}, u32[]{:S(2)}, u32[]{:S(2)}) collective-permute-start(bf16[1,128,128]{2,1,0:T(8,128)(2,1)S(1)} %get-tuple-element.47), channel_id=1, source_target_pairs={{1,2},{2,1},{3,4},{4,3},{5,6},{6,5},{9,10},{10,9},{11,12},{12,11},... | collective-permute-start | bytes 98312 | tf_op jit(solution)/shard_map/ppermute | solution.py:27
  93.0 12.9 %all-to-all-start.4 = ((bf16[8,112,128]{2,1,0:T(8,128)(2,1)}), bf16[8,112,128]{2,1,0:T(8,128)(2,1)S(1)}, u32[]{:S(2)}, u32[]{:S(2)}) async-start(bf16[8,112,128]{2,1,0:T(8,128)(2,1)} %shard_map.66), calls=%async_computation.4 | async-start | bytes 458752 | tf_op jit(solution)/shard_map/all_to_all | solution.py:383
  96.5 10.2 %collective-permute-start.12 = (bf16[2,128,128]{2,1,0:T(8,128)(2,1)S(1)}, bf16[2,128,128]{2,1,0:T(8,128)(2,1)S(1)}, u32[]{:S(2)}, u32[]{:S(2)}) collective-permute-start(bf16[2,128,128]{2,1,0:T(8,128)(2,1)S(1)} %shard_map.67.own_edge), channel_id=1, source_target_pairs={{8,16},{16,8},{24,32},{32,24},{40,48},{48,40},{56,64},{64,56},{72,... | collective-permute-start | bytes 196616 | tf_op jit(solution)/shard_map/ppermute | solution.py:27
  97.1 9.5 %collective-permute-start.11 = (bf16[2,128,128]{2,1,0:T(8,128)(2,1)S(1)}, bf16[2,128,128]{2,1,0:T(8,128)(2,1)S(1)}, u32[]{:S(2)}, u32[]{:S(2)}) collective-permute-start(bf16[2,128,128]{2,1,0:T(8,128)(2,1)S(1)} %shard_map.67.own_edge), channel_id=1, source_target_pairs={{0,8},{8,0},{16,24},{24,16},{32,40},{40,32},{48,56},{56,48},{64,72... | collective-permute-start | bytes 196616 | tf_op jit(solution)/shard_map/ppermute | solution.py:27
  106.7 9.4 %all-to-all-start.5 = ((bf16[4,112,128]{2,1,0:T(8,128)(2,1)}), bf16[4,112,128]{2,1,0:T(8,128)(2,1)S(1)}, u32[]{:S(2)}, u32[]{:S(2)}) async-start(bf16[4,112,128]{2,1,0:T(8,128)(2,1)} %shard_map.69), calls=%async_computation.5 | async-start | bytes 229376 | tf_op jit(solution)/shard_map/all_to_all | solution.py:383

commit v6 on v5

--- a/solution.py
+++ b/solution.py
@@ -16,8 +16,7 @@
 GZ = ("y", "z")
 GY = ("x", "c")
 SPREAD = ("y", "x", "c")
-VMEM_BYTES = 20 * 1024 * 1024
-JOIN_FLOPS = 2 * 2**30
+VMEM_BYTES = 12 * 1024 * 1024
 
 
 def swapped(block, axes, count, first):
@@ -27,16 +26,19 @@
     return lax.ppermute(block, axes, pairs)
 
 
-def join_kernel(even, odd, rows_out):
-    rows_out[0:1] = even[...]
-    rows_out[1:2] = odd[...]
-
-
-def row_swaps(first_send, second_send):
+def ends_kernel(own, even, odd, first_out, second_out):
+    last = own.shape[0] - 1
+    odd_row = lax.axis_index("c")
+    for place, plane in enumerate((own, even, odd)):
+        first_out[place : place + 1] = plane[pl.ds((1 - odd_row) * last, 1)]
+        second_out[place : place + 1] = plane[pl.ds(odd_row * last, 1)]
+
+
+def row_swaps(own, even, odd):
     ny = lax.axis_size(GY)
-    even, odd = swapped(first_send, GY, ny, 0), swapped(second_send, GY, ny, 1)
-    joined = jax.ShapeDtypeStruct((2,) + even.shape[1:], BF16)
-    return call(join_kernel, joined, [], JOIN_FLOPS, 2**18, even, odd)
+    ends = jax.ShapeDtypeStruct((3,) + own.shape[1:], BF16)
+    first, second = call(ends_kernel, [ends, ends], [], 0, 2**18, own, even, odd)
+    return swapped(first, GY, ny, 0), swapped(second, GY, ny, 1)
 
 
 def plane_swaps(block):
@@ -64,13 +66,18 @@
     cols = slice(slot * channels, (slot + 1) * channels)
     odd_row = lax.axis_index("c")
     if tap_y == 0:
-        wide[0:1, :, cols] = edge[pl.ds(1 - odd_row, 1)]
+        wide[0:1, :, cols] = edge[0][pl.ds(1 - odd_row, 1), edge[1]]
         wide[1:rows, :, cols] = plane[0 : rows - 1]
     elif tap_y == 1:
         wide[:, :, cols] = plane[...]
     else:
         wide[0 : rows - 1, :, cols] = plane[1:rows]
-        wide[rows - 1 : rows, :, cols] = edge[pl.ds(odd_row, 1)]
+        wide[rows - 1 : rows, :, cols] = edge[0][pl.ds(odd_row, 1), edge[1]]
+
+
+def gather_rows(even_rows, odd_rows, ends):
+    ends[0] = even_rows[...]
+    ends[1] = odd_rows[...]
 
 
 def place_all(wide, own, even, odd, flip):
@@ -128,11 +135,12 @@
 
 
 def conv_kernel(
-    own, own_edge, even, even_edge, odd, odd_edge, kernel_wide, target,
-    hidden_out, sheet_out, wide,
+    own, even, odd, even_rows, odd_rows, kernel_wide, target,
+    hidden_out, sheet_out, wide, ends,
 ):
     rows, columns, channels = own.shape
-    place_all(wide, (own, own_edge), (even, even_edge), (odd, odd_edge), False)
+    gather_rows(even_rows, odd_rows, ends)
+    place_all(wide, (own, (ends, 0)), (even, (ends, 1)), (odd, (ends, 2)), False)
     flat = wide[...].reshape(rows * columns, 9 * channels)
     product = jnp.dot(flat, kernel_wide[...], preferred_element_type=F32)
     total = product[:, channels : 2 * channels]
@@ -191,10 +199,13 @@
 
 
 def grad_kernel(
-    voxels, columns, share, sheet, hidden, target, turned,
-    grad_out, first_out, second_out, keep_out, send_out, whitener_out, offset_out,
-    mats, wide, terms,
+    voxels, columns, share, sheet, pack,
+    grad_out, keep_out, send_out, whitener_out, offset_out,
+    mats, wide, terms, taps,
 ):
+    place_turned(columns, pack, taps)
+    count = taps.shape[1]
+    base = pack.shape[0] - 2 * count
     spread, depth, channels = sheet.shape
     each = depth - 1
     for j in range(spread):
@@ -258,68 +269,65 @@
     target_offset = exact(jnp.broadcast_to(target_sum / voxels, (8, channels)), whitener)
     whitener_out[...] = whitener_t
     offset_out[...] = offset[:, :channels]
-    grad = through(hidden[...], backward) - through(target[...], whitener)
+    grad = through(pack[base : base + count], backward)
+    grad = grad - through(pack[base + count :], whitener)
     wide_grad = grad - (offset[:1, channels:] - target_offset[:1])
     grad = wide_grad.astype(BF16)
     grad_out[...] = grad
-    odd_row = lax.axis_index("c")
-
-    @pl.when(odd_row == 0)
-    def _():
-        first_out[0] = grad[-columns:]
-        second_out[0] = grad[:columns]
-
-    @pl.when(odd_row == 1)
-    def _():
-        first_out[0] = grad[:columns]
-        second_out[0] = grad[-columns:]
-
-    weight_terms(columns, share, turned, grad, keep_out, send_out, wide, terms)
-
-
-def white_kernel(hidden, whitener, offset, whitened_out):
-    whitened_out[...] = (through(hidden[...], whitener[...]) - offset[0:1]).astype(BF16)
-
-
-def turn_kernel(
-    own, own_edge, even, even_edge, odd, odd_edge, hidden, target,
-    turned_out, hidden_out, target_out,
-):
-    hidden_out[...] = hidden[...]
-    target_out[...] = target[...]
+    weight_terms(columns, share, taps, grad, keep_out, send_out, wide, terms)
+
+
+def white_kernel(pack, whitener, offset, whitened_out):
+    count = whitened_out.shape[0]
+    hidden = pack[pack.shape[0] - 2 * count : pack.shape[0] - count]
+    whitened_out[...] = (through(hidden, whitener[...]) - offset[0:1]).astype(BF16)
+
+
+def turn_kernel(own, even, odd, even_rows, odd_rows, hidden, target, pack_out, ends):
     rows, columns, channels = own.shape
+    count = rows * columns
+    base = 3 * (rows + 2) * channels
+    gather_rows(even_rows, odd_rows, ends)
+    pack_out[base : base + count] = hidden[...]
+    pack_out[base + count : base + 2 * count] = target[...]
     odd_row = lax.axis_index("c")
     odd_plane = lax.rem(lax.axis_index("z"), 2)
 
     def turn(tap_z, plane, edge):
         for source in range(-1, rows + 1):
             if source < 0:
-                tile = edge[1 - odd_row]
+                tile = ends[1 - odd_row, edge]
             elif source == rows:
-                tile = edge[odd_row]
+                tile = ends[odd_row, edge]
             else:
                 tile = plane[source]
-            tile = tile.T
-            for tap_y in range(3):
-                here = source + 1 - tap_y
-                if 0 <= here < rows:
-                    slot = tap_z * 3 + tap_y
-                    turned_out[
-                        slot * channels : (slot + 1) * channels,
-                        here * columns : (here + 1) * columns,
-                    ] = tile
-
-    turn(1, own, own_edge)
+            first = (tap_z * (rows + 2) + source + 1) * channels
+            pack_out[first : first + channels] = tile.T
+
+    turn(1, own, 0)
     for parity in range(2):
 
         @pl.when(odd_plane == parity)
         def _():
-            below, above = ((odd, odd_edge), (even, even_edge))[:: 1 - 2 * parity]
+            below, above = ((odd, 2), (even, 1))[:: 1 - 2 * parity]
             turn(0, *below)
             turn(2, *above)
 
 
-def weight_terms(columns, share, turned, grad, keep_out, send_out, wide, terms):
+def place_turned(columns, pack, taps):
+    rows_all, count = taps.shape
+    channels, rows = rows_all // 9, count // columns
+    for tap_z in range(3):
+        for tap_y in range(3):
+            slot = tap_z * 3 + tap_y
+            for row in range(rows):
+                first = (tap_z * (rows + 2) + row + tap_y) * channels
+                taps[
+                    slot * channels : (slot + 1) * channels, row * columns : (row + 1) * columns
+                ] = pack[first : first + channels]
+
+
+def weight_terms(columns, share, taps, grad, keep_out, send_out, wide, terms):
     _, channels = grad.shape
     value = grad.astype(F32)
     wide[:, :channels] = moved_columns(value, -1, columns).astype(BF16)
@@ -327,7 +335,7 @@
     wide[:, 2 * channels :] = moved_columns(value, 1, columns).astype(BF16)
     pairs = channels // share // 2
     taps_each = keep_out.shape[1] // share
-    terms[...] = jnp.dot(turned[...], wide[...], preferred_element_type=F32)
+    terms[...] = jnp.dot(taps[...], wide[...], preferred_element_type=F32)
     mine = pl.multiple_of(lax.axis_index("c") * share, share)
     others = pl.multiple_of((1 - lax.axis_index("c")) * share, share)
     for tap in range(keep_out.shape[0] // pairs * taps_each):
@@ -350,10 +358,11 @@
 
 
 def input_kernel(
-    own, own_edge, even, even_edge, odd, odd_edge, weight, grad_out, wide, kernel_wide
+    own, even, odd, even_rows, odd_rows, weight, grad_out, wide, ends, kernel_wide
 ):
     rows, columns, channels = own.shape
-    place_all(wide, (own, own_edge), (even, even_edge), (odd, odd_edge), True)
+    gather_rows(even_rows, odd_rows, ends)
+    place_all(wide, (own, (ends, 0)), (even, (ends, 1)), (odd, (ends, 2)), True)
     for slot in range(9):
         for tap_x in range(3):
             kernel_wide[
@@ -404,12 +413,7 @@
     target_flat = target.reshape(count, channels)
 
     block = volume.reshape(rows, columns, channels)
-    odd_row = lax.axis_index("c")
-    first_send = lax.dynamic_slice_in_dim(block, (1 - odd_row) * (rows - 1), 1, 0)
-    second_send = lax.dynamic_slice_in_dim(block, odd_row * (rows - 1), 1, 0)
-    edges = row_swaps(first_send, second_send)
     even, odd = plane_swaps(block)
-    even_edges, odd_edges = plane_swaps(edges)
     near, kernel_wide, target_near = call(
         ready_kernel,
         [
@@ -420,7 +424,8 @@
         [pltpu.SemaphoreType.DMA((29,))],
         0, 2**20, block, weight, target_flat, far=(0, 1, 2),
     )
-    planes = [near, edges, even, even_edges, odd, odd_edges]
+    planes = [near, even, odd, *row_swaps(near, even, odd)]
+    ends = pltpu.VMEM((2, 3, columns, channels), BF16)
     wide = pltpu.VMEM((rows, columns, 9 * channels), BF16)
     hidden, sheet = call(
         conv_kernel,
@@ -428,26 +433,25 @@
             jax.ShapeDtypeStruct((count, channels), BF16),
             jax.ShapeDtypeStruct((spread, 2 * G // spread + 1, channels), F32),
         ],
-        [wide],
+        [wide, ends],
         flops, 3 * 2**20, *planes, kernel_wide, target_near,
     )
     flat = jax.ShapeDtypeStruct((count, channels), BF16)
-    turned, hidden, target_near = call(
+    pack = call(
         turn_kernel,
-        [jax.ShapeDtypeStruct((9 * channels, count), BF16), flat, flat],
-        [], 0, 3 * 2**20, *planes, hidden, target_flat,
+        jax.ShapeDtypeStruct((3 * (rows + 2) * channels + 2 * count, channels), BF16),
+        [ends], 0, 3 * 2**20, *planes, hidden, target_near,
     )
 
     mine = total_copies(exchange(sheet, SPREAD), levels, F32)
     mine = total_copies(exchange(mine, ("z",)), spread, F32)
     sheet = exchange(mine, SPREAD)
-    line = jax.ShapeDtypeStruct((1, columns, channels), BF16)
     groups = spread // 2
     shape = (groups, taps_each * share, channels)
-    grad_hidden, first_send, second_send, keep, send, whitener, offset = call(
+    grad_hidden, keep, send, whitener, offset = call(
         lambda *refs: grad_kernel(voxels, columns, share, *refs),
         [
-            flat, line, line,
+            flat,
             jax.ShapeDtypeStruct(shape, F32),
             jax.ShapeDtypeStruct(shape, BF16),
             jax.ShapeDtypeStruct((channels, channels), F32),
@@ -457,35 +461,33 @@
             pltpu.VMEM((2 * G, channels), F32),
             pltpu.VMEM((count, 3 * channels), BF16),
             pltpu.VMEM((9 * channels, 3 * channels), F32),
+            pltpu.VMEM((9 * channels, count), BF16),
         ],
-        flops, 2**20, sheet, hidden, target_near, turned,
+        flops, 2**20, sheet, pack,
     )
     received = lax.ppermute(send, ("c",), [(0, 1), (1, 0)])
     parts = call(
         pair_kernel, jax.ShapeDtypeStruct(shape, BF16), [], keep.size, 2**21, keep, received
     )
-    block, first_send, second_send, whitener, parts = lax.optimization_barrier(
-        (grad_hidden.reshape(rows, columns, channels), first_send, second_send, whitener, parts)
-    )
-    whitened = call(white_kernel, flat, [], flops, 2**20, hidden, whitener, offset)
-    edges = row_swaps(first_send, second_send)
+    block, whitener, parts = lax.optimization_barrier(
+        (grad_hidden.reshape(rows, columns, channels), whitener, parts)
+    )
+    whitened = call(white_kernel, flat, [], flops, 2**20, pack, whitener, offset)
     even, odd = plane_swaps(block)
     part = total_copies(exchange(parts, ("y", "x")), levels, BF16)
-    part, edges, even, odd, whitened = lax.optimization_barrier(
-        (part, edges, even, odd, whitened)
-    )
-    even_edges, odd_edges = plane_swaps(edges)
+    part, even, odd, whitened = lax.optimization_barrier((part, even, odd, whitened))
+    row_ends = row_swaps(block, even, odd)
     part = total_copies(exchange(part, ("z",)), rows_y, BF16, 1.0 / math.sqrt(voxels))
-    part, even_edges, odd_edges = lax.optimization_barrier((part, even_edges, odd_edges))
+    part, *row_ends = lax.optimization_barrier((part, *row_ends))
     whole = exchange(part, ("y",))
     weight_grad = whole.reshape(rows_y * taps_each, share, channels)[:27].astype(F32)
     weight_grad = weight_grad.reshape(3, 3, 3, share, channels)
 
-    planes = [block, edges, even, even_edges, odd, odd_edges]
+    planes = [block, even, odd, *row_ends]
     input_grad = call(
         input_kernel,
         jax.ShapeDtypeStruct((count, channels), BF16),
-        [wide, pltpu.VMEM((3 * channels, 9 * channels), BF16)],
+        [wide, ends, pltpu.VMEM((3 * channels, 9 * channels), BF16)],
         flops, 3 * 2**20, *planes, weight,
     )
     return (whitened.reshape(volume.shape), input_grad.reshape(volume.shape), weight_grad)

time: 118 us -> 116 us (0.983)
  starting transfers between devices: 46.3 us -> 32.2 us
  waiting for transfers between devices: 22.3 us -> 34.6 us
  blocking collectives: 27.1 us -> 28.6 us
    ppermute x12 -> x8, starting transfers between devices: 27.4 us -> 13.4 us  [swapped(): return lax.ppermute(block, axes, pairs)]
    all_to_all x4, waiting for transfers between devices: 17.2 us -> 26.9 us  [exchange(): return lax.all_to_all(parts, axes, 0, 0, tiled=True)]
    ppermute x12 -> x8, waiting for transfers between devices: 3.31 us -> 6.04 us  [swapped(): return lax.ppermute(block, axes, pairs)]
    all_to_all x2, blocking collectives: 27.1 us -> 28.6 us  [exchange(): return lax.all_to_all(parts, axes, 0, 0, tiled=True)]
    unnamed x10 -> x8, local copies, waits for them, and re-layouts: 3.09 us -> 3.07 us
  transfers between devices with their start and end apart: 17 -> 13, of which waited for: 7 -> 7; matrix products, arithmetic and copies ran while one was open for 0% -> 0% of each run, Pallas kernels for 5% -> 5%
where the time goes in v6:
time: 116 us
  waiting for transfers between devices  34.6 us (30%)
  starting transfers between devices  32.2 us (28%)
  blocking collectives  28.6 us (25%)
  Pallas kernels  15.7 us (14%)
  local copies, waits for them, and re-layouts  3.08 us (3%)
    all_to_all x2, blocking collectives, exchange(): return lax.all_to_all(parts, axes, 0, 0, tiled=True)  28.6 us
    all_to_all x4, waiting for transfers between devices, exchange(): return lax.all_to_all(parts, axes, 0, 0, tiled=True)  26.9 us
    all_to_all x4, starting transfers between devices, exchange(): return lax.all_to_all(parts, axes, 0, 0, tiled=True)  18.6 us
    pallas_call x13, Pallas kernels, call(): pl.pallas_call(kernel, out_shape=out_shape, in_specs=[hbm if i in far els...  15.7 us
    ppermute x8, starting transfers between devices, swapped(): return lax.ppermute(block, axes, pairs)  13.4 us
    ppermute x8, waiting for transfers between devices, swapped(): return lax.ppermute(block, axes, pairs)  6.04 us
    unnamed x8, local copies, waits for them, and re-layouts  3.07 us
  transfers between devices with their start and end apart: 13, of which 7 were waited for; matrix products, arithmetic and copies ran while one was open for 0% of the time, Pallas kernels for 5%

profile of v6, /device:TPU:4, one launch (start us, length us, event | category | flops | bytes accessed | tf_op | source)
XLA Modules:
  0.0 115.7 jit_solution(17940579100115610788)
XLA Ops:
  0.6 0.7 collective-permute-start.1
  1.3 5.2 %collective-permute-start = (bf16[8,128,128]{2,1,0:T(8,128)(2,1)}, bf16[8,128,128]{2,1,0:T(8,128)(2,1)S(1)}, u32[]{:S(2)}, u32[]{:S(2)}) collective-permute-start(bf16[8,128,128]{2,1,0:T(8,128)(2,1)} %bitcast.17), channel_id=1, source_target_pairs={{0,8},{8,0},{16,24},{24,16},{32,40},{40,32},{48,56},{56,48},{64,72... | collective-permute-start | bytes 786440 | tf_op jit(solution)/shard_map/ppermute | solution.py:26
  6.5 0.0 copy-start
  6.5 1.2 %copy-done = bf16[3,3,3,128,128]{4,3,2,1,0:T(8,128)(2,1)S(1)} copy-done((bf16[3,3,3,128,128]{4,3,2,1,0:T(8,128)(2,1)S(1)}, bf16[3,3,3,128,128]{4,3,2,1,0:T(8,128)(2,1)}, u32[]{:S(2)}) %copy-start) | copy-done | bytes 884760
  7.6 0.0 copy-start.2
  7.6 0.9 copy-done.2
  8.6 0.0 copy-start.3
  8.6 0.9 copy-done.3
  9.5 0.5 shard_map.58
  10.1 0.0 collective-permute-done.1.odd
  10.1 2.6 %collective-permute-done.even = bf16[8,128,128]{2,1,0:T(8,128)(2,1)S(1)} collective-permute-done((bf16[8,128,128]{2,1,0:T(8,128)(2,1)}, bf16[8,128,128]{2,1,0:T(8,128)(2,1)S(1)}, u32[]{:S(2)}, u32[]{:S(2)}) %collective-permute-start) | collective-permute-done | bytes 262176 | tf_op jit(solution)/shard_map/ppermute | solution.py:26
  12.7 0.1 collective-permute-start.2
  12.8 2.5 %collective-permute-start.3 = (bf16[3,128,128]{2,1,0:T(8,128)(2,1)S(1)}, bf16[3,128,128]{2,1,0:T(8,128)(2,1)S(1)}, u32[]{:S(2)}, u32[]{:S(2)}) collective-permute-start(bf16[3,128,128]{2,1,0:T(8,128)(2,1)S(1)} %get-tuple-element.29), channel_id=1, source_target_pairs={{1,2},{2,1},{3,4},{4,3},{5,6},{6,5},{9,10},{10,9},{11,12},{12,11},... | collective-permute-start | bytes 294920 | tf_op jit(solution)/shard_map/ppermute | solution.py:26
  15.4 0.0 collective-permute-done.2.even_rows
  15.4 3.4 %collective-permute-done.3.odd_rows = bf16[3,128,128]{2,1,0:T(8,128)(2,1)S(1)} collective-permute-done((bf16[3,128,128]{2,1,0:T(8,128)(2,1)S(1)}, bf16[3,128,128]{2,1,0:T(8,128)(2,1)S(1)}, u32[]{:S(2)}, u32[]{:S(2)}) %collective-permute-start.3) | collective-permute-done | bytes 98336 | tf_op jit(solution)/shard_map/ppermute | solution.py:26
  18.8 2.2 %shard_map.60 = (bf16[1024,128]{1,0:T(8,128)(2,1)S(1)}, f32[32,5,128]{2,1,0:T(8,128)S(1)}) custom-call(bf16[8,128,128]{2,1,0:T(8,128)(2,1)S(1)} %get-tuple-element.27.own, bf16[8,128,128]{2,1,0:T(8,128)(2,1)S(1)} %collective-permute-done.even, bf16[8,128,128]{2,1,0:T(8,128)(2,1)S(1)} %collective-permute-done.1.odd, ...), custom_call_target="tpu_custom_call" | custom-call | flops 905969664 | bytes 3145728 | tf_op jit(solution)/shard_map/pallas_call | solution.py:53
  21.0 16.8 %all_to_all.30.refs_0_ = f32[32,5,128]{2,1,0:T(8,128)S(1)} all-to-all(f32[32,5,128]{2,1,0:T(8,128)S(1)} %get-tuple-element.32), channel_id=1, replica_groups=mesh['y'=4,'z'=8,'x'=4,'c'=2] {'y','x','c'}, dimensions={0} | all-to-all | bytes 163840 | tf_op jit(solution)/shard_map/all_to_all | solution.py:392
  37.8 11.8 %all_to_all.31.refs_0_ = f32[8,5,128]{2,1,0:T(8,128)S(1)} all-to-all(f32[8,5,128]{2,1,0:T(8,128)S(1)} %shard_map.61), channel_id=1, replica_groups=mesh['y'=4,'z'=8,'x'=4,'c'=2] {'z'}, dimensions={0} | all-to-all | bytes 40960 | tf_op jit(solution)/shard_map/all_to_all | solution.py:392
  49.6 0.7 shard_map.62
  50.3 6.0 %all-to-all-start.2 = ((f32[32,5,128]{2,1,0:T(8,128)}), f32[32,5,128]{2,1,0:T(8,128)S(1)}, u32[]{:S(2)}, u32[]{:S(2)}) async-start(f32[32,5,128]{2,1,0:T(8,128)} %shard_map.62), calls=%async_computation.2 | async-start | bytes 262144 | tf_op jit(solution)/shard_map/all_to_all | solution.py:392
  56.3 0.4 shard_map.63.refs_1_.pack
  56.7 5.3 %all-to-all-done.2.refs_0_ = f32[32,5,128]{2,1,0:T(8,128)S(1)} async-done(((f32[32,5,128]{2,1,0:T(8,128)}), f32[32,5,128]{2,1,0:T(8,128)S(1)}, u32[]{:S(2)}, u32[]{:S(2)}) %all-to-all-start.2) | async-done | bytes 81952 | tf_op jit(solution)/shard_map/all_to_all | solution.py:392
  62.0 5.9 %shard_map.64 = (bf16[1024,128]{1,0:T(8,128)(2,1)S(1)}, f32[16,112,128]{2,1,0:T(8,128)S(1)}, bf16[16,112,128]{2,1,0:T(8,128)(2,1)S(1)}, f32[128,128]{1,0:T(8,128)S(1)}, f32[8,128]{1,0:T(8,128)S(1)}) custom-call(f32[32,5,128]{2,1,0:T(8,128)S(1)} %all-to-all-done.2.refs_0_, bf16[5888,128]{1,0:T(8,128)(2,1)S(1)} %shard_map.63.refs_1_.pack), custom_call_target="tpu_custom_call" | custom-call | flops 905969664 | bytes 1048576 | tf_op jit(solution)/shard_map/pallas_call | solution.py:53
  67.8 0.2 collective-permute-start.4
  68.0 1.7 %collective-permute-done.4.received = bf16[16,112,128]{2,1,0:T(8,128)(2,1)S(1)} collective-permute-done((bf16[16,112,128]{2,1,0:T(8,128)(2,1)S(1)}, bf16[16,112,128]{2,1,0:T(8,128)(2,1)S(1)}, u32[]{:S(2)}, u32[]{:S(2)}) %collective-permute-start.4) | collective-permute-done | bytes 458784 | tf_op jit(solution)/shard_map/ppermute | solution.py:468
  69.7 0.9 shard_map.65
  70.6 5.8 %all-to-all-start.3 = ((bf16[16,112,128]{2,1,0:T(8,128)(2,1)}), bf16[16,112,128]{2,1,0:T(8,128)(2,1)S(1)}, u32[]{:S(2)}, u32[]{:S(2)}) async-start(bf16[16,112,128]{2,1,0:T(8,128)(2,1)} %shard_map.65), calls=%async_computation.3 | async-start | bytes 917504 | tf_op jit(solution)/shard_map/all_to_all | solution.py:392
  76.4 0.7 collective-permute-start.6
  77.1 2.3 %collective-permute-start.5 = (bf16[8,128,128]{2,1,0:T(8,128)(2,1)S(1)}, bf16[8,128,128]{2,1,0:T(8,128)(2,1)S(1)}, u32[]{:S(2)}, u32[]{:S(2)}) collective-permute-start(bf16[8,128,128]{2,1,0:T(8,128)(2,1)S(1)} %bitcast.12), channel_id=1, source_target_pairs={{0,8},{8,0},{16,24},{24,16},{32,40},{40,32},{48,56},{56,48},{64,72... | collective-permute-start | bytes 786440 | tf_op jit(solution)/shard_map/ppermute | solution.py:26
  79.4 1.1 shard_map.67
  80.5 0.0 copy-start.1
  80.5 10.4 %all-to-all-done.3.refs_0_ = bf16[16,112,128]{2,1,0:T(8,128)(2,1)S(1)} async-done(((bf16[16,112,128]{2,1,0:T(8,128)(2,1)}), bf16[16,112,128]{2,1,0:T(8,128)(2,1)S(1)}, u32[]{:S(2)}, u32[]{:S(2)}) %all-to-all-start.3) | async-done | bytes 458784 | tf_op jit(solution)/shard_map/all_to_all | solution.py:392
  90.9 0.8 shard_map.66
  91.6 0.0 collective-permute-done.6.odd
  91.6 0.0 collective-permute-done.5.even
  91.6 3.4 %all-to-all-start.4 = ((bf16[8,112,128]{2,1,0:T(8,128)(2,1)}), bf16[8,112,128]{2,1,0:T(8,128)(2,1)S(1)}, u32[]{:S(2)}, u32[]{:S(2)}) async-start(bf16[8,112,128]{2,1,0:T(8,128)(2,1)} %shard_map.66), calls=%async_computation.4 | async-start | bytes 458752 | tf_op jit(solution)/shard_map/all_to_all | solution.py:392
  95.1 0.1 collective-permute-start.7
  95.2 1.9 %collective-permute-start.8 = (bf16[3,128,128]{2,1,0:T(8,128)(2,1)S(1)}, bf16[3,128,128]{2,1,0:T(8,128)(2,1)S(1)}, u32[]{:S(2)}, u32[]{:S(2)}) collective-permute-start(bf16[3,128,128]{2,1,0:T(8,128)(2,1)S(1)} %get-tuple-element.47), channel_id=1, source_target_pairs={{1,2},{2,1},{3,4},{4,3},{5,6},{6,5},{9,10},{10,9},{11,12},{12,11},... | collective-permute-start | bytes 294920 | tf_op jit(solution)/shard_map/ppermute | solution.py:26
  97.1 8.0 %all-to-all-done.4.refs_0_ = bf16[8,112,128]{2,1,0:T(8,128)(2,1)S(1)} async-done(((bf16[8,112,128]{2,1,0:T(8,128)(2,1)}), bf16[8,112,128]{2,1,0:T(8,128)(2,1)S(1)}, u32[]{:S(2)}, u32[]{:S(2)}) %all-to-all-start.4) | async-done | bytes 229408 | tf_op jit(solution)/shard_map/all_to_all | solution.py:392
  105.1 0.7 shard_map.68
  105.8 0.0 collective-permute-done.7.even_rows
  105.8 0.0 collective-permute-done.8.odd_rows
  105.8 3.3 %all-to-all-start.5 = ((bf16[4,112,128]{2,1,0:T(8,128)(2,1)}), bf16[4,112,128]{2,1,0:T(8,128)(2,1)S(1)}, u32[]{:S(2)}, u32[]{:S(2)}) async-start(bf16[4,112,128]{2,1,0:T(8,128)(2,1)} %shard_map.68), calls=%async_computation.5 | async-start | bytes 229376 | tf_op jit(solution)/shard_map/all_to_all | solution.py:392
  109.1 0.0 copy-done.1
  109.1 2.6 %shard_map.70 = bf16[1024,128]{1,0:T(8,128)(2,1)} custom-call(bf16[8,128,128]{2,1,0:T(8,128)(2,1)S(1)} %bitcast.14, bf16[8,128,128]{2,1,0:T(8,128)(2,1)S(1)} %collective-permute-done.5.even, bf16[8,128,128]{2,1,0:T(8,128)(2,1)S(1)} %collective-permute-done.6.odd, bf16[3,128,128]{2,1,0:T(8,128)(2,1)S(1)} %collective-permute-done.7.even_rows, ...), custom_call_target="tpu_custom_call" | custom-call | flops 905969664 | bytes 3145728 | tf_op jit(solution)/shard_map/pallas_call | solution.py:53
  111.7 3.2 %all-to-all-done.5 = bf16[4,112,128]{2,1,0:T(8,128)(2,1)S(1)} async-done(((bf16[4,112,128]{2,1,0:T(8,128)(2,1)}), bf16[4,112,128]{2,1,0:T(8,128)(2,1)S(1)}, u32[]{:S(2)}, u32[]{:S(2)}) %all-to-all-start.5) | async-done | bytes 114720 | tf_op jit(solution)/shard_map/all_to_all | solution.py:392
  115.0 0.7 convert.1
  (4 shorter events, 0.1 us)
Async XLA Ops:
  0.6 9.4 %collective-permute-start.1 = (bf16[8,128,128]{2,1,0:T(8,128)(2,1)}, bf16[8,128,128]{2,1,0:T(8,128)(2,1)S(1)}, u32[]{:S(2)}, u32[]{:S(2)}) collective-permute-start(bf16[8,128,128]{2,1,0:T(8,128)(2,1)} %bitcast.16), channel_id=1, source_target_pairs={{8,16},{16,8},{24,32},{32,24},{40,48},{48,40},{56,64},{64,56},{72,... | collective-permute-start | bytes 786440 | tf_op jit(solution)/shard_map/ppermute | solution.py:26
  1.3 11.4 %collective-permute-start = (bf16[8,128,128]{2,1,0:T(8,128)(2,1)}, bf16[8,128,128]{2,1,0:T(8,128)(2,1)S(1)}, u32[]{:S(2)}, u32[]{:S(2)}) collective-permute-start(bf16[8,128,128]{2,1,0:T(8,128)(2,1)} %bitcast.17), channel_id=1, source_target_pairs={{0,8},{8,0},{16,24},{24,16},{32,40},{40,32},{48,56},{56,48},{64,72... | collective-permute-start | bytes 786440 | tf_op jit(solution)/shard_map/ppermute | solution.py:26
  6.5 1.2 %copy-start = (bf16[3,3,3,128,128]{4,3,2,1,0:T(8,128)(2,1)S(1)}, bf16[3,3,3,128,128]{4,3,2,1,0:T(8,128)(2,1)}, u32[]{:S(2)}) copy-start(bf16[3,3,3,128,128]{4,3,2,1,0:T(8,128)(2,1)} %param.4) | copy-start | bytes 2654212
  7.6 0.9 copy-start.2
  8.6 0.9 copy-start.3
  12.7 2.6 %collective-permute-start.2 = (bf16[3,128,128]{2,1,0:T(8,128)(2,1)S(1)}, bf16[3,128,128]{2,1,0:T(8,128)(2,1)S(1)}, u32[]{:S(2)}, u32[]{:S(2)}) collective-permute-start(bf16[3,128,128]{2,1,0:T(8,128)(2,1)S(1)} %get-tuple-element.28), channel_id=1, source_target_pairs={{0,1},{1,0},{2,3},{3,2},{4,5},{5,4},{6,7},{7,6},{8,9},{9,8},{10,11... | collective-permute-start | bytes 294920 | tf_op jit(solution)/shard_map/ppermute | solution.py:26
  12.8 5.9 %collective-permute-start.3 = (bf16[3,128,128]{2,1,0:T(8,128)(2,1)S(1)}, bf16[3,128,128]{2,1,0:T(8,128)(2,1)S(1)}, u32[]{:S(2)}, u32[]{:S(2)}) collective-permute-start(bf16[3,128,128]{2,1,0:T(8,128)(2,1)S(1)} %get-tuple-element.29), channel_id=1, source_target_pairs={{1,2},{2,1},{3,4},{4,3},{5,6},{6,5},{9,10},{10,9},{11,12},{12,11},... | collective-permute-start | bytes 294920 | tf_op jit(solution)/shard_map/ppermute | solution.py:26
  50.3 11.6 %all-to-all-start.2 = ((f32[32,5,128]{2,1,0:T(8,128)}), f32[32,5,128]{2,1,0:T(8,128)S(1)}, u32[]{:S(2)}, u32[]{:S(2)}) async-start(f32[32,5,128]{2,1,0:T(8,128)} %shard_map.62), calls=%async_computation.2 | async-start | bytes 262144 | tf_op jit(solution)/shard_map/all_to_all | solution.py:392
  67.8 1.9 %collective-permute-start.4 = (bf16[16,112,128]{2,1,0:T(8,128)(2,1)S(1)}, bf16[16,112,128]{2,1,0:T(8,128)(2,1)S(1)}, u32[]{:S(2)}, u32[]{:S(2)}) collective-permute-start(bf16[16,112,128]{2,1,0:T(8,128)(2,1)S(1)} %get-tuple-element.37), channel_id=1, source_target_pairs={{0,1},{1,0},{2,3},{3,2},{4,5},{5,4},{6,7},{7,6},{8,9},{9,8},{10,11... | collective-permute-start | bytes 1376264 | tf_op jit(solution)/shard_map/ppermute | solution.py:468
  70.6 20.3 %all-to-all-start.3 = ((bf16[16,112,128]{2,1,0:T(8,128)(2,1)}), bf16[16,112,128]{2,1,0:T(8,128)(2,1)S(1)}, u32[]{:S(2)}, u32[]{:S(2)}) async-start(bf16[16,112,128]{2,1,0:T(8,128)(2,1)} %shard_map.65), calls=%async_computation.3 | async-start | bytes 917504 | tf_op jit(solution)/shard_map/all_to_all | solution.py:392
  76.4 15.2 %collective-permute-start.6 = (bf16[8,128,128]{2,1,0:T(8,128)(2,1)S(1)}, bf16[8,128,128]{2,1,0:T(8,128)(2,1)S(1)}, u32[]{:S(2)}, u32[]{:S(2)}) collective-permute-start(bf16[8,128,128]{2,1,0:T(8,128)(2,1)S(1)} %bitcast.11), channel_id=1, source_target_pairs={{8,16},{16,8},{24,32},{32,24},{40,48},{48,40},{56,64},{64,56},{72,... | collective-permute-start | bytes 786440 | tf_op jit(solution)/shard_map/ppermute | solution.py:26
  77.1 14.5 %collective-permute-start.5 = (bf16[8,128,128]{2,1,0:T(8,128)(2,1)S(1)}, bf16[8,128,128]{2,1,0:T(8,128)(2,1)S(1)}, u32[]{:S(2)}, u32[]{:S(2)}) collective-permute-start(bf16[8,128,128]{2,1,0:T(8,128)(2,1)S(1)} %bitcast.12), channel_id=1, source_target_pairs={{0,8},{8,0},{16,24},{24,16},{32,40},{40,32},{48,56},{56,48},{64,72... | collective-permute-start | bytes 786440 | tf_op jit(solution)/shard_map/ppermute | solution.py:26
  80.5 28.6 %copy-start.1 = (bf16[3,3,3,128,128]{4,3,2,1,0:T(8,128)(2,1)S(1)}, bf16[3,3,3,128,128]{4,3,2,1,0:T(8,128)(2,1)}, u32[]{:S(2)}) copy-start(bf16[3,3,3,128,128]{4,3,2,1,0:T(8,128)(2,1)} %param.4) | copy-start | bytes 2654212
  91.6 13.4 %all-to-all-start.4 = ((bf16[8,112,128]{2,1,0:T(8,128)(2,1)}), bf16[8,112,128]{2,1,0:T(8,128)(2,1)S(1)}, u32[]{:S(2)}, u32[]{:S(2)}) async-start(bf16[8,112,128]{2,1,0:T(8,128)(2,1)} %shard_map.66), calls=%async_computation.4 | async-start | bytes 458752 | tf_op jit(solution)/shard_map/all_to_all | solution.py:392
  95.1 10.7 %collective-permute-start.7 = (bf16[3,128,128]{2,1,0:T(8,128)(2,1)S(1)}, bf16[3,128,128]{2,1,0:T(8,128)(2,1)S(1)}, u32[]{:S(2)}, u32[]{:S(2)}) collective-permute-start(bf16[3,128,128]{2,1,0:T(8,128)(2,1)S(1)} %get-tuple-element.46), channel_id=1, source_target_pairs={{0,1},{1,0},{2,3},{3,2},{4,5},{5,4},{6,7},{7,6},{8,9},{9,8},{10,11... | collective-permute-start | bytes 294920 | tf_op jit(solution)/shard_map/ppermute | solution.py:26
  95.2 10.6 %collective-permute-start.8 = (bf16[3,128,128]{2,1,0:T(8,128)(2,1)S(1)}, bf16[3,128,128]{2,1,0:T(8,128)(2,1)S(1)}, u32[]{:S(2)}, u32[]{:S(2)}) collective-permute-start(bf16[3,128,128]{2,1,0:T(8,128)(2,1)S(1)} %get-tuple-element.47), channel_id=1, source_target_pairs={{1,2},{2,1},{3,4},{4,3},{5,6},{6,5},{9,10},{10,9},{11,12},{12,11},... | collective-permute-start | bytes 294920 | tf_op jit(solution)/shard_map/ppermute | solution.py:26
  105.8 9.2 %all-to-all-start.5 = ((bf16[4,112,128]{2,1,0:T(8,128)(2,1)}), bf16[4,112,128]{2,1,0:T(8,128)(2,1)S(1)}, u32[]{:S(2)}, u32[]{:S(2)}) async-start(bf16[4,112,128]{2,1,0:T(8,128)(2,1)} %shard_map.68), calls=%async_computation.5 | async-start | bytes 229376 | tf_op jit(solution)/shard_map/all_to_all | solution.py:392

commit v7 on v6

--- a/solution.py
+++ b/solution.py
@@ -134,26 +134,69 @@
         move.wait()
 
 
+def with_shifts(product, columns):
+    channels = product.shape[1] // 3
+    total = product[:, channels : 2 * channels]
+    total = total + moved_columns(product[:, :channels], 1, columns)
+    return total + moved_columns(product[:, 2 * channels :], -1, columns)
+
+
+def moments(hidden, features):
+    second = over_rows(hidden, hidden)
+    cross = over_rows(features, hidden)
+    first = lax.broadcasted_iota(jnp.int32, (G, hidden.shape[1]), 1) < G
+    second = jnp.where(first, second[:G], second[G:])
+    return second, jnp.where(first, cross[:G], cross[G:])
+
+
 def conv_kernel(
-    own, even, odd, even_rows, odd_rows, kernel_wide, target,
-    hidden_out, sheet_out, wide, ends,
+    own, even, odd, kernel_wide, target,
+    hidden_out, ends_out, moments_out, sums_out, wide, none,
 ):
     rows, columns, channels = own.shape
-    gather_rows(even_rows, odd_rows, ends)
-    place_all(wide, (own, (ends, 0)), (even, (ends, 1)), (odd, (ends, 2)), False)
+    none[...] = jnp.zeros(none.shape, BF16)
+    place_all(wide, (own, (none, 0)), (even, (none, 0)), (odd, (none, 0)), False)
     flat = wide[...].reshape(rows * columns, 9 * channels)
     product = jnp.dot(flat, kernel_wide[...], preferred_element_type=F32)
-    total = product[:, channels : 2 * channels]
-    total = total + moved_columns(product[:, :channels], 1, columns)
-    total = total + moved_columns(product[:, 2 * channels :], -1, columns)
+    total = with_shifts(product, columns)
+    ends_out[:columns] = total[:columns]
+    ends_out[columns:] = total[-columns:]
     hidden = total.astype(BF16)
     hidden_out[...] = hidden
-    features = target[...]
-    second = over_rows(hidden, hidden)
-    cross = over_rows(features, hidden)
-    first = lax.broadcasted_iota(jnp.int32, (G, channels), 1) < G
-    second = jnp.where(first, second[:G], second[G:])
-    cross = jnp.where(first, cross[:G], cross[G:])
+    inner = hidden[columns:-columns]
+    moments_out[:G], moments_out[G:] = moments(inner, target[columns:-columns])
+    sums_out[0:1] = jnp.sum(inner.astype(F32), axis=0, keepdims=True)
+    sums_out[1:2] = jnp.sum(target[...].astype(F32), axis=0, keepdims=True)
+    sums_out[2:] = jnp.zeros((sums_out.shape[0] - 2, channels), F32)
+
+
+def finish_kernel(
+    totals, even_rows, odd_rows, kernel_wide, target, moments_in, sums,
+    hidden_out, sheet_out, ends,
+):
+    _, columns, channels = even_rows.shape
+    gather_rows(even_rows, odd_rows, ends)
+    odd_row = lax.axis_index("c")
+    odd_plane = lax.rem(lax.axis_index("z"), 2)
+    order = (2 - odd_plane, 0, 1 + odd_plane)
+
+    def part(side, tap_y):
+        tiles = [ends[side, place] for place in order]
+        taps = [(tap_z * 3 + tap_y) * channels for tap_z in range(3)]
+        kernel = [kernel_wide[tap : tap + channels, :] for tap in taps]
+        product = jnp.dot(
+            jnp.concatenate(tiles, axis=1),
+            jnp.concatenate(kernel, axis=0),
+            preferred_element_type=F32,
+        )
+        return with_shifts(product, columns)
+
+    total = totals[...] + jnp.concatenate([part(1 - odd_row, 0), part(odd_row, 2)], axis=0)
+    hidden = total.astype(BF16)
+    hidden_out[...] = hidden
+    features = jnp.concatenate([target[:columns], target[target.shape[0] - columns :]], axis=0)
+    second, cross = moments(hidden, features)
+    second, cross = second + moments_in[:G], cross + moments_in[G:]
     spread, depth, _ = sheet_out.shape
     each = depth - 1
     half = spread // 2
@@ -162,8 +205,9 @@
         sheet_out[half + j, 0:each, :] = cross[each * j : each * (j + 1)]
     for j in range(2, spread):
         sheet_out[j, each:depth, :] = jnp.zeros((1, channels), F32)
-    sheet_out[0, each:depth, :] = jnp.sum(hidden.astype(F32), axis=0, keepdims=True)
-    sheet_out[1, each:depth, :] = jnp.sum(features.astype(F32), axis=0, keepdims=True)
+    hidden_sum = jnp.sum(hidden.astype(F32), axis=0, keepdims=True)
+    sheet_out[0, each:depth, :] = sums[0:1] + hidden_sum
+    sheet_out[1, each:depth, :] = sums[1:2]
 
 
 def thirds(value):
@@ -283,12 +327,16 @@
     whitened_out[...] = (through(hidden, whitener[...]) - offset[0:1]).astype(BF16)
 
 
-def turn_kernel(own, even, odd, even_rows, odd_rows, hidden, target, pack_out, ends):
+def turn_kernel(
+    own, even, odd, even_rows, odd_rows, hidden, hidden_ends, target, pack_out, ends
+):
     rows, columns, channels = own.shape
     count = rows * columns
     base = 3 * (rows + 2) * channels
     gather_rows(even_rows, odd_rows, ends)
-    pack_out[base : base + count] = hidden[...]
+    pack_out[base : base + columns] = hidden_ends[:columns]
+    pack_out[base + columns : base + count - columns] = hidden[columns : count - columns]
+    pack_out[base + count - columns : base + count] = hidden_ends[columns:]
     pack_out[base + count : base + 2 * count] = target[...]
     odd_row = lax.axis_index("c")
     odd_plane = lax.rem(lax.axis_index("z"), 2)
@@ -424,23 +472,35 @@
         [pltpu.SemaphoreType.DMA((29,))],
         0, 2**20, block, weight, target_flat, far=(0, 1, 2),
     )
-    planes = [near, even, odd, *row_swaps(near, even, odd)]
+    even_rows, odd_rows = row_swaps(near, even, odd)
     ends = pltpu.VMEM((2, 3, columns, channels), BF16)
     wide = pltpu.VMEM((rows, columns, 9 * channels), BF16)
-    hidden, sheet = call(
+    hidden, totals, moments_here, sums_here = call(
         conv_kernel,
         [
             jax.ShapeDtypeStruct((count, channels), BF16),
+            jax.ShapeDtypeStruct((2 * columns, channels), F32),
+            jax.ShapeDtypeStruct((2 * G, channels), F32),
+            jax.ShapeDtypeStruct((8, channels), F32),
+        ],
+        [wide, pltpu.VMEM((2, 1, columns, channels), BF16)],
+        flops, 3 * 2**20, near, even, odd, kernel_wide, target_near,
+    )
+    hidden_ends, sheet = call(
+        finish_kernel,
+        [
+            jax.ShapeDtypeStruct((2 * columns, channels), BF16),
             jax.ShapeDtypeStruct((spread, 2 * G // spread + 1, channels), F32),
         ],
-        [wide, ends],
-        flops, 3 * 2**20, *planes, kernel_wide, target_near,
+        [ends],
+        flops // 12, 2**20,
+        totals, even_rows, odd_rows, kernel_wide, target_near, moments_here, sums_here,
     )
     flat = jax.ShapeDtypeStruct((count, channels), BF16)
     pack = call(
         turn_kernel,
         jax.ShapeDtypeStruct((3 * (rows + 2) * channels + 2 * count, channels), BF16),
-        [ends], 0, 3 * 2**20, *planes, hidden, target_near,
+        [ends], 0, 3 * 2**20, near, even, odd, even_rows, odd_rows, hidden, hidden_ends, target_near,
     )
 
     mine = total_copies(exchange(sheet, SPREAD), levels, F32)

time: 116 us -> 115 us (level)
  waiting for transfers between devices: 34.6 us -> 32.3 us
    ppermute x8, waiting for transfers between devices: 6.04 us -> 3.95 us  [swapped(): return lax.ppermute(block, axes, pairs)]
    pallas_call x13 -> x14, Pallas kernels: 15.7 us -> 16.1 us  [call(): pl.pallas_call(kernel, out_shape=out_shape, in_specs=[hbm if i in far els...]
  transfers between devices with their start and end apart: 13 -> 13, of which waited for: 7 -> 7; matrix products, arithmetic and copies ran while one was open for 0% -> 0% of each run, Pallas kernels for 5% -> 7%
where the time goes in v7:
time: 115 us; the launch traced here: 114 us
  starting transfers between devices  32.4 us (28%)
  waiting for transfers between devices  32.3 us (28%)
  blocking collectives  28.6 us (25%)
  Pallas kernels  16.1 us (14%)
  local copies, waits for them, and re-layouts  3.08 us (3%)
    all_to_all x2, blocking collectives, exchange(): return lax.all_to_all(parts, axes, 0, 0, tiled=True)  28.6 us
    all_to_all x4, waiting for transfers between devices, exchange(): return lax.all_to_all(parts, axes, 0, 0, tiled=True)  26.7 us
    all_to_all x4, starting transfers between devices, exchange(): return lax.all_to_all(parts, axes, 0, 0, tiled=True)  18.6 us
    pallas_call x14, Pallas kernels, call(): pl.pallas_call(kernel, out_shape=out_shape, in_specs=[hbm if i in far els...  16.1 us
    ppermute x8, starting transfers between devices, swapped(): return lax.ppermute(block, axes, pairs)  13.6 us
    ppermute x8, waiting for transfers between devices, swapped(): return lax.ppermute(block, axes, pairs)  3.95 us
    unnamed x8, local copies, waits for them, and re-layouts  3.07 us
  transfers between devices with their start and end apart: 13, of which 7 were waited for; matrix products, arithmetic and copies ran while one was open for 0% of the time, Pallas kernels for 7%

profile of v7, /device:TPU:4, one launch (start us, length us, event | category | flops | bytes accessed | tf_op | source)
XLA Modules:
  0.0 114.0 jit_solution(2725006301438205327)
XLA Ops:
  0.6 0.7 collective-permute-start.1
  1.3 5.2 %collective-permute-start = (bf16[8,128,128]{2,1,0:T(8,128)(2,1)}, bf16[8,128,128]{2,1,0:T(8,128)(2,1)S(1)}, u32[]{:S(2)}, u32[]{:S(2)}) collective-permute-start(bf16[8,128,128]{2,1,0:T(8,128)(2,1)} %bitcast.17), channel_id=1, source_target_pairs={{0,8},{8,0},{16,24},{24,16},{32,40},{40,32},{48,56},{56,48},{64,72... | collective-permute-start | bytes 786440 | tf_op jit(solution)/shard_map/ppermute | solution.py:26
  6.5 0.0 copy-start
  6.5 1.2 %copy-done = bf16[3,3,3,128,128]{4,3,2,1,0:T(8,128)(2,1)S(1)} copy-done((bf16[3,3,3,128,128]{4,3,2,1,0:T(8,128)(2,1)S(1)}, bf16[3,3,3,128,128]{4,3,2,1,0:T(8,128)(2,1)}, u32[]{:S(2)}) %copy-start) | copy-done | bytes 884760
  7.6 0.0 copy-start.2
  7.6 0.9 copy-done.2
  8.6 0.0 copy-start.3
  8.6 0.9 copy-done.3
  9.5 0.5 shard_map.58
  10.1 0.0 collective-permute-done.1.odd
  10.1 2.6 %collective-permute-done.even = bf16[8,128,128]{2,1,0:T(8,128)(2,1)S(1)} collective-permute-done((bf16[8,128,128]{2,1,0:T(8,128)(2,1)}, bf16[8,128,128]{2,1,0:T(8,128)(2,1)S(1)}, u32[]{:S(2)}, u32[]{:S(2)}) %collective-permute-start) | collective-permute-done | bytes 262176 | tf_op jit(solution)/shard_map/ppermute | solution.py:26
  12.7 0.1 collective-permute-start.2
  12.8 2.5 %collective-permute-start.3 = (bf16[3,128,128]{2,1,0:T(8,128)(2,1)S(1)}, bf16[3,128,128]{2,1,0:T(8,128)(2,1)S(1)}, u32[]{:S(2)}, u32[]{:S(2)}) collective-permute-start(bf16[3,128,128]{2,1,0:T(8,128)(2,1)S(1)} %get-tuple-element.36), channel_id=1, source_target_pairs={{1,2},{2,1},{3,4},{4,3},{5,6},{6,5},{9,10},{10,9},{11,12},{12,11},... | collective-permute-start | bytes 294920 | tf_op jit(solution)/shard_map/ppermute | solution.py:26
  15.4 2.1 %shard_map.59 = (bf16[1024,128]{1,0:T(8,128)(2,1)S(1)}, f32[256,128]{1,0:T(8,128)S(1)}, f32[128,128]{1,0:T(8,128)S(1)}, f32[8,128]{1,0:T(8,128)S(1)}) custom-call(bf16[8,128,128]{2,1,0:T(8,128)(2,1)S(1)} %get-tuple-element.31.own, bf16[8,128,128]{2,1,0:T(8,128)(2,1)S(1)} %collective-permute-done.even, bf16[8,128,128]{2,1,0:T(8,128)(2,1)S(1)} %collective-permute-done.1.odd, ...), custom_call_target="tpu_custom_call" | custom-call | flops 905969664 | bytes 3145728 | tf_op jit(solution)/shard_map/pallas_call | solution.py:53
  17.4 0.0 collective-permute-done.2.even_rows
  17.5 1.3 %collective-permute-done.3.odd_rows = bf16[3,128,128]{2,1,0:T(8,128)(2,1)S(1)} collective-permute-done((bf16[3,128,128]{2,1,0:T(8,128)(2,1)S(1)}, bf16[3,128,128]{2,1,0:T(8,128)(2,1)S(1)}, u32[]{:S(2)}, u32[]{:S(2)}) %collective-permute-start.3) | collective-permute-done | bytes 98336 | tf_op jit(solution)/shard_map/ppermute | solution.py:26
  18.8 0.5 shard_map.61
  19.3 16.8 %all_to_all.30.refs_0_ = f32[32,5,128]{2,1,0:T(8,128)S(1)} all-to-all(f32[32,5,128]{2,1,0:T(8,128)S(1)} %get-tuple-element.39), channel_id=1, replica_groups=mesh['y'=4,'z'=8,'x'=4,'c'=2] {'y','x','c'}, dimensions={0} | all-to-all | bytes 163840 | tf_op jit(solution)/shard_map/all_to_all | solution.py:440
  36.1 11.8 %all_to_all.31.refs_0_ = f32[8,5,128]{2,1,0:T(8,128)S(1)} all-to-all(f32[8,5,128]{2,1,0:T(8,128)S(1)} %shard_map.62), channel_id=1, replica_groups=mesh['y'=4,'z'=8,'x'=4,'c'=2] {'z'}, dimensions={0} | all-to-all | bytes 40960 | tf_op jit(solution)/shard_map/all_to_all | solution.py:440
  47.9 0.7 shard_map.63
  48.6 6.0 %all-to-all-start.2 = ((f32[32,5,128]{2,1,0:T(8,128)}), f32[32,5,128]{2,1,0:T(8,128)S(1)}, u32[]{:S(2)}, u32[]{:S(2)}) async-start(f32[32,5,128]{2,1,0:T(8,128)} %shard_map.63), calls=%async_computation.2 | async-start | bytes 262144 | tf_op jit(solution)/shard_map/all_to_all | solution.py:440
  54.6 0.4 shard_map.64.refs_1_.pack
  55.0 5.3 %all-to-all-done.2.refs_0_ = f32[32,5,128]{2,1,0:T(8,128)S(1)} async-done(((f32[32,5,128]{2,1,0:T(8,128)}), f32[32,5,128]{2,1,0:T(8,128)S(1)}, u32[]{:S(2)}, u32[]{:S(2)}) %all-to-all-start.2) | async-done | bytes 81952 | tf_op jit(solution)/shard_map/all_to_all | solution.py:440
  60.3 5.9 %shard_map.65 = (bf16[1024,128]{1,0:T(8,128)(2,1)S(1)}, f32[16,112,128]{2,1,0:T(8,128)S(1)}, bf16[16,112,128]{2,1,0:T(8,128)(2,1)S(1)}, f32[128,128]{1,0:T(8,128)S(1)}, f32[8,128]{1,0:T(8,128)S(1)}) custom-call(f32[32,5,128]{2,1,0:T(8,128)S(1)} %all-to-all-done.2.refs_0_, bf16[5888,128]{1,0:T(8,128)(2,1)S(1)} %shard_map.64.refs_1_.pack), custom_call_target="tpu_custom_call" | custom-call | flops 905969664 | bytes 1048576 | tf_op jit(solution)/shard_map/pallas_call | solution.py:53
  66.1 0.2 collective-permute-start.4
  66.4 1.7 %collective-permute-done.4.received = bf16[16,112,128]{2,1,0:T(8,128)(2,1)S(1)} collective-permute-done((bf16[16,112,128]{2,1,0:T(8,128)(2,1)S(1)}, bf16[16,112,128]{2,1,0:T(8,128)(2,1)S(1)}, u32[]{:S(2)}, u32[]{:S(2)}) %collective-permute-start.4) | collective-permute-done | bytes 458784 | tf_op jit(solution)/shard_map/ppermute | solution.py:528
  68.0 0.9 shard_map.66
  68.9 5.8 %all-to-all-start.3 = ((bf16[16,112,128]{2,1,0:T(8,128)(2,1)}), bf16[16,112,128]{2,1,0:T(8,128)(2,1)S(1)}, u32[]{:S(2)}, u32[]{:S(2)}) async-start(bf16[16,112,128]{2,1,0:T(8,128)(2,1)} %shard_map.66), calls=%async_computation.3 | async-start | bytes 917504 | tf_op jit(solution)/shard_map/all_to_all | solution.py:440
  74.8 0.7 collective-permute-start.6
  75.4 2.5 %collective-permute-start.5 = (bf16[8,128,128]{2,1,0:T(8,128)(2,1)S(1)}, bf16[8,128,128]{2,1,0:T(8,128)(2,1)S(1)}, u32[]{:S(2)}, u32[]{:S(2)}) collective-permute-start(bf16[8,128,128]{2,1,0:T(8,128)(2,1)S(1)} %bitcast.12), channel_id=1, source_target_pairs={{0,8},{8,0},{16,24},{24,16},{32,40},{40,32},{48,56},{56,48},{64,72... | collective-permute-start | bytes 786440 | tf_op jit(solution)/shard_map/ppermute | solution.py:26
  77.9 1.1 shard_map.68
  79.0 0.0 copy-start.1
  79.0 10.2 %all-to-all-done.3.refs_0_ = bf16[16,112,128]{2,1,0:T(8,128)(2,1)S(1)} async-done(((bf16[16,112,128]{2,1,0:T(8,128)(2,1)}), bf16[16,112,128]{2,1,0:T(8,128)(2,1)S(1)}, u32[]{:S(2)}, u32[]{:S(2)}) %all-to-all-start.3) | async-done | bytes 458784 | tf_op jit(solution)/shard_map/all_to_all | solution.py:440
  89.2 0.8 shard_map.67
  90.0 0.0 collective-permute-done.6.odd
  90.0 0.0 collective-permute-done.5.even
  90.0 3.4 %all-to-all-start.4 = ((bf16[8,112,128]{2,1,0:T(8,128)(2,1)}), bf16[8,112,128]{2,1,0:T(8,128)(2,1)S(1)}, u32[]{:S(2)}, u32[]{:S(2)}) async-start(bf16[8,112,128]{2,1,0:T(8,128)(2,1)} %shard_map.67), calls=%async_computation.4 | async-start | bytes 458752 | tf_op jit(solution)/shard_map/all_to_all | solution.py:440
  93.4 0.1 collective-permute-start.7
  93.5 1.9 %collective-permute-start.8 = (bf16[3,128,128]{2,1,0:T(8,128)(2,1)S(1)}, bf16[3,128,128]{2,1,0:T(8,128)(2,1)S(1)}, u32[]{:S(2)}, u32[]{:S(2)}) collective-permute-start(bf16[3,128,128]{2,1,0:T(8,128)(2,1)S(1)} %get-tuple-element.55), channel_id=1, source_target_pairs={{1,2},{2,1},{3,4},{4,3},{5,6},{6,5},{9,10},{10,9},{11,12},{12,11},... | collective-permute-start | bytes 294920 | tf_op jit(solution)/shard_map/ppermute | solution.py:26
  95.4 8.0 %all-to-all-done.4.refs_0_ = bf16[8,112,128]{2,1,0:T(8,128)(2,1)S(1)} async-done(((bf16[8,112,128]{2,1,0:T(8,128)(2,1)}), bf16[8,112,128]{2,1,0:T(8,128)(2,1)S(1)}, u32[]{:S(2)}, u32[]{:S(2)}) %all-to-all-start.4) | async-done | bytes 229408 | tf_op jit(solution)/shard_map/all_to_all | solution.py:440
  103.4 0.7 shard_map.69
  104.1 0.0 collective-permute-done.7.even_rows
  104.1 0.0 collective-permute-done.8.odd_rows
  104.1 3.3 %all-to-all-start.5 = ((bf16[4,112,128]{2,1,0:T(8,128)(2,1)}), bf16[4,112,128]{2,1,0:T(8,128)(2,1)S(1)}, u32[]{:S(2)}, u32[]{:S(2)}) async-start(bf16[4,112,128]{2,1,0:T(8,128)(2,1)} %shard_map.69), calls=%async_computation.5 | async-start | bytes 229376 | tf_op jit(solution)/shard_map/all_to_all | solution.py:440
  107.4 0.0 copy-done.1
  107.4 2.6 %shard_map.71 = bf16[1024,128]{1,0:T(8,128)(2,1)} custom-call(bf16[8,128,128]{2,1,0:T(8,128)(2,1)S(1)} %bitcast.14, bf16[8,128,128]{2,1,0:T(8,128)(2,1)S(1)} %collective-permute-done.5.even, bf16[8,128,128]{2,1,0:T(8,128)(2,1)S(1)} %collective-permute-done.6.odd, bf16[3,128,128]{2,1,0:T(8,128)(2,1)S(1)} %collective-permute-done.7.even_rows, ...), custom_call_target="tpu_custom_call" | custom-call | flops 905969664 | bytes 3145728 | tf_op jit(solution)/shard_map/pallas_call | solution.py:53
  110.1 3.2 %all-to-all-done.5 = bf16[4,112,128]{2,1,0:T(8,128)(2,1)S(1)} async-done(((bf16[4,112,128]{2,1,0:T(8,128)(2,1)}), bf16[4,112,128]{2,1,0:T(8,128)(2,1)S(1)}, u32[]{:S(2)}, u32[]{:S(2)}) %all-to-all-start.5) | async-done | bytes 114720 | tf_op jit(solution)/shard_map/all_to_all | solution.py:440
  113.3 0.7 convert.1
  (4 shorter events, 0.1 us)
Async XLA Ops:
  0.6 9.4 %collective-permute-start.1 = (bf16[8,128,128]{2,1,0:T(8,128)(2,1)}, bf16[8,128,128]{2,1,0:T(8,128)(2,1)S(1)}, u32[]{:S(2)}, u32[]{:S(2)}) collective-permute-start(bf16[8,128,128]{2,1,0:T(8,128)(2,1)} %bitcast.16), channel_id=1, source_target_pairs={{8,16},{16,8},{24,32},{32,24},{40,48},{48,40},{56,64},{64,56},{72,... | collective-permute-start | bytes 786440 | tf_op jit(solution)/shard_map/ppermute | solution.py:26
  1.3 11.4 %collective-permute-start = (bf16[8,128,128]{2,1,0:T(8,128)(2,1)}, bf16[8,128,128]{2,1,0:T(8,128)(2,1)S(1)}, u32[]{:S(2)}, u32[]{:S(2)}) collective-permute-start(bf16[8,128,128]{2,1,0:T(8,128)(2,1)} %bitcast.17), channel_id=1, source_target_pairs={{0,8},{8,0},{16,24},{24,16},{32,40},{40,32},{48,56},{56,48},{64,72... | collective-permute-start | bytes 786440 | tf_op jit(solution)/shard_map/ppermute | solution.py:26
  6.5 1.2 %copy-start = (bf16[3,3,3,128,128]{4,3,2,1,0:T(8,128)(2,1)S(1)}, bf16[3,3,3,128,128]{4,3,2,1,0:T(8,128)(2,1)}, u32[]{:S(2)}) copy-start(bf16[3,3,3,128,128]{4,3,2,1,0:T(8,128)(2,1)} %param.4) | copy-start | bytes 2654212
  7.6 0.9 copy-start.2
  8.6 0.9 copy-start.3
  12.7 4.7 %collective-permute-start.2 = (bf16[3,128,128]{2,1,0:T(8,128)(2,1)S(1)}, bf16[3,128,128]{2,1,0:T(8,128)(2,1)S(1)}, u32[]{:S(2)}, u32[]{:S(2)}) collective-permute-start(bf16[3,128,128]{2,1,0:T(8,128)(2,1)S(1)} %get-tuple-element.35), channel_id=1, source_target_pairs={{0,1},{1,0},{2,3},{3,2},{4,5},{5,4},{6,7},{7,6},{8,9},{9,8},{10,11... | collective-permute-start | bytes 294920 | tf_op jit(solution)/shard_map/ppermute | solution.py:26
  12.8 5.9 %collective-permute-start.3 = (bf16[3,128,128]{2,1,0:T(8,128)(2,1)S(1)}, bf16[3,128,128]{2,1,0:T(8,128)(2,1)S(1)}, u32[]{:S(2)}, u32[]{:S(2)}) collective-permute-start(bf16[3,128,128]{2,1,0:T(8,128)(2,1)S(1)} %get-tuple-element.36), channel_id=1, source_target_pairs={{1,2},{2,1},{3,4},{4,3},{5,6},{6,5},{9,10},{10,9},{11,12},{12,11},... | collective-permute-start | bytes 294920 | tf_op jit(solution)/shard_map/ppermute | solution.py:26
  48.6 11.6 %all-to-all-start.2 = ((f32[32,5,128]{2,1,0:T(8,128)}), f32[32,5,128]{2,1,0:T(8,128)S(1)}, u32[]{:S(2)}, u32[]{:S(2)}) async-start(f32[32,5,128]{2,1,0:T(8,128)} %shard_map.63), calls=%async_computation.2 | async-start | bytes 262144 | tf_op jit(solution)/shard_map/all_to_all | solution.py:440
  66.1 1.9 %collective-permute-start.4 = (bf16[16,112,128]{2,1,0:T(8,128)(2,1)S(1)}, bf16[16,112,128]{2,1,0:T(8,128)(2,1)S(1)}, u32[]{:S(2)}, u32[]{:S(2)}) collective-permute-start(bf16[16,112,128]{2,1,0:T(8,128)(2,1)S(1)} %get-tuple-element.45), channel_id=1, source_target_pairs={{0,1},{1,0},{2,3},{3,2},{4,5},{5,4},{6,7},{7,6},{8,9},{9,8},{10,11... | collective-permute-start | bytes 1376264 | tf_op jit(solution)/shard_map/ppermute | solution.py:528
  68.9 20.3 %all-to-all-start.3 = ((bf16[16,112,128]{2,1,0:T(8,128)(2,1)}), bf16[16,112,128]{2,1,0:T(8,128)(2,1)S(1)}, u32[]{:S(2)}, u32[]{:S(2)}) async-start(bf16[16,112,128]{2,1,0:T(8,128)(2,1)} %shard_map.66), calls=%async_computation.3 | async-start | bytes 917504 | tf_op jit(solution)/shard_map/all_to_all | solution.py:440
  74.8 15.2 %collective-permute-start.6 = (bf16[8,128,128]{2,1,0:T(8,128)(2,1)S(1)}, bf16[8,128,128]{2,1,0:T(8,128)(2,1)S(1)}, u32[]{:S(2)}, u32[]{:S(2)}) collective-permute-start(bf16[8,128,128]{2,1,0:T(8,128)(2,1)S(1)} %bitcast.11), channel_id=1, source_target_pairs={{8,16},{16,8},{24,32},{32,24},{40,48},{48,40},{56,64},{64,56},{72,... | collective-permute-start | bytes 786440 | tf_op jit(solution)/shard_map/ppermute | solution.py:26
  75.4 14.5 %collective-permute-start.5 = (bf16[8,128,128]{2,1,0:T(8,128)(2,1)S(1)}, bf16[8,128,128]{2,1,0:T(8,128)(2,1)S(1)}, u32[]{:S(2)}, u32[]{:S(2)}) collective-permute-start(bf16[8,128,128]{2,1,0:T(8,128)(2,1)S(1)} %bitcast.12), channel_id=1, source_target_pairs={{0,8},{8,0},{16,24},{24,16},{32,40},{40,32},{48,56},{56,48},{64,72... | collective-permute-start | bytes 786440 | tf_op jit(solution)/shard_map/ppermute | solution.py:26
  79.0 28.5 %copy-start.1 = (bf16[3,3,3,128,128]{4,3,2,1,0:T(8,128)(2,1)S(1)}, bf16[3,3,3,128,128]{4,3,2,1,0:T(8,128)(2,1)}, u32[]{:S(2)}) copy-start(bf16[3,3,3,128,128]{4,3,2,1,0:T(8,128)(2,1)} %param.4) | copy-start | bytes 2654212
  90.0 13.4 %all-to-all-start.4 = ((bf16[8,112,128]{2,1,0:T(8,128)(2,1)}), bf16[8,112,128]{2,1,0:T(8,128)(2,1)S(1)}, u32[]{:S(2)}, u32[]{:S(2)}) async-start(bf16[8,112,128]{2,1,0:T(8,128)(2,1)} %shard_map.67), calls=%async_computation.4 | async-start | bytes 458752 | tf_op jit(solution)/shard_map/all_to_all | solution.py:440
  93.4 10.7 %collective-permute-start.7 = (bf16[3,128,128]{2,1,0:T(8,128)(2,1)S(1)}, bf16[3,128,128]{2,1,0:T(8,128)(2,1)S(1)}, u32[]{:S(2)}, u32[]{:S(2)}) collective-permute-start(bf16[3,128,128]{2,1,0:T(8,128)(2,1)S(1)} %get-tuple-element.54), channel_id=1, source_target_pairs={{0,1},{1,0},{2,3},{3,2},{4,5},{5,4},{6,7},{7,6},{8,9},{9,8},{10,11... | collective-permute-start | bytes 294920 | tf_op jit(solution)/shard_map/ppermute | solution.py:26
  93.5 10.6 %collective-permute-start.8 = (bf16[3,128,128]{2,1,0:T(8,128)(2,1)S(1)}, bf16[3,128,128]{2,1,0:T(8,128)(2,1)S(1)}, u32[]{:S(2)}, u32[]{:S(2)}) collective-permute-start(bf16[3,128,128]{2,1,0:T(8,128)(2,1)S(1)} %get-tuple-element.55), channel_id=1, source_target_pairs={{1,2},{2,1},{3,4},{4,3},{5,6},{6,5},{9,10},{10,9},{11,12},{12,11},... | collective-permute-start | bytes 294920 | tf_op jit(solution)/shard_map/ppermute | solution.py:26
  104.1 9.2 %all-to-all-start.5 = ((bf16[4,112,128]{2,1,0:T(8,128)(2,1)}), bf16[4,112,128]{2,1,0:T(8,128)(2,1)S(1)}, u32[]{:S(2)}, u32[]{:S(2)}) async-start(bf16[4,112,128]{2,1,0:T(8,128)(2,1)} %shard_map.69), calls=%async_computation.5 | async-start | bytes 229376 | tf_op jit(solution)/shard_map/all_to_all | solution.py:440

commit v8 on v7

--- a/solution.py
+++ b/solution.py
@@ -37,7 +37,7 @@
 def row_swaps(own, even, odd):
     ny = lax.axis_size(GY)
     ends = jax.ShapeDtypeStruct((3,) + own.shape[1:], BF16)
-    first, second = call(ends_kernel, [ends, ends], [], 0, 2**18, own, even, odd)
+    first, second = call(ends_kernel, [ends, ends], [], 24 * 2**30, 2**18, own, even, odd)
     return swapped(first, GY, ny, 0), swapped(second, GY, ny, 1)
 
 
@@ -529,13 +529,12 @@
     parts = call(
         pair_kernel, jax.ShapeDtypeStruct(shape, BF16), [], keep.size, 2**21, keep, received
     )
-    block, whitener, parts = lax.optimization_barrier(
-        (grad_hidden.reshape(rows, columns, channels), whitener, parts)
-    )
+    block = grad_hidden.reshape(rows, columns, channels)
+    whitener, parts = lax.optimization_barrier((whitener, parts))
     whitened = call(white_kernel, flat, [], flops, 2**20, pack, whitener, offset)
     even, odd = plane_swaps(block)
     part = total_copies(exchange(parts, ("y", "x")), levels, BF16)
-    part, even, odd, whitened = lax.optimization_barrier((part, even, odd, whitened))
+    part, whitened = lax.optimization_barrier((part, whitened))
     row_ends = row_swaps(block, even, odd)
     part = total_copies(exchange(part, ("z",)), rows_y, BF16, 1.0 / math.sqrt(voxels))
     part, *row_ends = lax.optimization_barrier((part, *row_ends))

time: 115 us -> 112 us (0.974)
  waiting for transfers between devices: 32.3 us -> 27.5 us
  blocking collectives: 28.6 us -> 33 us
  starting transfers between devices: 32.4 us -> 29.4 us
    all_to_all x4, waiting for transfers between devices: 26.7 us -> 22.3 us  [exchange(): return lax.all_to_all(parts, axes, 0, 0, tiled=True)]
    all_to_all x2, blocking collectives: 28.6 us -> 33 us  [exchange(): return lax.all_to_all(parts, axes, 0, 0, tiled=True)]
    ppermute x8, starting transfers between devices: 13.6 us -> 10.6 us  [swapped(): return lax.ppermute(block, axes, pairs)]
where the time goes in v8:
time: 112 us; the launch traced here: 111 us
  blocking collectives  33 us (29%)
  starting transfers between devices  29.4 us (26%)
  waiting for transfers between devices  27.5 us (25%)
  Pallas kernels  16.1 us (14%)
  local copies, waits for them, and re-layouts  3.08 us (3%)
    all_to_all x2, blocking collectives, exchange(): return lax.all_to_all(parts, axes, 0, 0, tiled=True)  33 us
    all_to_all x4, waiting for transfers between devices, exchange(): return lax.all_to_all(parts, axes, 0, 0, tiled=True)  22.3 us
    all_to_all x4, starting transfers between devices, exchange(): return lax.all_to_all(parts, axes, 0, 0, tiled=True)  18.6 us
    pallas_call x14, Pallas kernels, call(): pl.pallas_call(kernel, out_shape=out_shape, in_specs=[hbm if i in far els...  16.1 us
    ppermute x8, starting transfers between devices, swapped(): return lax.ppermute(block, axes, pairs)  10.6 us
    ppermute x8, waiting for transfers between devices, swapped(): return lax.ppermute(block, axes, pairs)  3.56 us
    unnamed x8, local copies, waits for them, and re-layouts  3.07 us
  transfers between devices with their start and end apart: 13, of which 7 were waited for; matrix products, arithmetic and copies ran while one was open for 0% of the time, Pallas kernels for 7%

profile of v8, /device:TPU:4, one launch (start us, length us, event | category | flops | bytes accessed | tf_op | source)
XLA Modules:
  0.0 110.6 jit_solution(16595785648298362920)
XLA Ops:
  0.6 2.0 %collective-permute-start = (bf16[8,128,128]{2,1,0:T(8,128)(2,1)}, bf16[8,128,128]{2,1,0:T(8,128)(2,1)S(1)}, u32[]{:S(2)}, u32[]{:S(2)}) collective-permute-start(bf16[8,128,128]{2,1,0:T(8,128)(2,1)} %bitcast.12), channel_id=1, source_target_pairs={{0,8},{8,0},{16,24},{24,16},{32,40},{40,32},{48,56},{56,48},{64,72... | collective-permute-start | bytes 786440 | tf_op jit(solution)/shard_map/ppermute | solution.py:26
  2.6 0.7 collective-permute-start.1
  3.3 0.0 copy-start
  3.3 1.2 %copy-done = bf16[3,3,3,128,128]{4,3,2,1,0:T(8,128)(2,1)S(1)} copy-done((bf16[3,3,3,128,128]{4,3,2,1,0:T(8,128)(2,1)S(1)}, bf16[3,3,3,128,128]{4,3,2,1,0:T(8,128)(2,1)}, u32[]{:S(2)}) %copy-start) | copy-done | bytes 884760
  4.5 0.0 copy-start.2
  4.5 0.9 copy-done.2
  5.4 0.0 copy-start.3
  5.4 0.9 copy-done.3
  6.4 0.5 shard_map.58
  6.9 2.3 %collective-permute-done.even = bf16[8,128,128]{2,1,0:T(8,128)(2,1)S(1)} collective-permute-done((bf16[8,128,128]{2,1,0:T(8,128)(2,1)}, bf16[8,128,128]{2,1,0:T(8,128)(2,1)S(1)}, u32[]{:S(2)}, u32[]{:S(2)}) %collective-permute-start) | collective-permute-done | bytes 262176 | tf_op jit(solution)/shard_map/ppermute | solution.py:26
  9.2 0.0 collective-permute-done.1.odd
  9.2 0.1 collective-permute-start.2
  9.3 2.5 %collective-permute-start.3 = (bf16[3,128,128]{2,1,0:T(8,128)(2,1)S(1)}, bf16[3,128,128]{2,1,0:T(8,128)(2,1)S(1)}, u32[]{:S(2)}, u32[]{:S(2)}) collective-permute-start(bf16[3,128,128]{2,1,0:T(8,128)(2,1)S(1)} %get-tuple-element.33), channel_id=1, source_target_pairs={{1,2},{2,1},{3,4},{4,3},{5,6},{6,5},{9,10},{10,9},{11,12},{12,11},... | collective-permute-start | bytes 294920 | tf_op jit(solution)/shard_map/ppermute | solution.py:26
  11.8 2.1 %shard_map.59 = (bf16[1024,128]{1,0:T(8,128)(2,1)S(1)}, f32[256,128]{1,0:T(8,128)S(1)}, f32[128,128]{1,0:T(8,128)S(1)}, f32[8,128]{1,0:T(8,128)S(1)}) custom-call(bf16[8,128,128]{2,1,0:T(8,128)(2,1)S(1)} %get-tuple-element.28.own, bf16[8,128,128]{2,1,0:T(8,128)(2,1)S(1)} %collective-permute-done.even, bf16[8,128,128]{2,1,0:T(8,128)(2,1)S(1)} %collective-permute-done.1.odd, ...), custom_call_target="tpu_custom_call" | custom-call | flops 905969664 | bytes 3145728 | tf_op jit(solution)/shard_map/pallas_call | solution.py:53
  13.9 0.0 collective-permute-done.2.even_rows
  13.9 1.3 %collective-permute-done.3.odd_rows = bf16[3,128,128]{2,1,0:T(8,128)(2,1)S(1)} collective-permute-done((bf16[3,128,128]{2,1,0:T(8,128)(2,1)S(1)}, bf16[3,128,128]{2,1,0:T(8,128)(2,1)S(1)}, u32[]{:S(2)}, u32[]{:S(2)}) %collective-permute-start.3) | collective-permute-done | bytes 98336 | tf_op jit(solution)/shard_map/ppermute | solution.py:26
  15.2 0.5 shard_map.61
  15.7 19.6 %all_to_all.30.refs_0_ = f32[32,5,128]{2,1,0:T(8,128)S(1)} all-to-all(f32[32,5,128]{2,1,0:T(8,128)S(1)} %get-tuple-element.36), channel_id=1, replica_groups=mesh['y'=4,'z'=8,'x'=4,'c'=2] {'y','x','c'}, dimensions={0} | all-to-all | bytes 163840 | tf_op jit(solution)/shard_map/all_to_all | solution.py:440
  35.4 13.4 %all_to_all.31.refs_0_ = f32[8,5,128]{2,1,0:T(8,128)S(1)} all-to-all(f32[8,5,128]{2,1,0:T(8,128)S(1)} %shard_map.62), channel_id=1, replica_groups=mesh['y'=4,'z'=8,'x'=4,'c'=2] {'z'}, dimensions={0} | all-to-all | bytes 40960 | tf_op jit(solution)/shard_map/all_to_all | solution.py:440
  48.8 0.7 shard_map.63
  49.4 6.0 %all-to-all-start.2 = ((f32[32,5,128]{2,1,0:T(8,128)}), f32[32,5,128]{2,1,0:T(8,128)S(1)}, u32[]{:S(2)}, u32[]{:S(2)}) async-start(f32[32,5,128]{2,1,0:T(8,128)} %shard_map.63), calls=%async_computation.2 | async-start | bytes 262144 | tf_op jit(solution)/shard_map/all_to_all | solution.py:440
  55.4 0.4 shard_map.64.refs_1_.pack
  55.8 5.3 %all-to-all-done.2.refs_0_ = f32[32,5,128]{2,1,0:T(8,128)S(1)} async-done(((f32[32,5,128]{2,1,0:T(8,128)}), f32[32,5,128]{2,1,0:T(8,128)S(1)}, u32[]{:S(2)}, u32[]{:S(2)}) %all-to-all-start.2) | async-done | bytes 81952 | tf_op jit(solution)/shard_map/all_to_all | solution.py:440
  61.1 5.9 %shard_map.65 = (bf16[1024,128]{1,0:T(8,128)(2,1)S(1)}, f32[16,112,128]{2,1,0:T(8,128)S(1)}, bf16[16,112,128]{2,1,0:T(8,128)(2,1)S(1)}, f32[128,128]{1,0:T(8,128)S(1)}, f32[8,128]{1,0:T(8,128)S(1)}) custom-call(f32[32,5,128]{2,1,0:T(8,128)S(1)} %all-to-all-done.2.refs_0_, bf16[5888,128]{1,0:T(8,128)(2,1)S(1)} %shard_map.64.refs_1_.pack), custom_call_target="tpu_custom_call" | custom-call | flops 905969664 | bytes 1048576 | tf_op jit(solution)/shard_map/pallas_call | solution.py:53
  67.0 0.2 collective-permute-start.4
  67.2 1.7 %collective-permute-done.4.received = bf16[16,112,128]{2,1,0:T(8,128)(2,1)S(1)} collective-permute-done((bf16[16,112,128]{2,1,0:T(8,128)(2,1)S(1)}, bf16[16,112,128]{2,1,0:T(8,128)(2,1)S(1)}, u32[]{:S(2)}, u32[]{:S(2)}) %collective-permute-start.4) | collective-permute-done | bytes 458784 | tf_op jit(solution)/shard_map/ppermute | solution.py:528
  68.9 0.9 shard_map.66
  69.7 5.8 %all-to-all-start.3 = ((bf16[16,112,128]{2,1,0:T(8,128)(2,1)}), bf16[16,112,128]{2,1,0:T(8,128)(2,1)S(1)}, u32[]{:S(2)}, u32[]{:S(2)}) async-start(bf16[16,112,128]{2,1,0:T(8,128)(2,1)} %shard_map.66), calls=%async_computation.3 | async-start | bytes 917504 | tf_op jit(solution)/shard_map/all_to_all | solution.py:440
  75.6 0.5 collective-permute-start.5
  76.1 0.8 collective-permute-start.6
  76.9 1.1 shard_map.68
  78.0 6.4 %all-to-all-done.3.refs_0_ = bf16[16,112,128]{2,1,0:T(8,128)(2,1)S(1)} async-done(((bf16[16,112,128]{2,1,0:T(8,128)(2,1)}), bf16[16,112,128]{2,1,0:T(8,128)(2,1)S(1)}, u32[]{:S(2)}, u32[]{:S(2)}) %all-to-all-start.3) | async-done | bytes 458784 | tf_op jit(solution)/shard_map/all_to_all | solution.py:440
  84.4 0.8 shard_map.67
  85.2 3.4 %all-to-all-start.4 = ((bf16[8,112,128]{2,1,0:T(8,128)(2,1)}), bf16[8,112,128]{2,1,0:T(8,128)(2,1)S(1)}, u32[]{:S(2)}, u32[]{:S(2)}) async-start(bf16[8,112,128]{2,1,0:T(8,128)(2,1)} %shard_map.67), calls=%async_computation.4 | async-start | bytes 458752 | tf_op jit(solution)/shard_map/all_to_all | solution.py:440
  88.6 0.0 copy-start.1
  88.6 0.0 collective-permute-done.5.even
  88.6 0.0 collective-permute-done.6.odd
  88.6 0.1 collective-permute-start.7
  88.7 3.9 %collective-permute-start.8 = (bf16[3,128,128]{2,1,0:T(8,128)(2,1)S(1)}, bf16[3,128,128]{2,1,0:T(8,128)(2,1)S(1)}, u32[]{:S(2)}, u32[]{:S(2)}) collective-permute-start(bf16[3,128,128]{2,1,0:T(8,128)(2,1)S(1)} %get-tuple-element.49), channel_id=1, source_target_pairs={{1,2},{2,1},{3,4},{4,3},{5,6},{6,5},{9,10},{10,9},{11,12},{12,11},... | collective-permute-start | bytes 294920 | tf_op jit(solution)/shard_map/ppermute | solution.py:26
  92.6 7.4 %all-to-all-done.4.refs_0_ = bf16[8,112,128]{2,1,0:T(8,128)(2,1)S(1)} async-done(((bf16[8,112,128]{2,1,0:T(8,128)(2,1)}), bf16[8,112,128]{2,1,0:T(8,128)(2,1)S(1)}, u32[]{:S(2)}, u32[]{:S(2)}) %all-to-all-start.4) | async-done | bytes 229408 | tf_op jit(solution)/shard_map/all_to_all | solution.py:440
  100.0 0.7 shard_map.69
  100.7 0.0 collective-permute-done.7.even_rows
  100.7 0.0 collective-permute-done.8.odd_rows
  100.7 3.3 %all-to-all-start.5 = ((bf16[4,112,128]{2,1,0:T(8,128)(2,1)}), bf16[4,112,128]{2,1,0:T(8,128)(2,1)S(1)}, u32[]{:S(2)}, u32[]{:S(2)}) async-start(bf16[4,112,128]{2,1,0:T(8,128)(2,1)} %shard_map.69), calls=%async_computation.5 | async-start | bytes 229376 | tf_op jit(solution)/shard_map/all_to_all | solution.py:440
  104.0 0.0 copy-done.1
  104.0 2.6 %shard_map.71 = bf16[1024,128]{1,0:T(8,128)(2,1)} custom-call(bf16[8,128,128]{2,1,0:T(8,128)(2,1)S(1)} %bitcast.18, bf16[8,128,128]{2,1,0:T(8,128)(2,1)S(1)} %collective-permute-done.5.even, bf16[8,128,128]{2,1,0:T(8,128)(2,1)S(1)} %collective-permute-done.6.odd, bf16[3,128,128]{2,1,0:T(8,128)(2,1)S(1)} %collective-permute-done.7.even_rows, ...), custom_call_target="tpu_custom_call" | custom-call | flops 905969664 | bytes 3145728 | tf_op jit(solution)/shard_map/pallas_call | solution.py:53
  106.6 3.2 %all-to-all-done.5 = bf16[4,112,128]{2,1,0:T(8,128)(2,1)S(1)} async-done(((bf16[4,112,128]{2,1,0:T(8,128)(2,1)}), bf16[4,112,128]{2,1,0:T(8,128)(2,1)S(1)}, u32[]{:S(2)}, u32[]{:S(2)}) %all-to-all-start.5) | async-done | bytes 114720 | tf_op jit(solution)/shard_map/all_to_all | solution.py:440
  109.9 0.7 convert.1
  (4 shorter events, 0.1 us)
Async XLA Ops:
  0.6 8.5 %collective-permute-start = (bf16[8,128,128]{2,1,0:T(8,128)(2,1)}, bf16[8,128,128]{2,1,0:T(8,128)(2,1)S(1)}, u32[]{:S(2)}, u32[]{:S(2)}) collective-permute-start(bf16[8,128,128]{2,1,0:T(8,128)(2,1)} %bitcast.12), channel_id=1, source_target_pairs={{0,8},{8,0},{16,24},{24,16},{32,40},{40,32},{48,56},{56,48},{64,72... | collective-permute-start | bytes 786440 | tf_op jit(solution)/shard_map/ppermute | solution.py:26
  2.6 6.5 %collective-permute-start.1 = (bf16[8,128,128]{2,1,0:T(8,128)(2,1)}, bf16[8,128,128]{2,1,0:T(8,128)(2,1)S(1)}, u32[]{:S(2)}, u32[]{:S(2)}) collective-permute-start(bf16[8,128,128]{2,1,0:T(8,128)(2,1)} %bitcast.13), channel_id=1, source_target_pairs={{8,16},{16,8},{24,32},{32,24},{40,48},{48,40},{56,64},{64,56},{72,... | collective-permute-start | bytes 786440 | tf_op jit(solution)/shard_map/ppermute | solution.py:26
  3.3 1.2 %copy-start = (bf16[3,3,3,128,128]{4,3,2,1,0:T(8,128)(2,1)S(1)}, bf16[3,3,3,128,128]{4,3,2,1,0:T(8,128)(2,1)}, u32[]{:S(2)}) copy-start(bf16[3,3,3,128,128]{4,3,2,1,0:T(8,128)(2,1)} %param.4) | copy-start | bytes 2654212
  4.5 0.9 copy-start.2
  5.4 0.9 copy-start.3
  9.2 4.7 %collective-permute-start.2 = (bf16[3,128,128]{2,1,0:T(8,128)(2,1)S(1)}, bf16[3,128,128]{2,1,0:T(8,128)(2,1)S(1)}, u32[]{:S(2)}, u32[]{:S(2)}) collective-permute-start(bf16[3,128,128]{2,1,0:T(8,128)(2,1)S(1)} %get-tuple-element.32), channel_id=1, source_target_pairs={{0,1},{1,0},{2,3},{3,2},{4,5},{5,4},{6,7},{7,6},{8,9},{9,8},{10,11... | collective-permute-start | bytes 294920 | tf_op jit(solution)/shard_map/ppermute | solution.py:26
  9.3 5.9 %collective-permute-start.3 = (bf16[3,128,128]{2,1,0:T(8,128)(2,1)S(1)}, bf16[3,128,128]{2,1,0:T(8,128)(2,1)S(1)}, u32[]{:S(2)}, u32[]{:S(2)}) collective-permute-start(bf16[3,128,128]{2,1,0:T(8,128)(2,1)S(1)} %get-tuple-element.33), channel_id=1, source_target_pairs={{1,2},{2,1},{3,4},{4,3},{5,6},{6,5},{9,10},{10,9},{11,12},{12,11},... | collective-permute-start | bytes 294920 | tf_op jit(solution)/shard_map/ppermute | solution.py:26
  49.4 11.7 %all-to-all-start.2 = ((f32[32,5,128]{2,1,0:T(8,128)}), f32[32,5,128]{2,1,0:T(8,128)S(1)}, u32[]{:S(2)}, u32[]{:S(2)}) async-start(f32[32,5,128]{2,1,0:T(8,128)} %shard_map.63), calls=%async_computation.2 | async-start | bytes 262144 | tf_op jit(solution)/shard_map/all_to_all | solution.py:440
  67.0 1.9 %collective-permute-start.4 = (bf16[16,112,128]{2,1,0:T(8,128)(2,1)S(1)}, bf16[16,112,128]{2,1,0:T(8,128)(2,1)S(1)}, u32[]{:S(2)}, u32[]{:S(2)}) collective-permute-start(bf16[16,112,128]{2,1,0:T(8,128)(2,1)S(1)} %get-tuple-element.41), channel_id=1, source_target_pairs={{0,1},{1,0},{2,3},{3,2},{4,5},{5,4},{6,7},{7,6},{8,9},{9,8},{10,11... | collective-permute-start | bytes 1376264 | tf_op jit(solution)/shard_map/ppermute | solution.py:528
  69.7 14.7 %all-to-all-start.3 = ((bf16[16,112,128]{2,1,0:T(8,128)(2,1)}), bf16[16,112,128]{2,1,0:T(8,128)(2,1)S(1)}, u32[]{:S(2)}, u32[]{:S(2)}) async-start(bf16[16,112,128]{2,1,0:T(8,128)(2,1)} %shard_map.66), calls=%async_computation.3 | async-start | bytes 917504 | tf_op jit(solution)/shard_map/all_to_all | solution.py:440
  75.6 13.0 %collective-permute-start.5 = (bf16[8,128,128]{2,1,0:T(8,128)(2,1)S(1)}, bf16[8,128,128]{2,1,0:T(8,128)(2,1)S(1)}, u32[]{:S(2)}, u32[]{:S(2)}) collective-permute-start(bf16[8,128,128]{2,1,0:T(8,128)(2,1)S(1)} %bitcast.15), channel_id=1, source_target_pairs={{0,8},{8,0},{16,24},{24,16},{32,40},{40,32},{48,56},{56,48},{64,72... | collective-permute-start | bytes 786440 | tf_op jit(solution)/shard_map/ppermute | solution.py:26
  76.1 12.5 %collective-permute-start.6 = (bf16[8,128,128]{2,1,0:T(8,128)(2,1)S(1)}, bf16[8,128,128]{2,1,0:T(8,128)(2,1)S(1)}, u32[]{:S(2)}, u32[]{:S(2)}) collective-permute-start(bf16[8,128,128]{2,1,0:T(8,128)(2,1)S(1)} %bitcast.16), channel_id=1, source_target_pairs={{8,16},{16,8},{24,32},{32,24},{40,48},{48,40},{56,64},{64,56},{72,... | collective-permute-start | bytes 786440 | tf_op jit(solution)/shard_map/ppermute | solution.py:26
  85.2 14.8 %all-to-all-start.4 = ((bf16[8,112,128]{2,1,0:T(8,128)(2,1)}), bf16[8,112,128]{2,1,0:T(8,128)(2,1)S(1)}, u32[]{:S(2)}, u32[]{:S(2)}) async-start(bf16[8,112,128]{2,1,0:T(8,128)(2,1)} %shard_map.67), calls=%async_computation.4 | async-start | bytes 458752 | tf_op jit(solution)/shard_map/all_to_all | solution.py:440
  88.6 15.4 %copy-start.1 = (bf16[3,3,3,128,128]{4,3,2,1,0:T(8,128)(2,1)S(1)}, bf16[3,3,3,128,128]{4,3,2,1,0:T(8,128)(2,1)}, u32[]{:S(2)}) copy-start(bf16[3,3,3,128,128]{4,3,2,1,0:T(8,128)(2,1)} %param.4) | copy-start | bytes 2654212
  88.6 12.0 %collective-permute-start.7 = (bf16[3,128,128]{2,1,0:T(8,128)(2,1)S(1)}, bf16[3,128,128]{2,1,0:T(8,128)(2,1)S(1)}, u32[]{:S(2)}, u32[]{:S(2)}) collective-permute-start(bf16[3,128,128]{2,1,0:T(8,128)(2,1)S(1)} %get-tuple-element.48), channel_id=1, source_target_pairs={{0,1},{1,0},{2,3},{3,2},{4,5},{5,4},{6,7},{7,6},{8,9},{9,8},{10,11... | collective-permute-start | bytes 294920 | tf_op jit(solution)/shard_map/ppermute | solution.py:26
  88.7 11.9 %collective-permute-start.8 = (bf16[3,128,128]{2,1,0:T(8,128)(2,1)S(1)}, bf16[3,128,128]{2,1,0:T(8,128)(2,1)S(1)}, u32[]{:S(2)}, u32[]{:S(2)}) collective-permute-start(bf16[3,128,128]{2,1,0:T(8,128)(2,1)S(1)} %get-tuple-element.49), channel_id=1, source_target_pairs={{1,2},{2,1},{3,4},{4,3},{5,6},{6,5},{9,10},{10,9},{11,12},{12,11},... | collective-permute-start | bytes 294920 | tf_op jit(solution)/shard_map/ppermute | solution.py:26
  100.7 9.2 %all-to-all-start.5 = ((bf16[4,112,128]{2,1,0:T(8,128)(2,1)}), bf16[4,112,128]{2,1,0:T(8,128)(2,1)S(1)}, u32[]{:S(2)}, u32[]{:S(2)}) async-start(bf16[4,112,128]{2,1,0:T(8,128)(2,1)} %shard_map.69), calls=%async_computation.5 | async-start | bytes 229376 | tf_op jit(solution)/shard_map/all_to_all | solution.py:440

commit v9 on v8

--- a/solution.py
+++ b/solution.py
@@ -150,7 +150,7 @@
 
 
 def conv_kernel(
-    own, even, odd, kernel_wide, target,
+    own, odd, even, kernel_wide, target,
     hidden_out, ends_out, moments_out, sums_out, wide, none,
 ):
     rows, columns, channels = own.shape
@@ -171,7 +171,7 @@
 
 
 def finish_kernel(
-    totals, even_rows, odd_rows, kernel_wide, target, moments_in, sums,
+    totals, odd_rows, even_rows, kernel_wide, target, moments_in, sums,
     hidden_out, sheet_out, ends,
 ):
     _, columns, channels = even_rows.shape
@@ -484,7 +484,7 @@
             jax.ShapeDtypeStruct((8, channels), F32),
         ],
         [wide, pltpu.VMEM((2, 1, columns, channels), BF16)],
-        flops, 3 * 2**20, near, even, odd, kernel_wide, target_near,
+        flops, 3 * 2**20, near, odd, even, kernel_wide, target_near,
     )
     hidden_ends, sheet = call(
         finish_kernel,
@@ -494,7 +494,7 @@
         ],
         [ends],
         flops // 12, 2**20,
-        totals, even_rows, odd_rows, kernel_wide, target_near, moments_here, sums_here,
+        totals, odd_rows, even_rows, kernel_wide, target_near, moments_here, sums_here,
     )
     flat = jax.ShapeDtypeStruct((count, channels), BF16)
     pack = call(

time: 112 us -> 111 us (level)
  blocking collectives: 33 us -> 28.5 us
  starting transfers between devices: 29.4 us -> 33.2 us
    all_to_all x2, blocking collectives: 33 us -> 28.5 us  [exchange(): return lax.all_to_all(parts, axes, 0, 0, tiled=True)]
    ppermute x8, starting transfers between devices: 10.6 us -> 14.5 us  [swapped(): return lax.ppermute(block, axes, pairs)]
where the time goes in v9:
time: 111 us; the launch traced here: 110 us
  starting transfers between devices  33.2 us (30%)
  blocking collectives  28.5 us (26%)
  waiting for transfers between devices  27.1 us (24%)
  Pallas kernels  16.1 us (15%)
  local copies, waits for them, and re-layouts  3.08 us (3%)
    all_to_all x2, blocking collectives, exchange(): return lax.all_to_all(parts, axes, 0, 0, tiled=True)  28.5 us
    all_to_all x4, waiting for transfers between devices, exchange(): return lax.all_to_all(parts, axes, 0, 0, tiled=True)  22.3 us
    all_to_all x4, starting transfers between devices, exchange(): return lax.all_to_all(parts, axes, 0, 0, tiled=True)  18.6 us
    pallas_call x14, Pallas kernels, call(): pl.pallas_call(kernel, out_shape=out_shape, in_specs=[hbm if i in far els...  16.1 us
    ppermute x8, starting transfers between devices, swapped(): return lax.ppermute(block, axes, pairs)  14.5 us
    ppermute x8, waiting for transfers between devices, swapped(): return lax.ppermute(block, axes, pairs)  3.19 us
    unnamed x8, local copies, waits for them, and re-layouts  3.07 us
  transfers between devices with their start and end apart: 13, of which 7 were waited for; matrix products, arithmetic and copies ran while one was open for 0% of the time, Pallas kernels for 7%

profile of v9, /device:TPU:4, one launch (start us, length us, event | category | flops | bytes accessed | tf_op | source)
XLA Modules:
  0.0 109.6 jit_solution(8270216427577343395)
XLA Ops:
  0.6 0.7 collective-permute-start
  1.3 5.2 %collective-permute-start.1 = (bf16[8,128,128]{2,1,0:T(8,128)(2,1)}, bf16[8,128,128]{2,1,0:T(8,128)(2,1)S(1)}, u32[]{:S(2)}, u32[]{:S(2)}) collective-permute-start(bf16[8,128,128]{2,1,0:T(8,128)(2,1)} %bitcast.13), channel_id=1, source_target_pairs={{0,8},{8,0},{16,24},{24,16},{32,40},{40,32},{48,56},{56,48},{64,72... | collective-permute-start | bytes 786440 | tf_op jit(solution)/shard_map/ppermute | solution.py:26
  6.5 0.0 copy-start
  6.5 1.2 %copy-done = bf16[3,3,3,128,128]{4,3,2,1,0:T(8,128)(2,1)S(1)} copy-done((bf16[3,3,3,128,128]{4,3,2,1,0:T(8,128)(2,1)S(1)}, bf16[3,3,3,128,128]{4,3,2,1,0:T(8,128)(2,1)}, u32[]{:S(2)}) %copy-start) | copy-done | bytes 884760
  7.6 0.0 copy-start.2
  7.6 0.9 copy-done.2
  8.6 0.0 copy-start.3
  8.6 0.9 copy-done.3
  9.5 0.5 shard_map.58
  10.1 0.0 collective-permute-done.odd
  10.1 2.6 %collective-permute-done.1.even = bf16[8,128,128]{2,1,0:T(8,128)(2,1)S(1)} collective-permute-done((bf16[8,128,128]{2,1,0:T(8,128)(2,1)}, bf16[8,128,128]{2,1,0:T(8,128)(2,1)S(1)}, u32[]{:S(2)}, u32[]{:S(2)}) %collective-permute-start.1) | collective-permute-done | bytes 262176 | tf_op jit(solution)/shard_map/ppermute | solution.py:26
  12.7 1.9 %collective-permute-start.2 = (bf16[3,128,128]{2,1,0:T(8,128)(2,1)S(1)}, bf16[3,128,128]{2,1,0:T(8,128)(2,1)S(1)}, u32[]{:S(2)}, u32[]{:S(2)}) collective-permute-start(bf16[3,128,128]{2,1,0:T(8,128)(2,1)S(1)} %get-tuple-element.32), channel_id=1, source_target_pairs={{1,2},{2,1},{3,4},{4,3},{5,6},{6,5},{9,10},{10,9},{11,12},{12,11},... | collective-permute-start | bytes 294920 | tf_op jit(solution)/shard_map/ppermute | solution.py:26
  14.6 1.4 %collective-permute-start.3 = (bf16[3,128,128]{2,1,0:T(8,128)(2,1)S(1)}, bf16[3,128,128]{2,1,0:T(8,128)(2,1)S(1)}, u32[]{:S(2)}, u32[]{:S(2)}) collective-permute-start(bf16[3,128,128]{2,1,0:T(8,128)(2,1)S(1)} %get-tuple-element.33), channel_id=1, source_target_pairs={{0,1},{1,0},{2,3},{3,2},{4,5},{5,4},{6,7},{7,6},{8,9},{9,8},{10,11... | collective-permute-start | bytes 294920 | tf_op jit(solution)/shard_map/ppermute | solution.py:26
  16.0 2.1 %shard_map.59 = (bf16[1024,128]{1,0:T(8,128)(2,1)S(1)}, f32[256,128]{1,0:T(8,128)S(1)}, f32[128,128]{1,0:T(8,128)S(1)}, f32[8,128]{1,0:T(8,128)S(1)}) custom-call(bf16[8,128,128]{2,1,0:T(8,128)(2,1)S(1)} %get-tuple-element.28.own, bf16[8,128,128]{2,1,0:T(8,128)(2,1)S(1)} %collective-permute-done.odd, bf16[8,128,128]{2,1,0:T(8,128)(2,1)S(1)} %collective-permute-done.1.even, ...), custom_call_target="tpu_custom_call" | custom-call | flops 905969664 | bytes 3145728 | tf_op jit(solution)/shard_map/pallas_call | solution.py:53
  18.1 0.5 collective-permute-done.2.odd_rows
  18.7 0.0 collective-permute-done.3.even_rows
  18.7 0.5 shard_map.61
  19.2 16.7 %all_to_all.30.refs_0_ = f32[32,5,128]{2,1,0:T(8,128)S(1)} all-to-all(f32[32,5,128]{2,1,0:T(8,128)S(1)} %get-tuple-element.36), channel_id=1, replica_groups=mesh['y'=4,'z'=8,'x'=4,'c'=2] {'y','x','c'}, dimensions={0} | all-to-all | bytes 163840 | tf_op jit(solution)/shard_map/all_to_all | solution.py:440
  36.0 11.8 %all_to_all.31.refs_0_ = f32[8,5,128]{2,1,0:T(8,128)S(1)} all-to-all(f32[8,5,128]{2,1,0:T(8,128)S(1)} %shard_map.62), channel_id=1, replica_groups=mesh['y'=4,'z'=8,'x'=4,'c'=2] {'z'}, dimensions={0} | all-to-all | bytes 40960 | tf_op jit(solution)/shard_map/all_to_all | solution.py:440
  47.8 0.7 shard_map.63
  48.4 6.0 %all-to-all-start.2 = ((f32[32,5,128]{2,1,0:T(8,128)}), f32[32,5,128]{2,1,0:T(8,128)S(1)}, u32[]{:S(2)}, u32[]{:S(2)}) async-start(f32[32,5,128]{2,1,0:T(8,128)} %shard_map.63), calls=%async_computation.2 | async-start | bytes 262144 | tf_op jit(solution)/shard_map/all_to_all | solution.py:440
  54.4 0.4 shard_map.64.refs_1_.pack
  54.8 5.3 %all-to-all-done.2.refs_0_ = f32[32,5,128]{2,1,0:T(8,128)S(1)} async-done(((f32[32,5,128]{2,1,0:T(8,128)}), f32[32,5,128]{2,1,0:T(8,128)S(1)}, u32[]{:S(2)}, u32[]{:S(2)}) %all-to-all-start.2) | async-done | bytes 81952 | tf_op jit(solution)/shard_map/all_to_all | solution.py:440
  60.1 5.9 %shard_map.65 = (bf16[1024,128]{1,0:T(8,128)(2,1)S(1)}, f32[16,112,128]{2,1,0:T(8,128)S(1)}, bf16[16,112,128]{2,1,0:T(8,128)(2,1)S(1)}, f32[128,128]{1,0:T(8,128)S(1)}, f32[8,128]{1,0:T(8,128)S(1)}) custom-call(f32[32,5,128]{2,1,0:T(8,128)S(1)} %all-to-all-done.2.refs_0_, bf16[5888,128]{1,0:T(8,128)(2,1)S(1)} %shard_map.64.refs_1_.pack), custom_call_target="tpu_custom_call" | custom-call | flops 905969664 | bytes 1048576 | tf_op jit(solution)/shard_map/pallas_call | solution.py:53
  66.0 0.2 collective-permute-start.4
  66.2 1.7 %collective-permute-done.4.received = bf16[16,112,128]{2,1,0:T(8,128)(2,1)S(1)} collective-permute-done((bf16[16,112,128]{2,1,0:T(8,128)(2,1)S(1)}, bf16[16,112,128]{2,1,0:T(8,128)(2,1)S(1)}, u32[]{:S(2)}, u32[]{:S(2)}) %collective-permute-start.4) | collective-permute-done | bytes 458784 | tf_op jit(solution)/shard_map/ppermute | solution.py:528
  67.9 0.9 shard_map.66
  68.7 5.8 %all-to-all-start.3 = ((bf16[16,112,128]{2,1,0:T(8,128)(2,1)}), bf16[16,112,128]{2,1,0:T(8,128)(2,1)S(1)}, u32[]{:S(2)}, u32[]{:S(2)}) async-start(bf16[16,112,128]{2,1,0:T(8,128)(2,1)} %shard_map.66), calls=%async_computation.3 | async-start | bytes 917504 | tf_op jit(solution)/shard_map/all_to_all | solution.py:440
  74.6 0.5 collective-permute-start.5
  75.1 0.8 collective-permute-start.6
  75.9 1.1 shard_map.68
  77.0 6.4 %all-to-all-done.3.refs_0_ = bf16[16,112,128]{2,1,0:T(8,128)(2,1)S(1)} async-done(((bf16[16,112,128]{2,1,0:T(8,128)(2,1)}), bf16[16,112,128]{2,1,0:T(8,128)(2,1)S(1)}, u32[]{:S(2)}, u32[]{:S(2)}) %all-to-all-start.3) | async-done | bytes 458784 | tf_op jit(solution)/shard_map/all_to_all | solution.py:440
  83.4 0.8 shard_map.67
  84.2 3.4 %all-to-all-start.4 = ((bf16[8,112,128]{2,1,0:T(8,128)(2,1)}), bf16[8,112,128]{2,1,0:T(8,128)(2,1)S(1)}, u32[]{:S(2)}, u32[]{:S(2)}) async-start(bf16[8,112,128]{2,1,0:T(8,128)(2,1)} %shard_map.67), calls=%async_computation.4 | async-start | bytes 458752 | tf_op jit(solution)/shard_map/all_to_all | solution.py:440
  87.6 0.0 copy-start.1
  87.6 0.0 collective-permute-done.5.even
  87.6 0.0 collective-permute-done.6.odd
  87.6 0.1 collective-permute-start.7
  87.7 3.9 %collective-permute-start.8 = (bf16[3,128,128]{2,1,0:T(8,128)(2,1)S(1)}, bf16[3,128,128]{2,1,0:T(8,128)(2,1)S(1)}, u32[]{:S(2)}, u32[]{:S(2)}) collective-permute-start(bf16[3,128,128]{2,1,0:T(8,128)(2,1)S(1)} %get-tuple-element.49), channel_id=1, source_target_pairs={{1,2},{2,1},{3,4},{4,3},{5,6},{6,5},{9,10},{10,9},{11,12},{12,11},... | collective-permute-start | bytes 294920 | tf_op jit(solution)/shard_map/ppermute | solution.py:26
  91.6 7.4 %all-to-all-done.4.refs_0_ = bf16[8,112,128]{2,1,0:T(8,128)(2,1)S(1)} async-done(((bf16[8,112,128]{2,1,0:T(8,128)(2,1)}), bf16[8,112,128]{2,1,0:T(8,128)(2,1)S(1)}, u32[]{:S(2)}, u32[]{:S(2)}) %all-to-all-start.4) | async-done | bytes 229408 | tf_op jit(solution)/shard_map/all_to_all | solution.py:440
  99.0 0.7 shard_map.69
  99.7 0.0 collective-permute-done.7.even_rows
  99.7 0.0 collective-permute-done.8.odd_rows
  99.7 3.3 %all-to-all-start.5 = ((bf16[4,112,128]{2,1,0:T(8,128)(2,1)}), bf16[4,112,128]{2,1,0:T(8,128)(2,1)S(1)}, u32[]{:S(2)}, u32[]{:S(2)}) async-start(bf16[4,112,128]{2,1,0:T(8,128)(2,1)} %shard_map.69), calls=%async_computation.5 | async-start | bytes 229376 | tf_op jit(solution)/shard_map/all_to_all | solution.py:440
  103.0 0.0 copy-done.1
  103.0 2.6 %shard_map.71 = bf16[1024,128]{1,0:T(8,128)(2,1)} custom-call(bf16[8,128,128]{2,1,0:T(8,128)(2,1)S(1)} %bitcast.18, bf16[8,128,128]{2,1,0:T(8,128)(2,1)S(1)} %collective-permute-done.5.even, bf16[8,128,128]{2,1,0:T(8,128)(2,1)S(1)} %collective-permute-done.6.odd, bf16[3,128,128]{2,1,0:T(8,128)(2,1)S(1)} %collective-permute-done.7.even_rows, ...), custom_call_target="tpu_custom_call" | custom-call | flops 905969664 | bytes 3145728 | tf_op jit(solution)/shard_map/pallas_call | solution.py:53
  105.6 3.2 %all-to-all-done.5 = bf16[4,112,128]{2,1,0:T(8,128)(2,1)S(1)} async-done(((bf16[4,112,128]{2,1,0:T(8,128)(2,1)}), bf16[4,112,128]{2,1,0:T(8,128)(2,1)S(1)}, u32[]{:S(2)}, u32[]{:S(2)}) %all-to-all-start.5) | async-done | bytes 114720 | tf_op jit(solution)/shard_map/all_to_all | solution.py:440
  108.9 0.7 convert.1
  (4 shorter events, 0.1 us)
Async XLA Ops:
  0.6 9.4 %collective-permute-start = (bf16[8,128,128]{2,1,0:T(8,128)(2,1)}, bf16[8,128,128]{2,1,0:T(8,128)(2,1)S(1)}, u32[]{:S(2)}, u32[]{:S(2)}) collective-permute-start(bf16[8,128,128]{2,1,0:T(8,128)(2,1)} %bitcast.12), channel_id=1, source_target_pairs={{8,16},{16,8},{24,32},{32,24},{40,48},{48,40},{56,64},{64,56},{72,... | collective-permute-start | bytes 786440 | tf_op jit(solution)/shard_map/ppermute | solution.py:26
  1.3 11.4 %collective-permute-start.1 = (bf16[8,128,128]{2,1,0:T(8,128)(2,1)}, bf16[8,128,128]{2,1,0:T(8,128)(2,1)S(1)}, u32[]{:S(2)}, u32[]{:S(2)}) collective-permute-start(bf16[8,128,128]{2,1,0:T(8,128)(2,1)} %bitcast.13), channel_id=1, source_target_pairs={{0,8},{8,0},{16,24},{24,16},{32,40},{40,32},{48,56},{56,48},{64,72... | collective-permute-start | bytes 786440 | tf_op jit(solution)/shard_map/ppermute | solution.py:26
  6.5 1.2 %copy-start = (bf16[3,3,3,128,128]{4,3,2,1,0:T(8,128)(2,1)S(1)}, bf16[3,3,3,128,128]{4,3,2,1,0:T(8,128)(2,1)}, u32[]{:S(2)}) copy-start(bf16[3,3,3,128,128]{4,3,2,1,0:T(8,128)(2,1)} %param.4) | copy-start | bytes 2654212
  7.6 0.9 copy-start.2
  8.6 0.9 copy-start.3
  12.7 5.9 %collective-permute-start.2 = (bf16[3,128,128]{2,1,0:T(8,128)(2,1)S(1)}, bf16[3,128,128]{2,1,0:T(8,128)(2,1)S(1)}, u32[]{:S(2)}, u32[]{:S(2)}) collective-permute-start(bf16[3,128,128]{2,1,0:T(8,128)(2,1)S(1)} %get-tuple-element.32), channel_id=1, source_target_pairs={{1,2},{2,1},{3,4},{4,3},{5,6},{6,5},{9,10},{10,9},{11,12},{12,11},... | collective-permute-start | bytes 294920 | tf_op jit(solution)/shard_map/ppermute | solution.py:26
  14.6 4.0 %collective-permute-start.3 = (bf16[3,128,128]{2,1,0:T(8,128)(2,1)S(1)}, bf16[3,128,128]{2,1,0:T(8,128)(2,1)S(1)}, u32[]{:S(2)}, u32[]{:S(2)}) collective-permute-start(bf16[3,128,128]{2,1,0:T(8,128)(2,1)S(1)} %get-tuple-element.33), channel_id=1, source_target_pairs={{0,1},{1,0},{2,3},{3,2},{4,5},{5,4},{6,7},{7,6},{8,9},{9,8},{10,11... | collective-permute-start | bytes 294920 | tf_op jit(solution)/shard_map/ppermute | solution.py:26
  48.4 11.6 %all-to-all-start.2 = ((f32[32,5,128]{2,1,0:T(8,128)}), f32[32,5,128]{2,1,0:T(8,128)S(1)}, u32[]{:S(2)}, u32[]{:S(2)}) async-start(f32[32,5,128]{2,1,0:T(8,128)} %shard_map.63), calls=%async_computation.2 | async-start | bytes 262144 | tf_op jit(solution)/shard_map/all_to_all | solution.py:440
  66.0 1.9 %collective-permute-start.4 = (bf16[16,112,128]{2,1,0:T(8,128)(2,1)S(1)}, bf16[16,112,128]{2,1,0:T(8,128)(2,1)S(1)}, u32[]{:S(2)}, u32[]{:S(2)}) collective-permute-start(bf16[16,112,128]{2,1,0:T(8,128)(2,1)S(1)} %get-tuple-element.41), channel_id=1, source_target_pairs={{0,1},{1,0},{2,3},{3,2},{4,5},{5,4},{6,7},{7,6},{8,9},{9,8},{10,11... | collective-permute-start | bytes 1376264 | tf_op jit(solution)/shard_map/ppermute | solution.py:528
  68.7 14.7 %all-to-all-start.3 = ((bf16[16,112,128]{2,1,0:T(8,128)(2,1)}), bf16[16,112,128]{2,1,0:T(8,128)(2,1)S(1)}, u32[]{:S(2)}, u32[]{:S(2)}) async-start(bf16[16,112,128]{2,1,0:T(8,128)(2,1)} %shard_map.66), calls=%async_computation.3 | async-start | bytes 917504 | tf_op jit(solution)/shard_map/all_to_all | solution.py:440
  74.6 13.0 %collective-permute-start.5 = (bf16[8,128,128]{2,1,0:T(8,128)(2,1)S(1)}, bf16[8,128,128]{2,1,0:T(8,128)(2,1)S(1)}, u32[]{:S(2)}, u32[]{:S(2)}) collective-permute-start(bf16[8,128,128]{2,1,0:T(8,128)(2,1)S(1)} %bitcast.15), channel_id=1, source_target_pairs={{0,8},{8,0},{16,24},{24,16},{32,40},{40,32},{48,56},{56,48},{64,72... | collective-permute-start | bytes 786440 | tf_op jit(solution)/shard_map/ppermute | solution.py:26
  75.1 12.5 %collective-permute-start.6 = (bf16[8,128,128]{2,1,0:T(8,128)(2,1)S(1)}, bf16[8,128,128]{2,1,0:T(8,128)(2,1)S(1)}, u32[]{:S(2)}, u32[]{:S(2)}) collective-permute-start(bf16[8,128,128]{2,1,0:T(8,128)(2,1)S(1)} %bitcast.16), channel_id=1, source_target_pairs={{8,16},{16,8},{24,32},{32,24},{40,48},{48,40},{56,64},{64,56},{72,... | collective-permute-start | bytes 786440 | tf_op jit(solution)/shard_map/ppermute | solution.py:26
  84.2 14.8 %all-to-all-start.4 = ((bf16[8,112,128]{2,1,0:T(8,128)(2,1)}), bf16[8,112,128]{2,1,0:T(8,128)(2,1)S(1)}, u32[]{:S(2)}, u32[]{:S(2)}) async-start(bf16[8,112,128]{2,1,0:T(8,128)(2,1)} %shard_map.67), calls=%async_computation.4 | async-start | bytes 458752 | tf_op jit(solution)/shard_map/all_to_all | solution.py:440
  87.6 15.4 %copy-start.1 = (bf16[3,3,3,128,128]{4,3,2,1,0:T(8,128)(2,1)S(1)}, bf16[3,3,3,128,128]{4,3,2,1,0:T(8,128)(2,1)}, u32[]{:S(2)}) copy-start(bf16[3,3,3,128,128]{4,3,2,1,0:T(8,128)(2,1)} %param.4) | copy-start | bytes 2654212
  87.6 12.0 %collective-permute-start.7 = (bf16[3,128,128]{2,1,0:T(8,128)(2,1)S(1)}, bf16[3,128,128]{2,1,0:T(8,128)(2,1)S(1)}, u32[]{:S(2)}, u32[]{:S(2)}) collective-permute-start(bf16[3,128,128]{2,1,0:T(8,128)(2,1)S(1)} %get-tuple-element.48), channel_id=1, source_target_pairs={{0,1},{1,0},{2,3},{3,2},{4,5},{5,4},{6,7},{7,6},{8,9},{9,8},{10,11... | collective-permute-start | bytes 294920 | tf_op jit(solution)/shard_map/ppermute | solution.py:26
  87.7 11.9 %collective-permute-start.8 = (bf16[3,128,128]{2,1,0:T(8,128)(2,1)S(1)}, bf16[3,128,128]{2,1,0:T(8,128)(2,1)S(1)}, u32[]{:S(2)}, u32[]{:S(2)}) collective-permute-start(bf16[3,128,128]{2,1,0:T(8,128)(2,1)S(1)} %get-tuple-element.49), channel_id=1, source_target_pairs={{1,2},{2,1},{3,4},{4,3},{5,6},{6,5},{9,10},{10,9},{11,12},{12,11},... | collective-permute-start | bytes 294920 | tf_op jit(solution)/shard_map/ppermute | solution.py:26
  99.7 9.2 %all-to-all-start.5 = ((bf16[4,112,128]{2,1,0:T(8,128)(2,1)}), bf16[4,112,128]{2,1,0:T(8,128)(2,1)S(1)}, u32[]{:S(2)}, u32[]{:S(2)}) async-start(bf16[4,112,128]{2,1,0:T(8,128)(2,1)} %shard_map.69), calls=%async_computation.5 | async-start | bytes 229376 | tf_op jit(solution)/shard_map/all_to_all | solution.py:440

commit v10 on v9

--- a/solution.py
+++ b/solution.py
@@ -406,7 +406,7 @@
 
 
 def input_kernel(
-    own, even, odd, even_rows, odd_rows, weight, grad_out, wide, ends, kernel_wide
+    own, even, odd, odd_rows, even_rows, weight, grad_out, wide, ends, kernel_wide
 ):
     rows, columns, channels = own.shape
     gather_rows(even_rows, odd_rows, ends)
@@ -537,12 +537,13 @@
     part, whitened = lax.optimization_barrier((part, whitened))
     row_ends = row_swaps(block, even, odd)
     part = total_copies(exchange(part, ("z",)), rows_y, BF16, 1.0 / math.sqrt(voxels))
-    part, *row_ends = lax.optimization_barrier((part, *row_ends))
+    odd_rows, even_rows, part = lax.optimization_barrier((row_ends[1], row_ends[0], part))
+    row_ends = (even_rows, odd_rows)
     whole = exchange(part, ("y",))
     weight_grad = whole.reshape(rows_y * taps_each, share, channels)[:27].astype(F32)
     weight_grad = weight_grad.reshape(3, 3, 3, share, channels)
 
-    planes = [block, even, odd, *row_ends]
+    planes = [block, even, odd, *row_ends[::-1]]
     input_grad = call(
         input_kernel,
         jax.ShapeDtypeStruct((count, channels), BF16),

time: 111 us -> 111 us (level)
  no operation moved by 1% of the time
where the time goes in v10:
time: 111 us; the launch traced here: 110 us
  starting transfers between devices  32.7 us (29%)
  blocking collectives  28.5 us (26%)
  waiting for transfers between devices  27.7 us (25%)
  Pallas kernels  16.1 us (15%)
  local copies, waits for them, and re-layouts  3.08 us (3%)
    all_to_all x2, blocking collectives, exchange(): return lax.all_to_all(parts, axes, 0, 0, tiled=True)  28.5 us
    all_to_all x4, waiting for transfers between devices, exchange(): return lax.all_to_all(parts, axes, 0, 0, tiled=True)  22.8 us
    all_to_all x4, starting transfers between devices, exchange(): return lax.all_to_all(parts, axes, 0, 0, tiled=True)  18.6 us
    pallas_call x14, Pallas kernels, call(): pl.pallas_call(kernel, out_shape=out_shape, in_specs=[hbm if i in far els...  16.1 us
    ppermute x8, starting transfers between devices, swapped(): return lax.ppermute(block, axes, pairs)  13.9 us
    ppermute x8, waiting for transfers between devices, swapped(): return lax.ppermute(block, axes, pairs)  3.19 us
    unnamed x8, local copies, waits for them, and re-layouts  3.07 us
  transfers between devices with their start and end apart: 13, of which 7 were waited for; matrix products, arithmetic and copies ran while one was open for 0% of the time, Pallas kernels for 7%

profile of v10, /device:TPU:4, one launch (start us, length us, event | category | flops | bytes accessed | tf_op | source)
XLA Modules:
  0.0 109.6 jit_solution(3020350146335743448)
XLA Ops:
  0.6 0.7 collective-permute-start
  1.3 5.2 %collective-permute-start.1 = (bf16[8,128,128]{2,1,0:T(8,128)(2,1)}, bf16[8,128,128]{2,1,0:T(8,128)(2,1)S(1)}, u32[]{:S(2)}, u32[]{:S(2)}) collective-permute-start(bf16[8,128,128]{2,1,0:T(8,128)(2,1)} %bitcast.13), channel_id=1, source_target_pairs={{0,8},{8,0},{16,24},{24,16},{32,40},{40,32},{48,56},{56,48},{64,72... | collective-permute-start | bytes 786440 | tf_op jit(solution)/shard_map/ppermute | solution.py:26
  6.5 0.0 copy-start
  6.5 1.2 %copy-done = bf16[3,3,3,128,128]{4,3,2,1,0:T(8,128)(2,1)S(1)} copy-done((bf16[3,3,3,128,128]{4,3,2,1,0:T(8,128)(2,1)S(1)}, bf16[3,3,3,128,128]{4,3,2,1,0:T(8,128)(2,1)}, u32[]{:S(2)}) %copy-start) | copy-done | bytes 884760
  7.6 0.0 copy-start.2
  7.6 0.9 copy-done.2
  8.6 0.0 copy-start.3
  8.6 0.9 copy-done.3
  9.5 0.5 shard_map.58
  10.1 0.0 collective-permute-done.odd
  10.1 2.6 %collective-permute-done.1.even = bf16[8,128,128]{2,1,0:T(8,128)(2,1)S(1)} collective-permute-done((bf16[8,128,128]{2,1,0:T(8,128)(2,1)}, bf16[8,128,128]{2,1,0:T(8,128)(2,1)S(1)}, u32[]{:S(2)}, u32[]{:S(2)}) %collective-permute-start.1) | collective-permute-done | bytes 262176 | tf_op jit(solution)/shard_map/ppermute | solution.py:26
  12.7 1.9 %collective-permute-start.2 = (bf16[3,128,128]{2,1,0:T(8,128)(2,1)S(1)}, bf16[3,128,128]{2,1,0:T(8,128)(2,1)S(1)}, u32[]{:S(2)}, u32[]{:S(2)}) collective-permute-start(bf16[3,128,128]{2,1,0:T(8,128)(2,1)S(1)} %get-tuple-element.32), channel_id=1, source_target_pairs={{1,2},{2,1},{3,4},{4,3},{5,6},{6,5},{9,10},{10,9},{11,12},{12,11},... | collective-permute-start | bytes 294920 | tf_op jit(solution)/shard_map/ppermute | solution.py:26
  14.6 1.4 %collective-permute-start.3 = (bf16[3,128,128]{2,1,0:T(8,128)(2,1)S(1)}, bf16[3,128,128]{2,1,0:T(8,128)(2,1)S(1)}, u32[]{:S(2)}, u32[]{:S(2)}) collective-permute-start(bf16[3,128,128]{2,1,0:T(8,128)(2,1)S(1)} %get-tuple-element.33), channel_id=1, source_target_pairs={{0,1},{1,0},{2,3},{3,2},{4,5},{5,4},{6,7},{7,6},{8,9},{9,8},{10,11... | collective-permute-start | bytes 294920 | tf_op jit(solution)/shard_map/ppermute | solution.py:26
  16.0 2.1 %shard_map.59 = (bf16[1024,128]{1,0:T(8,128)(2,1)S(1)}, f32[256,128]{1,0:T(8,128)S(1)}, f32[128,128]{1,0:T(8,128)S(1)}, f32[8,128]{1,0:T(8,128)S(1)}) custom-call(bf16[8,128,128]{2,1,0:T(8,128)(2,1)S(1)} %get-tuple-element.28.own, bf16[8,128,128]{2,1,0:T(8,128)(2,1)S(1)} %collective-permute-done.odd, bf16[8,128,128]{2,1,0:T(8,128)(2,1)S(1)} %collective-permute-done.1.even, ...), custom_call_target="tpu_custom_call" | custom-call | flops 905969664 | bytes 3145728 | tf_op jit(solution)/shard_map/pallas_call | solution.py:53
  18.1 0.5 collective-permute-done.2.odd_rows
  18.7 0.0 collective-permute-done.3.even_rows
  18.7 0.5 shard_map.61
  19.2 16.7 %all_to_all.30.refs_0_ = f32[32,5,128]{2,1,0:T(8,128)S(1)} all-to-all(f32[32,5,128]{2,1,0:T(8,128)S(1)} %get-tuple-element.36), channel_id=1, replica_groups=mesh['y'=4,'z'=8,'x'=4,'c'=2] {'y','x','c'}, dimensions={0} | all-to-all | bytes 163840 | tf_op jit(solution)/shard_map/all_to_all | solution.py:440
  36.0 11.8 %all_to_all.31.refs_0_ = f32[8,5,128]{2,1,0:T(8,128)S(1)} all-to-all(f32[8,5,128]{2,1,0:T(8,128)S(1)} %shard_map.62), channel_id=1, replica_groups=mesh['y'=4,'z'=8,'x'=4,'c'=2] {'z'}, dimensions={0} | all-to-all | bytes 40960 | tf_op jit(solution)/shard_map/all_to_all | solution.py:440
  47.8 0.7 shard_map.63
  48.4 6.0 %all-to-all-start.2 = ((f32[32,5,128]{2,1,0:T(8,128)}), f32[32,5,128]{2,1,0:T(8,128)S(1)}, u32[]{:S(2)}, u32[]{:S(2)}) async-start(f32[32,5,128]{2,1,0:T(8,128)} %shard_map.63), calls=%async_computation.2 | async-start | bytes 262144 | tf_op jit(solution)/shard_map/all_to_all | solution.py:440
  54.4 0.4 shard_map.64.refs_1_.pack
  54.8 5.3 %all-to-all-done.2.refs_0_ = f32[32,5,128]{2,1,0:T(8,128)S(1)} async-done(((f32[32,5,128]{2,1,0:T(8,128)}), f32[32,5,128]{2,1,0:T(8,128)S(1)}, u32[]{:S(2)}, u32[]{:S(2)}) %all-to-all-start.2) | async-done | bytes 81952 | tf_op jit(solution)/shard_map/all_to_all | solution.py:440
  60.1 5.9 %shard_map.65 = (bf16[1024,128]{1,0:T(8,128)(2,1)S(1)}, f32[16,112,128]{2,1,0:T(8,128)S(1)}, bf16[16,112,128]{2,1,0:T(8,128)(2,1)S(1)}, f32[128,128]{1,0:T(8,128)S(1)}, f32[8,128]{1,0:T(8,128)S(1)}) custom-call(f32[32,5,128]{2,1,0:T(8,128)S(1)} %all-to-all-done.2.refs_0_, bf16[5888,128]{1,0:T(8,128)(2,1)S(1)} %shard_map.64.refs_1_.pack), custom_call_target="tpu_custom_call" | custom-call | flops 905969664 | bytes 1048576 | tf_op jit(solution)/shard_map/pallas_call | solution.py:53
  66.0 0.2 collective-permute-start.4
  66.2 1.7 %collective-permute-done.4.received = bf16[16,112,128]{2,1,0:T(8,128)(2,1)S(1)} collective-permute-done((bf16[16,112,128]{2,1,0:T(8,128)(2,1)S(1)}, bf16[16,112,128]{2,1,0:T(8,128)(2,1)S(1)}, u32[]{:S(2)}, u32[]{:S(2)}) %collective-permute-start.4) | collective-permute-done | bytes 458784 | tf_op jit(solution)/shard_map/ppermute | solution.py:528
  67.9 0.9 shard_map.66
  68.7 5.8 %all-to-all-start.3 = ((bf16[16,112,128]{2,1,0:T(8,128)(2,1)}), bf16[16,112,128]{2,1,0:T(8,128)(2,1)S(1)}, u32[]{:S(2)}, u32[]{:S(2)}) async-start(bf16[16,112,128]{2,1,0:T(8,128)(2,1)} %shard_map.66), calls=%async_computation.3 | async-start | bytes 917504 | tf_op jit(solution)/shard_map/all_to_all | solution.py:440
  74.6 0.5 collective-permute-start.5
  75.1 0.8 collective-permute-start.6
  75.9 1.1 shard_map.68
  77.0 6.4 %all-to-all-done.3.refs_0_ = bf16[16,112,128]{2,1,0:T(8,128)(2,1)S(1)} async-done(((bf16[16,112,128]{2,1,0:T(8,128)(2,1)}), bf16[16,112,128]{2,1,0:T(8,128)(2,1)S(1)}, u32[]{:S(2)}, u32[]{:S(2)}) %all-to-all-start.3) | async-done | bytes 458784 | tf_op jit(solution)/shard_map/all_to_all | solution.py:440
  83.4 0.8 shard_map.67
  84.2 3.4 %all-to-all-start.4 = ((bf16[8,112,128]{2,1,0:T(8,128)(2,1)}), bf16[8,112,128]{2,1,0:T(8,128)(2,1)S(1)}, u32[]{:S(2)}, u32[]{:S(2)}) async-start(bf16[8,112,128]{2,1,0:T(8,128)(2,1)} %shard_map.67), calls=%async_computation.4 | async-start | bytes 458752 | tf_op jit(solution)/shard_map/all_to_all | solution.py:440
  87.6 0.0 copy-start.1
  87.6 0.0 collective-permute-done.5.even
  87.6 0.0 collective-permute-done.6.odd
  87.6 2.5 %collective-permute-start.7 = (bf16[3,128,128]{2,1,0:T(8,128)(2,1)S(1)}, bf16[3,128,128]{2,1,0:T(8,128)(2,1)S(1)}, u32[]{:S(2)}, u32[]{:S(2)}) collective-permute-start(bf16[3,128,128]{2,1,0:T(8,128)(2,1)S(1)} %get-tuple-element.47), channel_id=1, source_target_pairs={{1,2},{2,1},{3,4},{4,3},{5,6},{6,5},{9,10},{10,9},{11,12},{12,11},... | collective-permute-start | bytes 294920 | tf_op jit(solution)/shard_map/ppermute | solution.py:26
  90.2 0.9 collective-permute-start.8
  91.1 7.9 %all-to-all-done.4.refs_0_ = bf16[8,112,128]{2,1,0:T(8,128)(2,1)S(1)} async-done(((bf16[8,112,128]{2,1,0:T(8,128)(2,1)}), bf16[8,112,128]{2,1,0:T(8,128)(2,1)S(1)}, u32[]{:S(2)}, u32[]{:S(2)}) %all-to-all-start.4) | async-done | bytes 229408 | tf_op jit(solution)/shard_map/all_to_all | solution.py:440
  99.0 0.7 shard_map.70
  99.7 0.0 collective-permute-done.7.odd_rows
  99.7 0.0 collective-permute-done.8.even_rows
  99.7 3.3 %all-to-all-start.5 = ((bf16[4,112,128]{2,1,0:T(8,128)(2,1)}), bf16[4,112,128]{2,1,0:T(8,128)(2,1)S(1)}, u32[]{:S(2)}, u32[]{:S(2)}) async-start(bf16[4,112,128]{2,1,0:T(8,128)(2,1)} %shard_map.70), calls=%async_computation.5 | async-start | bytes 229376 | tf_op jit(solution)/shard_map/all_to_all | solution.py:440
  103.0 0.0 copy-done.1
  103.0 2.6 %shard_map.71 = bf16[1024,128]{1,0:T(8,128)(2,1)} custom-call(bf16[8,128,128]{2,1,0:T(8,128)(2,1)S(1)} %bitcast.18, bf16[8,128,128]{2,1,0:T(8,128)(2,1)S(1)} %collective-permute-done.5.even, bf16[8,128,128]{2,1,0:T(8,128)(2,1)S(1)} %collective-permute-done.6.odd, bf16[3,128,128]{2,1,0:T(8,128)(2,1)S(1)} %collective-permute-done.7.odd_rows, ...), custom_call_target="tpu_custom_call" | custom-call | flops 905969664 | bytes 3145728 | tf_op jit(solution)/shard_map/pallas_call | solution.py:53
  105.6 3.2 %all-to-all-done.5 = bf16[4,112,128]{2,1,0:T(8,128)(2,1)S(1)} async-done(((bf16[4,112,128]{2,1,0:T(8,128)(2,1)}), bf16[4,112,128]{2,1,0:T(8,128)(2,1)S(1)}, u32[]{:S(2)}, u32[]{:S(2)}) %all-to-all-start.5) | async-done | bytes 114720 | tf_op jit(solution)/shard_map/all_to_all | solution.py:440
  108.9 0.7 convert.1
  (4 shorter events, 0.1 us)
Async XLA Ops:
  0.6 9.4 %collective-permute-start = (bf16[8,128,128]{2,1,0:T(8,128)(2,1)}, bf16[8,128,128]{2,1,0:T(8,128)(2,1)S(1)}, u32[]{:S(2)}, u32[]{:S(2)}) collective-permute-start(bf16[8,128,128]{2,1,0:T(8,128)(2,1)} %bitcast.12), channel_id=1, source_target_pairs={{8,16},{16,8},{24,32},{32,24},{40,48},{48,40},{56,64},{64,56},{72,... | collective-permute-start | bytes 786440 | tf_op jit(solution)/shard_map/ppermute | solution.py:26
  1.3 11.4 %collective-permute-start.1 = (bf16[8,128,128]{2,1,0:T(8,128)(2,1)}, bf16[8,128,128]{2,1,0:T(8,128)(2,1)S(1)}, u32[]{:S(2)}, u32[]{:S(2)}) collective-permute-start(bf16[8,128,128]{2,1,0:T(8,128)(2,1)} %bitcast.13), channel_id=1, source_target_pairs={{0,8},{8,0},{16,24},{24,16},{32,40},{40,32},{48,56},{56,48},{64,72... | collective-permute-start | bytes 786440 | tf_op jit(solution)/shard_map/ppermute | solution.py:26
  6.5 1.2 %copy-start = (bf16[3,3,3,128,128]{4,3,2,1,0:T(8,128)(2,1)S(1)}, bf16[3,3,3,128,128]{4,3,2,1,0:T(8,128)(2,1)}, u32[]{:S(2)}) copy-start(bf16[3,3,3,128,128]{4,3,2,1,0:T(8,128)(2,1)} %param.4) | copy-start | bytes 2654212
  7.6 0.9 copy-start.2
  8.6 0.9 copy-start.3
  12.7 5.9 %collective-permute-start.2 = (bf16[3,128,128]{2,1,0:T(8,128)(2,1)S(1)}, bf16[3,128,128]{2,1,0:T(8,128)(2,1)S(1)}, u32[]{:S(2)}, u32[]{:S(2)}) collective-permute-start(bf16[3,128,128]{2,1,0:T(8,128)(2,1)S(1)} %get-tuple-element.32), channel_id=1, source_target_pairs={{1,2},{2,1},{3,4},{4,3},{5,6},{6,5},{9,10},{10,9},{11,12},{12,11},... | collective-permute-start | bytes 294920 | tf_op jit(solution)/shard_map/ppermute | solution.py:26
  14.6 4.0 %collective-permute-start.3 = (bf16[3,128,128]{2,1,0:T(8,128)(2,1)S(1)}, bf16[3,128,128]{2,1,0:T(8,128)(2,1)S(1)}, u32[]{:S(2)}, u32[]{:S(2)}) collective-permute-start(bf16[3,128,128]{2,1,0:T(8,128)(2,1)S(1)} %get-tuple-element.33), channel_id=1, source_target_pairs={{0,1},{1,0},{2,3},{3,2},{4,5},{5,4},{6,7},{7,6},{8,9},{9,8},{10,11... | collective-permute-start | bytes 294920 | tf_op jit(solution)/shard_map/ppermute | solution.py:26
  48.4 11.6 %all-to-all-start.2 = ((f32[32,5,128]{2,1,0:T(8,128)}), f32[32,5,128]{2,1,0:T(8,128)S(1)}, u32[]{:S(2)}, u32[]{:S(2)}) async-start(f32[32,5,128]{2,1,0:T(8,128)} %shard_map.63), calls=%async_computation.2 | async-start | bytes 262144 | tf_op jit(solution)/shard_map/all_to_all | solution.py:440
  66.0 1.9 %collective-permute-start.4 = (bf16[16,112,128]{2,1,0:T(8,128)(2,1)S(1)}, bf16[16,112,128]{2,1,0:T(8,128)(2,1)S(1)}, u32[]{:S(2)}, u32[]{:S(2)}) collective-permute-start(bf16[16,112,128]{2,1,0:T(8,128)(2,1)S(1)} %get-tuple-element.41), channel_id=1, source_target_pairs={{0,1},{1,0},{2,3},{3,2},{4,5},{5,4},{6,7},{7,6},{8,9},{9,8},{10,11... | collective-permute-start | bytes 1376264 | tf_op jit(solution)/shard_map/ppermute | solution.py:528
  68.7 14.7 %all-to-all-start.3 = ((bf16[16,112,128]{2,1,0:T(8,128)(2,1)}), bf16[16,112,128]{2,1,0:T(8,128)(2,1)S(1)}, u32[]{:S(2)}, u32[]{:S(2)}) async-start(bf16[16,112,128]{2,1,0:T(8,128)(2,1)} %shard_map.66), calls=%async_computation.3 | async-start | bytes 917504 | tf_op jit(solution)/shard_map/all_to_all | solution.py:440
  74.6 13.0 %collective-permute-start.5 = (bf16[8,128,128]{2,1,0:T(8,128)(2,1)S(1)}, bf16[8,128,128]{2,1,0:T(8,128)(2,1)S(1)}, u32[]{:S(2)}, u32[]{:S(2)}) collective-permute-start(bf16[8,128,128]{2,1,0:T(8,128)(2,1)S(1)} %bitcast.15), channel_id=1, source_target_pairs={{0,8},{8,0},{16,24},{24,16},{32,40},{40,32},{48,56},{56,48},{64,72... | collective-permute-start | bytes 786440 | tf_op jit(solution)/shard_map/ppermute | solution.py:26
  75.1 12.5 %collective-permute-start.6 = (bf16[8,128,128]{2,1,0:T(8,128)(2,1)S(1)}, bf16[8,128,128]{2,1,0:T(8,128)(2,1)S(1)}, u32[]{:S(2)}, u32[]{:S(2)}) collective-permute-start(bf16[8,128,128]{2,1,0:T(8,128)(2,1)S(1)} %bitcast.16), channel_id=1, source_target_pairs={{8,16},{16,8},{24,32},{32,24},{40,48},{48,40},{56,64},{64,56},{72,... | collective-permute-start | bytes 786440 | tf_op jit(solution)/shard_map/ppermute | solution.py:26
  84.2 14.8 %all-to-all-start.4 = ((bf16[8,112,128]{2,1,0:T(8,128)(2,1)}), bf16[8,112,128]{2,1,0:T(8,128)(2,1)S(1)}, u32[]{:S(2)}, u32[]{:S(2)}) async-start(bf16[8,112,128]{2,1,0:T(8,128)(2,1)} %shard_map.67), calls=%async_computation.4 | async-start | bytes 458752 | tf_op jit(solution)/shard_map/all_to_all | solution.py:440
  87.6 15.4 %copy-start.1 = (bf16[3,3,3,128,128]{4,3,2,1,0:T(8,128)(2,1)S(1)}, bf16[3,3,3,128,128]{4,3,2,1,0:T(8,128)(2,1)}, u32[]{:S(2)}) copy-start(bf16[3,3,3,128,128]{4,3,2,1,0:T(8,128)(2,1)} %param.4) | copy-start | bytes 2654212
  87.6 12.0 %collective-permute-start.7 = (bf16[3,128,128]{2,1,0:T(8,128)(2,1)S(1)}, bf16[3,128,128]{2,1,0:T(8,128)(2,1)S(1)}, u32[]{:S(2)}, u32[]{:S(2)}) collective-permute-start(bf16[3,128,128]{2,1,0:T(8,128)(2,1)S(1)} %get-tuple-element.47), channel_id=1, source_target_pairs={{1,2},{2,1},{3,4},{4,3},{5,6},{6,5},{9,10},{10,9},{11,12},{12,11},... | collective-permute-start | bytes 294920 | tf_op jit(solution)/shard_map/ppermute | solution.py:26
  90.2 9.5 %collective-permute-start.8 = (bf16[3,128,128]{2,1,0:T(8,128)(2,1)S(1)}, bf16[3,128,128]{2,1,0:T(8,128)(2,1)S(1)}, u32[]{:S(2)}, u32[]{:S(2)}) collective-permute-start(bf16[3,128,128]{2,1,0:T(8,128)(2,1)S(1)} %get-tuple-element.48), channel_id=1, source_target_pairs={{0,1},{1,0},{2,3},{3,2},{4,5},{5,4},{6,7},{7,6},{8,9},{9,8},{10,11... | collective-permute-start | bytes 294920 | tf_op jit(solution)/shard_map/ppermute | solution.py:26
  99.7 9.2 %all-to-all-start.5 = ((bf16[4,112,128]{2,1,0:T(8,128)(2,1)}), bf16[4,112,128]{2,1,0:T(8,128)(2,1)S(1)}, u32[]{:S(2)}, u32[]{:S(2)}) async-start(bf16[4,112,128]{2,1,0:T(8,128)(2,1)} %shard_map.70), calls=%async_computation.5 | async-start | bytes 229376 | tf_op jit(solution)/shard_map/all_to_all | solution.py:440
